TPU v7x, 32 devices: a whole 2x2x4 slice. The times are simulated.
32 devices in a mesh: dp: 8 (over z, core), tensor: 4 (over y, x).
Axes of the slice: x: 2, y: 2, z: 4, core: 2. Of those that a mesh axis runs over, the one named last changes fastest.
Arguments:
- tokens: bfloat16 [16, 2048, 1280], P('dp', 'tensor'), may hold values from -6 to 6
- segments: int32 [16, 2048], P('dp'), may hold values from 0 to 255, as said below
- attn_gain: float32 [1280], replicated, may hold values from 0.1 to 1.9
- w_query: bfloat16 [1280, 1280], P('dp', 'tensor'), may hold values from -0.15625 to 0.15625
- w_key: bfloat16 [1280, 1280], P('dp', 'tensor'), may hold values from -0.15625 to 0.15625
- w_value: bfloat16 [1280, 1280], P('dp', 'tensor'), may hold values from -0.15625 to 0.15625
- w_out: bfloat16 [1280, 1280], P('tensor', 'dp'), may hold values from -1 to 1
- query_scale: float32 [80], replicated, may hold values from 0 to 1.5
- mlp_gain: float32 [1280], replicated, may hold values from 0.1 to 1.9
- w_up: bfloat16 [1280, 1280], P('dp', 'tensor'), may hold values from -0.15625 to 0.15625
- w_down: bfloat16 [1280, 1280], P('tensor', 'dp'), may hold values from -0.15625 to 0.15625
- cotangent: bfloat16 [16, 2048, 1280], P('dp', 'tensor'), may hold values from -6 to 6
Outputs:
- block_out: bfloat16 [16, 2048, 1280], P('dp', 'tensor')
- input_grad: float32 [16, 2048, 1280], P('dp', 'tensor')
- grad_attn_gain: float32 [1280], replicated
- grad_query: float32 [1280, 1280], P('dp', 'tensor')
- grad_key: float32 [1280, 1280], P('dp', 'tensor')
- grad_value: float32 [1280, 1280], P('dp', 'tensor')
- grad_out: float32 [1280, 1280], P('tensor', 'dp')
- grad_query_scale: float32 [80], replicated
- grad_mlp_gain: float32 [1280], replicated
- grad_up: float32 [1280, 1280], P('dp', 'tensor')
- grad_down: float32 [1280, 1280], P('tensor', 'dp')
Inputs may be any that keep to these rules, and one draw needn't show every extreme that they name: `segments`: each row holds the document numbers of one sequence: they start at 0, never fall and rise by at most 1 from one position to the next. In every aligned group of 2 rows (the sequences of one index of dp) one row is a single document.
All inputs are finite; a program needn't handle non-finite values.
Results may differ from a plain program's by a relative error of at most 0.012.
The roundings to bfloat16 on the way count: a program that leaves them out, or rounds other values in their place, can miss the bound.
Values may be sent and summed in bfloat16 or wider, within the bound.
A program may use at most 320 MiB of HBM per device.

v0:
```python
import functools
import itertools
import math
import jax, jax.numpy as jnp
from jax import lax
from jax.experimental import pallas as pl
from jax.experimental.pallas import tpu as pltpu
from jax.sharding import Mesh, PartitionSpec as P

AXES=("zz","core","q","s")
norm_eps = 1e-06
HD=80
BQ=256
NEG=-1e30
f32=jnp.float32; bf16=jnp.bfloat16
NT=(((1,),(1,)),((),()))
NN=(((1,),(0,)),((),()))
TN=(((0,),(0,)),((),()))
def dot(a,b,dims=NN): return lax.dot_general(a,b,dims,preferred_element_type=f32)

def merge(*gens):
    gens=list(gens)
    while gens:
        for g in list(gens):
            try: next(g)
            except StopIteration: gens.remove(g)

def fwd_kernel(hb, first_ref, last_ref, x_ref, wt_ref, pd_ref, segk_ref, segq_ref,
               qt_ref, kt_ref, k_ref, v_ref, ot_ref, lse_ref, vt_scr, s_scr, m_scr, l_scr, acc_scr):
    L=x_ref.shape[0]; nb=L//BQ; W=hb*HD
    CH=512
    for c in range(L//CH):
        cs=slice(c*CH,(c+1)*CH)
        r=dot(wt_ref[...],x_ref[cs,:],NT)
        qt_ref[:,cs]=(r[:W]*pd_ref[:,:1]).astype(bf16)
        kt_ref[:,cs]=r[W:2*W].astype(bf16)
        vt_scr[:,cs]=r[2*W:].astype(bf16)
        for h in range(hb):
            k_ref[h,cs,:]=r[W+h*HD:W+(h+1)*HD].T.astype(bf16)
            v_ref[h,cs,:]=r[2*W+h*HD:2*W+(h+1)*HD].T.astype(bf16)
    rowi=lax.broadcasted_iota(jnp.int32,(BQ,BQ),0)
    coli=lax.broadcasted_iota(jnp.int32,(BQ,BQ),1)
    hs=[slice(h*HD,(h+1)*HD) for h in range(hb)]
    single = first_ref[0]==last_ref[nb-1]
    @pl.when(single)
    def _():
        units=[(i,h) for i in range(nb) for h in range(hb)]
        st={}
        def phase_a(u):
            i,h=units[u]; c0=i*BQ
            qi=qt_ref[hs[h],c0:c0+BQ]
            m8=None
            for j in range(i+1):
                s=dot(k_ref[h,j*BQ:(j+1)*BQ,:],qi)
                if j==i: s=jnp.where(rowi<=coli,s,NEG)
                s_scr[u%2,j*BQ:(j+1)*BQ,:]=s
                mm=s.reshape(BQ//8,8,BQ).max(0)
                m8=mm if m8 is None else jnp.maximum(m8,mm)
                yield
            st[u]=m8.max(0,keepdims=True)
        def phase_b(u):
            i,h=units[u]; c0=i*BQ
            m=st[u]; l8=None; acc=None
            for j in range(i+1):
                p=jnp.exp(s_scr[u%2,j*BQ:(j+1)*BQ,:]-m)
                ll=p.reshape(BQ//8,8,BQ).sum(0)
                l8=ll if l8 is None else l8+ll
                pv=dot(vt_scr[hs[h],j*BQ:(j+1)*BQ],p.astype(bf16))
                acc=pv if acc is None else acc+pv
                yield
            l=l8.sum(0,keepdims=True)
            ot_ref[hs[h],c0:c0+BQ]=(acc*(1.0/l)).astype(bf16)
            lse_ref[h,:,c0:c0+BQ]=m+jnp.log(l)
        merge(phase_a(0))
        for u in range(len(units)):
            gs=[phase_b(u)]
            if u+1<len(units): gs=[phase_a(u+1)]+gs
            merge(*gs)
    @pl.when(jnp.logical_not(single))
    def _():
        def qblock(i,_):
            c0=pl.multiple_of(i*BQ,BQ)
            def cnt(j,a): return a+jnp.where(last_ref[j]<first_ref[i],1,0)
            j0=lax.fori_loop(0,i,cnt,jnp.int32(0))
            m_scr[...]=jnp.full_like(m_scr,NEG); l_scr[...]=jnp.zeros_like(l_scr); acc_scr[...]=jnp.zeros_like(acc_scr)
            def step(j,_):
                r0=pl.multiple_of(j*BQ,BQ)
                sk=segk_ref[pl.ds(r0,BQ),:]
                ok=(jnp.concatenate([sk]*(BQ//128),axis=1)==segq_ref[:,pl.ds(c0,BQ)])&(rowi+r0<=coli+c0)
                for h in range(hb):
                    s=dot(k_ref[h,pl.ds(r0,BQ),:],qt_ref[hs[h],pl.ds(c0,BQ)])
                    s=jnp.where(ok,s,NEG)
                    mo=m_scr[h]
                    m=jnp.maximum(mo,s.max(0,keepdims=True))
                    al=jnp.exp(mo-m)
                    p=jnp.where(ok,jnp.exp(s-m),0.0)
                    l_scr[h]=l_scr[h]*al+p.sum(0,keepdims=True)
                    acc_scr[hs[h],:]=acc_scr[hs[h],:]*al+dot(vt_scr[hs[h],pl.ds(r0,BQ)],p.astype(bf16))
                    m_scr[h]=m
                return 0
            lax.fori_loop(j0,i+1,step,0)
            for h in range(hb):
                ot_ref[hs[h],pl.ds(c0,BQ)]=(acc_scr[hs[h],:]*(1.0/l_scr[h])).astype(bf16)
                lse_ref[h,:,pl.ds(c0,BQ)]=m_scr[h]+jnp.log(l_scr[h])
            return 0
        lax.fori_loop(0,nb,qblock,0)

def attn_fwd(first,last,x,wt,pd,segk,segq):
    L,D=x.shape; W=wt.shape[0]//3; hb=W//HD
    V=pl.BlockSpec(memory_space=pltpu.VMEM); S=pl.BlockSpec(memory_space=pltpu.SMEM)
    hd=jax.ShapeDtypeStruct((hb,L,HD),bf16); td=jax.ShapeDtypeStruct((W,L),bf16)
    flops=2*L*D*3*W+2*2*L*L//2*256*hb
    return pl.pallas_call(functools.partial(fwd_kernel,hb),
        out_shape=(td,td,hd,hd,td,jax.ShapeDtypeStruct((hb,1,L),f32)),
        in_specs=[S,S,V,V,V,V,V],out_specs=(V,)*6,
        scratch_shapes=[pltpu.VMEM((W,L),bf16),pltpu.VMEM((2,L,BQ),f32),
            pltpu.VMEM((hb,1,BQ),f32),pltpu.VMEM((hb,1,BQ),f32),pltpu.VMEM((W,BQ),f32)],
        compiler_params=pltpu.CompilerParams(vmem_limit_bytes=56*2**20),
        cost_estimate=pl.CostEstimate(flops=flops,bytes_accessed=x.size*2+wt.size*2+4*L*W*2,transcendentals=L*L//2*hb),
        name="attn_fwd")(first,last,x,wt,pd,segk,segq)

def bwd_kernel(hb, first_ref, last_ref, qt_ref, kt_ref, k_ref, v_ref, ot_ref, dot_ref, lse_ref, pd_ref, segk_ref, segq_ref,
               g_ref, sc_ref, p_scr, ds_scr, dq_scr, dl_scr, dv_scr, dk_scr):
    W=hb*HD; L=qt_ref.shape[1]; nb=L//BQ
    rowi=lax.broadcasted_iota(jnp.int32,(BQ,BQ),0)
    coli=lax.broadcasted_iota(jnp.int32,(BQ,BQ),1)
    hs=[slice(h*HD,(h+1)*HD) for h in range(hb)]
    for h in range(hb):
        dl_scr[h]=(dot_ref[hs[h],:].astype(f32)*ot_ref[hs[h],:].astype(f32)).sum(0,keepdims=True)
    single = first_ref[0]==last_ref[nb-1]
    @pl.when(single)
    def _():
        units=[(j,h,i) for j in range(nb) for h in range(hb) for i in range(j,nb)]
        acc={}
        def phase_a(u):
            j,h,i=units[u]; js=slice(j*BQ,(j+1)*BQ); cs=slice(i*BQ,(i+1)*BQ)
            H2=BQ//2
            for a in range(2):
                ks=slice(j*BQ+a*H2,j*BQ+(a+1)*H2)
                s=dot(k_ref[h,ks,:],qt_ref[hs[h],cs])
                dp=dot(v_ref[h,ks,:],dot_ref[hs[h],cs])
                if j==i: s=jnp.where(rowi[a*H2:(a+1)*H2]<=coli[a*H2:(a+1)*H2],s,NEG)
                p=jnp.exp(s-lse_ref[h,:,cs])
                p_scr[u%2,a*H2:(a+1)*H2,:]=p.astype(bf16)
                ds_scr[u%2,a*H2:(a+1)*H2,:]=(p*(dp-dl_scr[h,:,cs])).astype(bf16)
                yield
        def phase_b(u):
            j,h,i=units[u]; js=slice(j*BQ,(j+1)*BQ); cs=slice(i*BQ,(i+1)*BQ)
            p=p_scr[u%2]; ds=ds_scr[u%2]
            dv=dot(dot_ref[hs[h],cs],p,NT); dk=dot(qt_ref[hs[h],cs],ds,NT)
            if i==j: dv_scr[h]=dv; dk_scr[h]=dk
            else: dv_scr[h]+=dv; dk_scr[h]+=dk
            yield
            dq=dot(kt_ref[hs[h],js],ds)
            if j==0: dq_scr[hs[h],cs]=dq
            else: dq_scr[hs[h],cs]+=dq
            if i==nb-1:
                g_ref[W+h*HD:W+(h+1)*HD,js]=dk_scr[h].astype(bf16)
                g_ref[2*W+h*HD:2*W+(h+1)*HD,js]=dv_scr[h].astype(bf16)
            yield
        merge(phase_a(0))
        for u in range(len(units)):
            gs=[phase_b(u)]
            if u+1<len(units): gs=[phase_a(u+1)]+gs
            merge(*gs)
    @pl.when(jnp.logical_not(single))
    def _():
        dq_scr[...]=jnp.zeros_like(dq_scr)
        def kblock(j,_):
            r0=pl.multiple_of(j*BQ,BQ)
            def cnt(i,a): return a+jnp.where(first_ref[i]<=last_ref[j],1,0)
            iend=lax.fori_loop(j,nb,cnt,j)
            dv_scr[...]=jnp.zeros_like(dv_scr); dk_scr[...]=jnp.zeros_like(dk_scr)
            sk=segk_ref[pl.ds(r0,BQ),:]
            sk=jnp.concatenate([sk]*(BQ//128),axis=1)
            def step(i,_):
                c0=pl.multiple_of(i*BQ,BQ); cs=pl.ds(c0,BQ)
                ok=(sk==segq_ref[:,cs])&(rowi+r0<=coli+c0)
                for h in range(hb):
                    qt=qt_ref[hs[h],cs]; do=dot_ref[hs[h],cs]
                    s=dot(k_ref[h,pl.ds(r0,BQ),:],qt)
                    dp=dot(v_ref[h,pl.ds(r0,BQ),:],do)
                    p=jnp.exp(jnp.where(ok,s-lse_ref[h,:,cs],NEG))
                    ds=(p*(dp-dl_scr[h,:,cs])).astype(bf16)
                    dv_scr[h]+=dot(do,p.astype(bf16),NT)
                    dk_scr[h]+=dot(qt,ds,NT)
                    dq_scr[hs[h],cs]+=dot(kt_ref[hs[h],pl.ds(r0,BQ)],ds)
                return 0
            lax.fori_loop(j,iend,step,0)
            for h in range(hb):
                g_ref[W+h*HD:W+(h+1)*HD,pl.ds(r0,BQ)]=dk_scr[h].astype(bf16)
                g_ref[2*W+h*HD:2*W+(h+1)*HD,pl.ds(r0,BQ)]=dv_scr[h].astype(bf16)
            return 0
        lax.fori_loop(0,nb,kblock,0)
    dq=dq_scr[...]
    g_ref[:W,:]=(dq*pd_ref[:,:1]).astype(bf16)
    sc=(dq*qt_ref[...].astype(f32)).sum(1,keepdims=True)
    sc_ref[...]=jnp.broadcast_to(sc/pd_ref[:,:1],sc_ref.shape)

def attn_bwd(first,last,qt,kt,k,v,ot,dot_,lse,pd,segk,segq):
    W,L=qt.shape; hb=W//HD
    V=pl.BlockSpec(memory_space=pltpu.VMEM); S=pl.BlockSpec(memory_space=pltpu.SMEM)
    flops=5*2*L*L//2*256*hb
    return pl.pallas_call(functools.partial(bwd_kernel,hb),
        out_shape=(jax.ShapeDtypeStruct((3*W,L),bf16),jax.ShapeDtypeStruct((W,128),f32)),
        in_specs=[S,S]+[V]*10,out_specs=(V,)*2,
        scratch_shapes=[pltpu.VMEM((2,BQ,BQ),bf16),pltpu.VMEM((2,BQ,BQ),bf16),pltpu.VMEM((W,L),f32),
            pltpu.VMEM((hb,1,L),f32),pltpu.VMEM((hb,HD,BQ),f32),pltpu.VMEM((hb,HD,BQ),f32)],
        compiler_params=pltpu.CompilerParams(vmem_limit_bytes=56*2**20),
        cost_estimate=pl.CostEstimate(flops=flops,bytes_accessed=8*L*W*2,transcendentals=L*L//2*hb),
        name="attn_bwd")(first,last,qt,kt,k,v,ot,dot_,lse,pd,segk,segq)


MESH=pl.DeviceIdType.MESH

def rcopy(src,dst,ss,rs,dev):
    return pltpu.make_async_remote_copy(src_ref=src,dst_ref=dst,send_sem=ss,recv_sem=rs,device_id=dev,device_id_type=MESH)

def transpose_rows(src, dst):
    P_,rows,cols=src.shape
    per=max(1,640//rows)
    for i in range(P_//per):
        dst[:,i*per*rows:(i+1)*per*rows]=src[i*per:(i+1)*per].reshape(per*rows,cols).T

def partner(q, m):
    return (q,q+1-2*lax.rem(q,2),lax.rem(q+2,4),3-q)[m]

def greet(Z, C):
    z,k,q,s=[lax.axis_index(a) for a in AXES]
    bar=pltpu.get_barrier_semaphore()
    plane=list(itertools.product(range(2),range(4),range(C)))[1:]
    column=[(j,a) for j in range(1,Z) for a in range(2)]
    for a,b,c in plane:
        pl.semaphore_signal(bar,inc=1,device_id=(z,lax.rem(k+a,2),lax.rem(q+b,4),lax.rem(s+c,C)),device_id_type=MESH)
    for j,a in column:
        pl.semaphore_signal(bar,inc=1,device_id=(lax.rem(z+j,Z),lax.rem(k+a,2),q,s),device_id_type=MESH)
    pl.semaphore_wait(bar,len(plane)+len(column))

def col_copies(Z, src, dst, ss, rs):
    z,k,q,s=[lax.axis_index(a) for a in AXES]
    out=[]
    for j in range(Z):
        for a in range(2):
            kk=lax.rem(k+a,2)
            if j==0 and a==0: out.append(pltpu.make_async_copy(src.at[k],dst.at[2*z+k],rs.at[2*z+k]))
            else: out.append(rcopy(src.at[kk],dst.at[2*z+k],ss.at[j*2+a],rs.at[2*z+k],(lax.rem(z+j,Z),kk,q,s)))
    return out

def spread_copies(C, n, src, dst, ss, rs):
    z,k,q,s=[lax.axis_index(a) for a in AXES]
    out=[]
    for r in range(2):
        for h in range(2):
            for s2 in range(C):
                i=(r*2+h)*C+s2
                piece=src.at[r,pl.ds((h*C+s2)*n,n),:]
                out.append(((k==h)&(q==2*k+r)&(s==s2),pltpu.make_async_copy(piece,dst.at[q*C+s],rs.at[q*C+s]),
                            rcopy(piece,dst.at[q*C+s],ss.at[i],rs.at[q*C+s],(z,h,2*k+r,s2))))
    return out

def spread_start(cps):
    for mine,loc,cp in cps:
        @pl.when(mine)
        def _(loc=loc): loc.start()
        @pl.when(jnp.logical_not(mine))
        def _(cp=cp): cp.start()

def spread_sent(cps):
    for mine,loc,cp in cps:
        @pl.when(jnp.logical_not(mine))
        def _(cp=cp): cp.wait_send()

def arrived(ref, sem):
    z,k,q,s=[lax.axis_index(a) for a in AXES]
    rcopy(ref,ref,sem,sem,(z,1-k,q,s)).wait_recv()

def fwd_kernel(Z, C, n, x_ref, w1_ref, w2_ref, cot_ref, gain_ref, pd_ref, segk_ref, segq_ref,
               xo_ref, ain_ref, wts_ref, w2o_ref, coto_ref, mix_ref, qt_ref, kt_ref, k_ref, v_ref, ot_ref, lse_ref,
               wa_scr, wb_scr, wc_scr, wd_scr, d3_scr, o3_scr, w2_scr, vt_scr, s_scr,
               tok_s, tok_r, ain_s, ain_r, a_s, a_r, b_s, b_r, c_s, c_r, dd_s, dd_r, d3_s, o3_s, do_r,
               wt_s, wt_r, w2_s, w2_r, gr_s, gr_r, loc_s, cot_s, cot_r, mix_s, mix_r):
    z,k,q,s=[lax.axis_index(a) for a in AXES]
    G=2*C; g0=k*C+s; NB=4*C
    D=gain_ref.shape[1]; L=segq_ref.shape[1]; W=pd_ref.shape[0]; hb=W//HD; nb=L//BQ
    peers=list(itertools.product(range(2),range(C)))[1:]
    pdev=[(z,lax.rem(k+gc,2),q,lax.rem(s+gs,C)) for gc,gs in peers]
    pidx=[lax.rem(k+gc,2)*C+lax.rem(s+gs,C) for gc,gs in peers]
    back=[gc*C+(C-gs)%C for gc,gs in peers]
    fore=[gc*C+gs for gc,gs in peers]
    chipdev=[(z,k,partner(q,m),s) for m in range(4)]
    toks=spread_copies(C,n,x_ref,xo_ref,tok_s,tok_r)
    cots=spread_copies(C,n,cot_ref,coto_ref,cot_s,cot_r)
    ca=col_copies(Z,w1_ref,wa_scr,a_s,a_r)
    cb=col_copies(Z,w2_ref,wb_scr,b_s,b_r)
    cc=col_copies(Z,d3_scr,wc_scr,c_s,c_r)
    cd=col_copies(Z,o3_scr,wd_scr,dd_s,dd_r)
    d3=rcopy(w1_ref,d3_scr,d3_s,do_r.at[0],chipdev[3])
    o3=rcopy(w2_ref,o3_scr,o3_s,do_r.at[1],chipdev[3])
    wcp=[rcopy(wts_ref.at[0],wts_ref.at[m],wt_s.at[m],wt_r.at[m],chipdev[m]) for m in (1,2)]
    w2cp=[rcopy(w2_scr.at[0],w2_scr.at[m],w2_s.at[m],w2_r.at[m],chipdev[m]) for m in (1,2)]
    grp=[[rcopy(w2_scr.at[m],w2o_ref.at[back[i],m],gr_s.at[i,m],gr_r.at[back[i],m],pdev[i]) for i in range(G-1)] for m in range(4)]
    loc=[pltpu.make_async_copy(w2_scr.at[m],w2o_ref.at[0,m],loc_s.at[m]) for m in range(4)]
    def share(m):
        loc[m].start()
        for cp in grp[m]: cp.start()
    greet(Z,C)
    spread_start(toks)
    for cp in ca: cp.start()
    ains=[]
    for j in range(NB):
        arrived(xo_ref.at[j],tok_r.at[j])
        x=xo_ref[j].astype(f32)
        inv=lax.rsqrt(jnp.mean(x*x,axis=-1,keepdims=True)+norm_eps)
        slot=j*G+g0
        ain_ref[slot]=(x*inv*gain_ref[...]).astype(bf16)
        for i in range(G-1):
            cp=rcopy(ain_ref.at[slot],ain_ref.at[slot],ain_s.at[i,j],ain_r.at[slot],pdev[i])
            cp.start(); ains.append(cp)
    for i in range(2*Z): arrived(wa_scr.at[i],a_r.at[i])
    transpose_rows(wa_scr,wts_ref.at[0])
    for cp in wcp: cp.start()
    for cp in cb: cp.start()
    d3.start(); o3.start()
    for j in range(NB):
        for i in range(G-1): arrived(ain_ref.at[j*G+pidx[i]],ain_r.at[j*G+pidx[i]])
    rowi=lax.broadcasted_iota(jnp.int32,(BQ,BQ),0)
    coli=lax.broadcasted_iota(jnp.int32,(BQ,BQ),1)
    hs=[slice(h*HD,(h+1)*HD) for h in range(hb)]
    CH=512; per=CH//n; sub=BQ//n

    def block(m,_):
        @pl.when(m==1)
        def _():
            arrived(wts_ref.at[1],wt_r.at[1])
            for i in range(2*Z): arrived(wb_scr.at[i],b_r.at[i])
            transpose_rows(wb_scr,w2_scr.at[0])
            for cp in w2cp: cp.start()
            share(0)
            arrived(d3_scr,do_r.at[0])
            for cp in cc: cp.start()
        @pl.when(m==2)
        def _():
            arrived(wts_ref.at[2],wt_r.at[2])
            arrived(o3_scr,do_r.at[1])
            for cp in cd: cp.start()
        @pl.when(m==3)
        def _():
            for i in range(2*Z): arrived(wc_scr.at[i],c_r.at[i])
            transpose_rows(wc_scr,wts_ref.at[3])
            spread_start(cots)
        for c in range(L//CH):
            cs=slice(c*CH,(c+1)*CH)
            r=dot(wts_ref[m],ain_ref[c*per:(c+1)*per].reshape(CH,D),NT)
            qt_ref[m,:,cs]=(r[:W]*pd_ref[:,:1]).astype(bf16)
            kt_ref[m,:,cs]=r[W:2*W].astype(bf16)
            vt_scr[:,cs]=r[2*W:].astype(bf16)
            for h in range(hb):
                k_ref[m*hb+h,cs,:]=r[W+h*HD:W+(h+1)*HD].T.astype(bf16)
                v_ref[m*hb+h,cs,:]=r[2*W+h*HD:2*W+(h+1)*HD].T.astype(bf16)
        units=[(i,h) for i in range(nb) for h in range(hb)]
        st={}
        def phase_a(u):
            i,h=units[u]; c0=i*BQ
            qi=qt_ref[m,hs[h],c0:c0+BQ]
            sq=segq_ref[:,c0:c0+BQ]
            m8=None
            for j in range(i+1):
                t=dot(k_ref[m*hb+h,j*BQ:(j+1)*BQ,:],qi)
                sk=segk_ref[j*BQ:(j+1)*BQ,:]
                ok=jnp.concatenate([sk]*(BQ//128),axis=1)==sq
                if j==i: ok=ok&(rowi<=coli)
                t=jnp.where(ok,t,NEG)
                s_scr[u%2,j*BQ:(j+1)*BQ,:]=t
                mm=t.reshape(BQ//8,8,BQ).max(0)
                m8=mm if m8 is None else jnp.maximum(m8,mm)
                yield
            st[u]=m8.max(0,keepdims=True)
        def phase_b(u):
            i,h=units[u]; c0=i*BQ
            mx=st[u]; l8=None; acc=None
            for j in range(i+1):
                p=jnp.exp(s_scr[u%2,j*BQ:(j+1)*BQ,:]-mx)
                ll=p.reshape(BQ//8,8,BQ).sum(0)
                l8=ll if l8 is None else l8+ll
                pv=dot(vt_scr[hs[h],j*BQ:(j+1)*BQ],p.astype(bf16))
                acc=pv if acc is None else acc+pv
                yield
            l=l8.sum(0,keepdims=True)
            o=(acc*(1.0/l)).astype(bf16)
            for t in range(sub): ot_ref[i*sub+t,m,hs[h],:]=o[:,t*n:(t+1)*n]
            lse_ref[m*hb+h,:,c0:c0+BQ]=mx+jnp.log(l)
        merge(phase_a(0))
        for u in range(len(units)):
            gs=[phase_b(u)]
            if u+1<len(units): gs=[phase_a(u+1)]+gs
            merge(*gs)
        for b in range(NB):
            mix_ref[b,0,m]=ot_ref[b*G+g0,m]
            for i in range(G-1):
                rcopy(ot_ref.at[b*G+pidx[i],m],mix_ref.at[b,back[i],m],mix_s.at[i,b,m],mix_r.at[back[i],b,m],pdev[i]).start()
        return 0
    lax.fori_loop(0,4,block,0)
    for m in (1,2):
        arrived(w2_scr.at[m],w2_r.at[m])
        share(m)
    for i in range(2*Z): arrived(wd_scr.at[i],dd_r.at[i])
    transpose_rows(wd_scr,w2_scr.at[3])
    share(3)
    for j in range(NB): arrived(coto_ref.at[j],cot_r.at[j])
    for i in range(G-1):
        for b in range(NB):
            for m in range(4):
                arrived(mix_ref.at[b,fore[i],m],mix_r.at[fore[i],b,m])
                rcopy(ot_ref.at[b*G+pidx[i],m],mix_ref.at[b,back[i],m],mix_s.at[i,b,m],mix_r.at[back[i],b,m],pdev[i]).wait_send()
        for m in range(4): arrived(w2o_ref.at[fore[i],m],gr_r.at[fore[i],m])
    for m in range(4):
        loc[m].wait()
        for cp in grp[m]: cp.wait_send()
    for cps in (ca,cb,cc,cd):
        for cp in cps[1:]: cp.wait_send()
    for cp in wcp+w2cp+ains+[d3,o3]: cp.wait_send()
    spread_sent(toks); spread_sent(cots)

def forward(Z, C, tokens, w1h, w2h, cot, gain, pd, segk, segq):
    R,Pn,D=tokens.shape; G=2*C; n=Pn//G; _,Dd,nC=w1h.shape; NB=4*C
    L=segq.shape[1]; W=pd.shape[0]; hb=W//HD
    V=pl.BlockSpec(memory_space=pltpu.VMEM); A=pl.BlockSpec(memory_space=pl.ANY)
    S=lambda *sh: pltpu.SemaphoreType.DMA(sh) if sh else pltpu.SemaphoreType.DMA
    B=lambda *sh: jax.ShapeDtypeStruct(sh,bf16)
    col=pltpu.VMEM((2*Z,Dd,nC),bf16); half=pltpu.VMEM((2,Dd,nC),bf16)
    return pl.pallas_call(functools.partial(fwd_kernel,Z,C,n),
        out_shape=(B(NB,n,D),B(NB*G,n,D),B(4,nC,D),B(G,4,nC,D),B(NB,n,D),B(NB,G,4,W,n),B(4,W,L),B(4,W,L),
                   B(4*hb,L,HD),B(4*hb,L,HD),B(NB*G,4,W,n),jax.ShapeDtypeStruct((4*hb,1,L),f32)),
        in_specs=[A,A,A,A,V,V,V,V],out_specs=(V,V,V,A,A,V,V,V,V,V,V,V),
        scratch_shapes=[col,col,col,col,half,half,pltpu.VMEM((4,nC,D),bf16),pltpu.VMEM((W,L),bf16),pltpu.VMEM((2,L,BQ),f32),
            S(NB),S(NB),S(G-1,NB),S(NB*G),S(2*Z),S(2*Z),S(2*Z),S(2*Z),S(2*Z),S(2*Z),S(2*Z),S(2*Z),S(),S(),S(2),
            S(4),S(4),S(4),S(4),S(G-1,4),S(G,4),S(4),S(NB),S(NB),S(G-1,NB,4),S(G,NB,4)],
        compiler_params=pltpu.CompilerParams(collective_id=0,has_side_effects=True,vmem_limit_bytes=60*2**20),
        cost_estimate=pl.CostEstimate(flops=3*10**10,bytes_accessed=10**8,transcendentals=0),
        name="forward")(tokens,w1h,w2h,cot,gain[None],pd,segk,segq)


def assemble_kernel(Z, zi_ref, *refs):
    parts,out,scr=refs[:Z],refs[Z],refs[Z+1]
    for j in range(Z):
        scr[zi_ref[0]^j]=parts[j][...]
    transpose_rows(scr,out)

def assemble(zi, parts):
    Z=len(parts); rows,nC=parts[0].shape
    V=pl.BlockSpec(memory_space=pltpu.VMEM)
    return pl.pallas_call(functools.partial(assemble_kernel,Z),out_shape=jax.ShapeDtypeStruct((nC,Z*rows),bf16),
        in_specs=[pl.BlockSpec(memory_space=pltpu.SMEM)]+[V]*Z,out_specs=V,
        scratch_shapes=[pltpu.VMEM((Z,rows,nC),bf16)],
        compiler_params=pltpu.CompilerParams(vmem_limit_bytes=56*2**20),name="assemble")(zi[None],*parts)

def split_kernel(Z, nr, zi_ref, own_ref, *refs):
    recvs,outs,scr=refs[:nr],refs[nr:nr+Z],refs[nr+Z]
    nC,D=own_ref.shape; rows=D//Z
    per=max(1,640//rows)
    for i in range(Z//per):
        ls=slice(i*per*rows,(i+1)*per*rows)
        t=own_ref[:,ls].astype(f32)
        for r in recvs: t=t+r[:,ls].astype(f32)
        scr[i*per:(i+1)*per]=t.T.reshape(per,rows,nC)
    for j in range(Z):
        outs[j][...]=scr[zi_ref[0]^j].astype(outs[j].dtype)

def split(zi, Z, own, recvs):
    nC,D=own.shape
    V=pl.BlockSpec(memory_space=pltpu.VMEM)
    return pl.pallas_call(functools.partial(split_kernel,Z,len(recvs)),
        out_shape=tuple(jax.ShapeDtypeStruct((D//Z,nC),f32 if j==0 else bf16) for j in range(Z)),
        in_specs=[pl.BlockSpec(memory_space=pltpu.SMEM)]+[V]*(1+len(recvs)),out_specs=(V,)*Z,
        scratch_shapes=[pltpu.VMEM((Z,D//Z,nC),f32)],
        compiler_params=pltpu.CompilerParams(vmem_limit_bytes=56*2**20),name="split")(zi[None],own,*recvs)


scale_base = 1.442695041

def silu_slope(u):
    sg=jax.nn.sigmoid(u)
    return sg*(1.0+u*(1.0-sg))

def make_local(Z, C):
    sizes=(Z,2,4,C)
    coords=list(itertools.product(*[range(n) for n in sizes]))
    lin={c:i for i,c in enumerate(coords)}
    G=2*C
    def pp(x, fn):
        return lax.ppermute(x, AXES, [(lin[c], lin[fn(*c)]) for c in coords])
    def unxor(parts, idx):
        b=1
        while b<len(parts):
            c=(idx & b)!=0
            parts=[jnp.where(c,parts[a^b],parts[a]) for a in range(len(parts))]
            b*=2
        return parts
    def allsum(v):
        for ax,n in enumerate(sizes):
            b=1
            while b<n:
                v=v+pp(v,lambda *c,ax=ax,b=b: tuple(ci^b if i==ax else ci for i,ci in enumerate(c)))
                b*=2
        return v
    def gsend(x, gamma):
        gc,gs=divmod(gamma,C)
        return pp(x, lambda z,k,q,s: (z,k^gc,q,s^gs))

    def after(x, *deps):
        return lax.optimization_barrier((x,)+deps)[0] if deps else x

    def local(tokens, segments, attn_gain, w_query, w_key, w_value, w_out, query_scale, mlp_gain, w_up, w_down, cotangent):
        zi,k,qi,si=[lax.axis_index(a) for a in AXES]
        R,Pn,D=tokens.shape; L=segments.shape[1]
        n=Pn//G
        N=4*C*n
        Dd,Ct=w_query.shape; Ch=Ct//2; W=Ch; hb=W//HD
        g0=k*C+si
        k0=k==0
        q0=2*(k^(qi//2))+qi%2
        rounds=list(itertools.product(range(2),range(2),range(C)))

        def spread(x):
            got=[]
            for eta,rho,sg in rounds:
                r=(qi%2)^rho; h=(qi//2)^k^eta; s2=si^sg
                piece=lax.dynamic_slice(x,(r,(h*C+s2)*n,0),(1,n,D))[0]
                got.append(pp(piece, lambda z,kk,q,s: (z,(q//2)^kk^eta,2*kk+((q%2)^rho),s^sg)))
            return jnp.concatenate(unxor(got,q0*C+si),0)
        def collect(y):
            parts=unxor([y[i*n:(i+1)*n] for i in range(4*C)],q0*C+si)
            got=[]
            for idx,(eta,rho,sg) in enumerate(rounds):
                got.append(pp(parts[idx], lambda z,kk,q,s: (z,q//2,(2*(kk^(q//2))+q%2)^(2*eta+rho),s^sg)))
            ab=unxor(got,((qi//2)^k)*(2*C)+(qi%2)*C+si)
            rows=[jnp.concatenate([ab[(h*2+r)*C+s2] for h in range(2) for s2 in range(C)],0) for r in range(R)]
            return jnp.stack(rows,0)
        def halves(shards):
            return jnp.stack([jnp.concatenate([w[:,h*Ch:(h+1)*Ch] for w in shards],1) for h in range(2)],0)
        def gatherD(w2h, *deps):
            keep=jnp.where(k0,w2h[0],w2h[1]); send=jnp.where(k0,w2h[1],w2h[0])
            recv=pp(send,lambda z,kk,q,s:(z,1-kk,q,s))
            rows=jnp.concatenate([jnp.where(k0,keep,recv),jnp.where(k0,recv,keep)],0)
            rows=after(rows,*deps)
            parts=[rows]+[pp(rows,lambda z,kk,q,s:(z^j,kk,q,s)) for j in range(1,Z)]
            return assemble(zi,parts),parts[-1]
        def chip(x, m):
            return pp(x,lambda z,kk,q,s:(z,kk,q^m,s))
        def reduceZ(rel):
            tot=rel[0]
            for j in range(1,Z):
                tot=tot+pp(rel[j],lambda z,kk,q,s:(z^j,kk,q,s)).astype(f32)
            return tot
        def finish(tot, nw):
            keep=jnp.where(k0,tot[:Dd],tot[Dd:]); send=jnp.where(k0,tot[Dd:],tot[:Dd])
            recv=pp(send,lambda z,kk,q,s:(z,1-kk,q,s))
            lo=jnp.where(k0,keep,recv); hi=jnp.where(k0,recv,keep)
            return [jnp.concatenate([lo[:,i*Ch:(i+1)*Ch],hi[:,i*Ch:(i+1)*Ch]],1) for i in range(nw)]
        def tok_lanes(xT):
            return [jnp.concatenate([xT[:,(b*G+g)*n:(b*G+g+1)*n] for b in range(4*C)],1) for g in range(G)]
        def tok_rows_join(parts):
            return jnp.concatenate([parts[g][b*n:(b+1)*n] for b in range(4*C) for g in range(G)],0)
        def tok_lanes_join(parts):
            return jnp.concatenate([parts[g][:,b*n:(b+1)*n] for b in range(4*C) for g in range(G)],1)

        seg_o=pp(segments,lambda z,kk,q,s:(z,1-kk,q,s))
        seg2=jnp.where(k==qi//2,segments,seg_o)
        seg=jnp.where(qi%2==0,seg2[0],seg2[1])
        first=seg[::BQ]; last=seg[BQ-1::BQ]
        segk=jnp.broadcast_to(seg[:,None],(L,128)); segq=seg[None]
        per_dim=scale_base/math.sqrt(HD)*jax.nn.softplus(query_scale)
        pd=jnp.broadcast_to(jnp.tile(per_dim,hb)[:,None],(W,128))
        w1h=halves([w_query,w_key,w_value]); w2h=halves([w_out.T,w_up,w_down.T])
        xo,ain,wts,w2o,cot,mix,qt,kt,kn,vn,ot,lse=forward(Z,C,tokens,w1h,w2h,cotangent,attn_gain,pd,segk,segq)
        x=xo.reshape(N,D).astype(f32); ain=ain.reshape(L,D); cot=cot.reshape(N,D)
        otT=jnp.concatenate([ot[i] for i in range(4*C*G)],-1)
        saved=[(qt[m],kt[m],kn[m*hb:(m+1)*hb],vn[m*hb:(m+1)*hb],otT[m],lse[m*hb:(m+1)*hb]) for m in range(4)]
        mixT_own=jnp.concatenate([mix[b].reshape(G*4*W,n) for b in range(4*C)],1)
        wo,wu,wd=[w2o[:,:,i*Ch:(i+1)*Ch].reshape(G*4*Ch,D) for i in range(3)]

        inv1=lax.rsqrt(jnp.mean(x*x,axis=-1,keepdims=True)+norm_eps)
        attn=dot(mixT_own,wo,TN)
        middle=x+attn
        inv2=lax.rsqrt(jnp.mean(middle*middle,axis=-1,keepdims=True)+norm_eps)
        norm2=middle*inv2
        mlp_in=(norm2*mlp_gain).astype(bf16)
        up=dot(mlp_in,wu,NT)
        hid=jax.nn.silu(up).astype(bf16)
        block=(middle+dot(hid,wd)).astype(bf16)
        block_out=collect(block)
        gup=(dot(cot,wd,NT)*silu_slope(up)).astype(bf16)
        gmlp=dot(gup,wu)
        dn=gmlp*mlp_gain
        gmid=cot.astype(f32)+inv2*(dn-norm2*jnp.mean(dn*norm2,axis=-1,keepdims=True))
        mlp_gain_part=jnp.sum(gmlp*norm2,axis=0)
        gattn=gmid.astype(bf16)
        gmixT=dot(wo,gattn,NT).astype(bf16)
        K=gmixT.shape[0]//G
        doT=tok_lanes_join(unxor([gmixT[:K]]+[gsend(gmixT[g*K:(g+1)*K],g) for g in range(1,G)],g0))
        g3=[dot(mixT_own,gattn),dot(gup,mlp_in,TN),dot(hid,cot,TN)]

        K4=4*Ch
        mine=list(g3)
        mine=[t[:K4] for t in g3]
        for g in range(1,G):
            for i,t in enumerate(g3):
                mine[i]=mine[i]+gsend(t[g*K4:(g+1)*K4].astype(bf16),g).astype(f32)
        fb=[jnp.concatenate([t[m*Ch:(m+1)*Ch] for t in mine],0) for m in range(4)]
        gT=[None]*4; dW=[None]*4; sc=0.0
        def bwd(m,*deps):
            qt,kt,kn,vn,ot,lse=saved[m]
            qt=after(qt,*deps)
            gT[m],s_=attn_bwd(first,last,qt,kt,kn,vn,ot,doT[m*W:(m+1)*W],lse,pd,segk,segq)
            return s_[:,0]
        sc=sc+bwd(3)
        dW[3]=dot(gT[3],ain).astype(bf16)
        fr=[chip(fb[m].astype(bf16),m) for m in (1,2)]
        f3=reduceZ(split(zi,Z,fb[3],[]))
        sc=sc+bwd(1,gT[3],fb[0])
        dW[1]=dot(gT[1],ain).astype(bf16)
        q1=chip(dW[1],1)
        f0=reduceZ(split(zi,Z,fb[0],fr))
        f3=chip(f3.astype(bf16),3)
        sc=sc+bwd(2,gT[1],fr[0],fr[1])
        dW[2]=dot(gT[2],ain).astype(bf16)
        q2=chip(dW[2],2)
        q3=reduceZ(split(zi,Z,after(dW[3],f0),[]))
        sc=sc+bwd(0,gT[2],f0,q1)
        q3=chip(after(q3,gT[0]).astype(bf16),3)
        g_out,g_up,g_down=finish(f0+f3.astype(f32),3)
        grad_out=g_out.T; grad_up=g_up; grad_down=g_down.T
        gTall=jnp.concatenate(gT,0); wtall=jnp.concatenate(wts,0)
        grel=unxor(tok_lanes(gTall),g0)
        gain=0.0
        for g in range(1,G):
            gain=gain+gsend(dot(grel[g],wtall,TN).astype(bf16),g).astype(f32)
        gain=gain+dot(grel[0],wtall,TN)
        norm1=x*inv1
        dn1=gain*attn_gain
        gin=gmid+inv1*(dn1-norm1*jnp.mean(dn1*norm1,axis=-1,keepdims=True))
        attn_gain_part=jnp.sum(gain*norm1,axis=0)
        ginb=gin.astype(bf16)
        input_grad=collect(ginb).astype(f32)
        dW[0]=dot(after(gT[0],ginb),ain)
        q0s=reduceZ(split(zi,Z,dW[0],[q1,q2]))
        grad_query,grad_key,grad_value=finish(q0s+q3.astype(f32),3)

        scale_part=jnp.sum(sc.reshape(hb,HD),axis=0)*(scale_base/math.sqrt(HD))*jax.nn.sigmoid(query_scale)
        grad_mlp_gain=allsum(mlp_gain_part)
        late=allsum(jnp.concatenate([attn_gain_part,scale_part]))
        return (block_out,input_grad,late[:D],grad_query,grad_key,grad_value,grad_out,late[D:],grad_mlp_gain,grad_up,grad_down)
    return local

def solution(mesh):
    dp,T=mesh.shape["dp"],mesh.shape["tensor"]
    Z,C=dp//2,T//4
    fine=Mesh(mesh.devices.reshape(Z,2,4,C),AXES)
    dpx=("zz","core"); tx=("q","s")
    in_specs=(P(dpx,tx,None),P(dpx,None),P(),P(dpx,tx),P(dpx,tx),P(dpx,tx),P(tx,dpx),P(),P(),P(dpx,tx),P(tx,dpx),P(dpx,tx,None))
    out_specs=(P(dpx,tx,None),P(dpx,tx,None),P(),P(dpx,tx),P(dpx,tx),P(dpx,tx),P(tx,dpx),P(),P(),P(dpx,tx),P(tx,dpx))
    return jax.shard_map(make_local(Z,C),mesh=fine,in_specs=in_specs,out_specs=out_specs,check_vma=False)
```

profile of v0, /device:TPU:6, one launch (start us, length us, event | category | flops | bytes accessed | tf_op | source)
XLA Modules:
  0.0 608.0 jit_solution(14285903015392982094)
XLA Ops:
  12.5 144.4 %forward.1 = (bf16[4,256,1280]{2,1,0:T(8,128)(2,1)}, bf16[8,256,1280]{2,1,0:T(8,128)(2,1)}, bf16[4,480,1280]{2,1,0:T(8,128)(2,1)}, bf16[2,4,480,1280]{3,2,1,0:T(...) custom-call(bf16[2,512,1280]{2,1,0:T(8,128)(2,1)} %x_ref.1, ...), custom_call_target="tpu_custom_call" | custom-call | flops 30000001024 | bytes 100000000 | tf_op jit(solution)/shard_map/forward/pallas_call | solution.py:431
  167.5 5.5 fusion.30
  173.0 6.9 %add_convert_fusion = bf16[1024,1280]{1,0:T(8,128)(2,1)S(1)} fusion(f32[1024,1280]{1,0:T(8,128)S(1)} %get-tuple-element.209, bf16[1280,1280]{1,0:T(8,128)(2,1)S(1)} %bitcast.128, f32[1024,1280]{1,0:T(8,128)} %fusion.30), kind=kOutput, calls=%fused_computation.18 | convolution fusion | flops 3364618240 | bytes 16384000 | tf_op jit(solution)/shard_map/dot_general | solution.py:19
  179.9 6.7 %multiply_convert_fusion = bf16[1024,1280]{1,0:T(8,128)(2,1)S(1)} fusion(f32[1024,1280]{1,0:T(8,128)} %fusion.30, bf16[1024,1280]{1,0:T(8,128)(2,1)S(1)} %bitcast.130, bf16[1280,1280]{1,0:T(8,128)(2,1)S(1)} %bitcast.129), kind=kOutput, calls=%fused_computation.17 | convolution fusion | flops 3367239680 | bytes 13762560 | tf_op jit(solution)/shard_map/dot_general | solution.py:19
  186.6 8.9 %fusion.31 = f32[1280,1280]{1,0:T(8,128)} fusion(bf16[1024,1280]{1,0:T(8,128)(2,1)S(1)} %bitcast.131, f32[1024,1280]{1,0:T(8,128)} %fusion.30), kind=kOutput, calls=%fused_computation.164 | convolution fusion | flops 3361996800 | bytes 14417920 | tf_op jit(solution)/shard_map/dot_general | solution.py:19
  199.6 6.1 fusion.29
  207.6 5.0 convolution_convert_fusion
  212.6 5.8 fusion.21
  240.4 11.8 %collective-permute-start.39 = (f32[1280]{0:T(1024)S(1)}, f32[1280]{0:T(1024)S(1)}, u32[]{:S(2)}, u32[]{:S(2)}) collective-permute-start(f32[1280]{0:T(1024)S(1)} %get-tuple-element.95), channel_id=1, source_target_pairs={{0,8},{1,9},{2,10},{3,11},{4,12},{5,13},{6,14},{7,15},{8,0},{9,1},... | collective-permute-start | bytes 15368 | tf_op jit(solution)/shard_map/ppermute | solution.py:491
  292.4 24.7 %attn_bwd.4 = (bf16[480,2048]{1,0:T(8,128)(2,1)}, f32[160,128]{1,0:T(8,128)}) custom-call(s32[8]{0:T(128)} %slice.413.first_ref, s32[8]{0:T(128)} %slice.414.last_ref, bf16[160,2048]{1,0:T(8,128)(2,1)} %get-tuple-element.154.qt_ref, bf16[160,2048]{1,0:T(8,128)(2,1)} %get-tuple-element.153.kt_ref, bf16[2,2048,80]{2,1,0:T(8,128)(2,1)} %get-tuple-element.125.k_ref, ...), custom_call_target="tpu_custom_call" | custom-call | flops 10737418240 | bytes 5242880 | tf_op jit(solution)/shard_map/attn_bwd/pallas_call | solution.py:204
  336.8 25.3 %attn_bwd.5 = (bf16[480,2048]{1,0:T(8,128)(2,1)}, f32[160,128]{1,0:T(8,128)}) custom-call(s32[8]{0:T(128)} %slice.413.first_ref, s32[8]{0:T(128)} %slice.414.last_ref, bf16[160,2048]{1,0:T(8,128)(2,1)} %get-tuple-element.64.qt_ref, bf16[160,2048]{1,0:T(8,128)(2,1)} %get-tuple-element.152.kt_ref, bf16[2,2048,80]{2,1,0:T(8,128)(2,1)} %get-tuple-element.124.k_ref, ...), custom_call_target="tpu_custom_call" | custom-call | flops 10737418240 | bytes 5242880 | tf_op jit(solution)/shard_map/attn_bwd/pallas_call | solution.py:204
  362.1 6.9 %convolution_convert_fusion.3 = bf16[480,1280]{1,0:T(8,128)(2,1)} fusion(bf16[480,2048]{1,0:T(8,128)(2,1)} %get-tuple-element.65, bf16[2048,1280]{1,0:T(8,128)(2,1)} %bitcast.148), kind=kOutput, calls=%fused_computation.41 | convolution fusion | flops 2517196800 | bytes 8437760 | tf_op jit(solution)/shard_map/dot_general | solution.py:19
  381.4 24.8 %attn_bwd.6 = (bf16[480,2048]{1,0:T(8,128)(2,1)}, f32[160,128]{1,0:T(8,128)}) custom-call(s32[8]{0:T(128)} %slice.413.first_ref, s32[8]{0:T(128)} %slice.414.last_ref, bf16[160,2048]{1,0:T(8,128)(2,1)} %get-tuple-element.66.qt_ref, bf16[160,2048]{1,0:T(8,128)(2,1)} %get-tuple-element.151.kt_ref, bf16[2,2048,80]{2,1,0:T(8,128)(2,1)} %get-tuple-element.123.k_ref, ...), custom_call_target="tpu_custom_call" | custom-call | flops 10737418240 | bytes 5242880 | tf_op jit(solution)/shard_map/attn_bwd/pallas_call | solution.py:204
  408.1 25.7 %attn_bwd.7 = (bf16[480,2048]{1,0:T(8,128)(2,1)}, f32[160,128]{1,0:T(8,128)}) custom-call(s32[8]{0:T(128)} %slice.413.first_ref, s32[8]{0:T(128)} %slice.414.last_ref, bf16[160,2048]{1,0:T(8,128)(2,1)} %get-tuple-element.73.qt_ref, bf16[160,2048]{1,0:T(8,128)(2,1)} %get-tuple-element.150.kt_ref, bf16[2,2048,80]{2,1,0:T(8,128)(2,1)} %get-tuple-element.122.k_ref, ...), custom_call_target="tpu_custom_call" | custom-call | flops 10737418240 | bytes 5242880 | tf_op jit(solution)/shard_map/attn_bwd/pallas_call | solution.py:204
  440.3 14.7 %fusion.18 = bf16[1024,1280]{1,0:T(8,128)(2,1)} fusion(bf16[1920,1280]{1,0:T(8,128)(2,1)} %bitcast.152, pred[]{:T(512)S(6)} %ne.49, bf16[1920,256]{1,0:T(8,128)(2,1)S(1)} %get-tuple-element.111, bf16[1920,256]{1,0:T(8,128)(2,1)S(1)} %get-tuple-element.112, bf16[1920,256]{1,0:T(8,128)(2,1)S(1)} %get-tuple-element.113, ...), kind=kOutput, calls=%fused_computation.31 | convolution fusion | flops 5067898880 | bytes 15400961 | tf_op jit(solution)/shard_map/dot_general | solution.py:19
  455.2 6.3 %convolution_convert_fusion.1.own_ref = bf16[480,1280]{1,0:T(8,128)(2,1)} fusion(bf16[480,2048]{1,0:T(8,128)(2,1)S(1)} %copy-done.10, bf16[2048,1280]{1,0:T(8,128)(2,1)} %bitcast.149), kind=kOutput, calls=%fused_computation.39 | convolution fusion | flops 2517196800 | bytes 8437760 | tf_op jit(solution)/shard_map/dot_general | solution.py:19
  461.5 6.3 %convolution_convert_fusion.2 = bf16[480,1280]{1,0:T(8,128)(2,1)} fusion(bf16[480,2048]{1,0:T(8,128)(2,1)S(1)} %copy-done.13, bf16[2048,1280]{1,0:T(8,128)(2,1)} %bitcast.150), kind=kOutput, calls=%fused_computation.40 | convolution fusion | flops 2517196800 | bytes 8437760 | tf_op jit(solution)/shard_map/dot_general | solution.py:19
  476.2 7.3 %collective-permute-done.31 = bf16[320,480]{1,0:T(8,128)(2,1)} collective-permute-done((bf16[320,480]{1,0:T(8,128)(2,1)}, bf16[320,480]{1,0:T(8,128)(2,1)}, u32[]{:S(2)}, u32[]{:S(2)}) %collective-permute-start.31) | collective-permute-done | bytes 307232 | tf_op jit(solution)/shard_map/ppermute | solution.py:491
  483.5 12.6 %collective-permute-done.30 = bf16[320,480]{1,0:T(8,128)(2,1)} collective-permute-done((bf16[320,480]{1,0:T(8,128)(2,1)}, bf16[320,480]{1,0:T(8,128)(2,1)}, u32[]{:S(2)}, u32[]{:S(2)}) %collective-permute-start.30) | collective-permute-done | bytes 307232 | tf_op jit(solution)/shard_map/ppermute | solution.py:491
  500.0 15.2 %fusion.8 = (f32[1280]{0:T(1024)S(1)}, f32[1024]{0:T(1024)S(1)}, f32[1024,1280]{1,0:T(8,128)}) fusion(bf16[4,256,1280]{2,1,0:T(8,128)(2,1)S(1)} %copy-done.1, f32[1024]{0:T(1024)S(1)} %bitcast.145, f32[1280]{0:T(1024)S(1)} %copy-done.40, bf16[1920,1280]{1,0:T(8,128)(2,1)} %bitcast.153, pred[]{:T(512)S(6)} %ne.49, bf16[1920,256]{1,0:T(8,128)(2,1)S(1)} %copy-done.21, ...), kind=kOutput, calls=%fused_computation.11 | convolution fusion | flops 5078382592 | bytes 23283712 | tf_op jit(solution)/shard_map/dot_general | solution.py:19
  518.8 6.6 %fusion.58.own_ref = f32[480,1280]{1,0:T(8,128)} fusion(bf16[480,2048]{1,0:T(8,128)(2,1)S(1)} %copy-done.11, bf16[2048,1280]{1,0:T(8,128)(2,1)} %bitcast.151), kind=kOutput, calls=%fused_computation.191 | convolution fusion | flops 2516582400 | bytes 9666560 | tf_op jit(solution)/shard_map/dot_general | solution.py:19
  537.6 25.3 %collective-permute-done.21 = f32[1360]{0:T(1024)S(1)} collective-permute-done((f32[1360]{0:T(1024)S(1)}, f32[1360]{0:T(1024)S(1)}, u32[]{:S(2)}, u32[]{:S(2)}) %collective-permute-start.21) | collective-permute-done | bytes 5472 | tf_op jit(solution)/shard_map/ppermute | solution.py:491
  581.2 8.3 %collective-permute-done.16 = bf16[256,1280]{1,0:T(8,128)(2,1)S(1)} collective-permute-done((bf16[256,1280]{1,0:T(8,128)(2,1)S(1)}, bf16[256,1280]{1,0:T(8,128)(2,1)S(1)}, u32[]{:S(2)}, u32[]{:S(2)}) %collective-permute-start.16) | collective-permute-done | bytes 655392 | tf_op jit(solution)/shard_map/ppermute | solution.py:491
  589.5 14.2 %collective-permute-done.17 = bf16[256,1280]{1,0:T(8,128)(2,1)S(1)} collective-permute-done((bf16[256,1280]{1,0:T(8,128)(2,1)S(1)}, bf16[256,1280]{1,0:T(8,128)(2,1)S(1)}, u32[]{:S(2)}, u32[]{:S(2)}) %collective-permute-start.17) | collective-permute-done | bytes 655392 | tf_op jit(solution)/shard_map/ppermute | solution.py:491
  (308 shorter events, 180.7 us)
Async XLA Ops:
  220.2 64.4 %collective-permute-start.1 = (bf16[256,1280]{1,0:T(8,128)(2,1)}, bf16[256,1280]{1,0:T(8,128)(2,1)S(1)}, u32[]{:S(2)}, u32[]{:S(2)}) collective-permute-start(bf16[256,1280]{1,0:T(8,128)(2,1)} %get-tuple-element.165), channel_id=1, source_target_pairs={{0,3},{1,2},{2,5},{3,4},{4,1},{5,0},{6,7},{7,6},{8,11},{9,10},{10,... | collective-permute-start | bytes 1966088 | tf_op jit(solution)/shard_map/ppermute | solution.py:491
  220.2 64.9 %collective-permute-start.2 = (bf16[256,1280]{1,0:T(8,128)(2,1)}, bf16[256,1280]{1,0:T(8,128)(2,1)}, u32[]{:S(2)}, u32[]{:S(2)}) collective-permute-start(bf16[256,1280]{1,0:T(8,128)(2,1)} %get-tuple-element.163), channel_id=1, source_target_pairs={{0,2},{1,3},{2,4},{3,5},{4,0},{5,1},{6,6},{7,7},{8,10},{9,11},{10,... | collective-permute-start | bytes 1966088 | tf_op jit(solution)/shard_map/ppermute | solution.py:491
  224.2 61.0 %collective-permute-start.3 = (bf16[256,1280]{1,0:T(8,128)(2,1)}, bf16[256,1280]{1,0:T(8,128)(2,1)}, u32[]{:S(2)}, u32[]{:S(2)}) collective-permute-start(bf16[256,1280]{1,0:T(8,128)(2,1)} %get-tuple-element.162), channel_id=1, source_target_pairs={{0,1},{1,0},{2,7},{3,6},{4,3},{5,2},{6,5},{7,4},{8,9},{9,8},{10,15... | collective-permute-start | bytes 1966088 | tf_op jit(solution)/shard_map/ppermute | solution.py:491
  225.3 60.4 %collective-permute-start.4 = (bf16[256,1280]{1,0:T(8,128)(2,1)}, bf16[256,1280]{1,0:T(8,128)(2,1)}, u32[]{:S(2)}, u32[]{:S(2)}) collective-permute-start(bf16[256,1280]{1,0:T(8,128)(2,1)} %get-tuple-element.164), channel_id=1, source_target_pairs={{0,0},{1,1},{2,6},{3,7},{4,2},{5,3},{6,4},{7,5},{8,8},{9,9},{10,14... | collective-permute-start | bytes 1966088 | tf_op jit(solution)/shard_map/ppermute | solution.py:491
  284.6 32.5 %collective-permute-start.8 = (bf16[640,1280]{1,0:T(8,128)(2,1)}, bf16[640,1280]{1,0:T(8,128)(2,1)S(1)}, u32[]{:S(2)}, u32[]{:S(2)}) collective-permute-start(bf16[640,1280]{1,0:T(8,128)(2,1)} %slice.735), channel_id=1, source_target_pairs={{0,4},{1,5},{2,6},{3,7},{4,0},{5,1},{6,2},{7,3},{8,12},{9,13},{10,... | collective-permute-start | bytes 4915208 | tf_op jit(solution)/shard_map/ppermute | solution.py:491
  285.1 34.4 %collective-permute-start.7 = (bf16[640,1280]{1,0:T(8,128)(2,1)}, bf16[640,1280]{1,0:T(8,128)(2,1)S(1)}, u32[]{:S(2)}, u32[]{:S(2)}) collective-permute-start(bf16[640,1280]{1,0:T(8,128)(2,1)} %slice.736), channel_id=1, source_target_pairs={{0,4},{1,5},{2,6},{3,7},{4,0},{5,1},{6,2},{7,3},{8,12},{9,13},{10,... | collective-permute-start | bytes 4915208 | tf_op jit(solution)/shard_map/ppermute | solution.py:491
  285.2 36.9 %collective-permute-start.6 = (bf16[640,1280]{1,0:T(8,128)(2,1)}, bf16[640,1280]{1,0:T(8,128)(2,1)S(1)}, u32[]{:S(2)}, u32[]{:S(2)}) collective-permute-start(bf16[640,1280]{1,0:T(8,128)(2,1)} %slice.737), channel_id=1, source_target_pairs={{0,4},{1,5},{2,6},{3,7},{4,0},{5,1},{6,2},{7,3},{8,12},{9,13},{10,... | collective-permute-start | bytes 4915208 | tf_op jit(solution)/shard_map/ppermute | solution.py:491
  325.8 45.3 %collective-permute-start.9 = (bf16[480,1280]{1,0:T(8,128)(2,1)S(1)}, bf16[480,1280]{1,0:T(8,128)(2,1)S(1)}, u32[]{:S(2)}, u32[]{:S(2)}) collective-permute-start(bf16[480,1280]{1,0:T(8,128)(2,1)S(1)} %pad_maximum_fusion.6), channel_id=1, source_target_pairs={{0,1},{1,0},{2,3},{3,2},{4,5},{5,4},{6,7},{7,6},{8,9},{9,8},{10,11... | collective-permute-start | bytes 3686408 | tf_op jit(solution)/shard_map/ppermute | solution.py:491
  327.1 44.0 %collective-permute-start.10 = (bf16[480,1280]{1,0:T(8,128)(2,1)}, bf16[480,1280]{1,0:T(8,128)(2,1)S(1)}, u32[]{:S(2)}, u32[]{:S(2)}) collective-permute-start(bf16[480,1280]{1,0:T(8,128)(2,1)} %pad_maximum_fusion.7), channel_id=1, source_target_pairs={{0,2},{1,3},{2,0},{3,1},{4,6},{5,7},{6,4},{7,5},{8,10},{9,11},{10,... | collective-permute-start | bytes 3686408 | tf_op jit(solution)/shard_map/ppermute | solution.py:491
  332.4 36.6 %collective-permute-start.36 = (bf16[320,480]{1,0:T(8,128)(2,1)}, bf16[320,480]{1,0:T(8,128)(2,1)S(1)}, u32[]{:S(2)}, u32[]{:S(2)}) collective-permute-start(bf16[320,480]{1,0:T(8,128)(2,1)} %get-tuple-element.94), channel_id=1, source_target_pairs={{0,24},{1,25},{2,26},{3,27},{4,28},{5,29},{6,30},{7,31},{8,16},{9,... | collective-permute-start | bytes 921608 | tf_op jit(solution)/shard_map/ppermute | solution.py:491
  332.4 36.6 %collective-permute-start.35 = (bf16[320,480]{1,0:T(8,128)(2,1)}, bf16[320,480]{1,0:T(8,128)(2,1)S(1)}, u32[]{:S(2)}, u32[]{:S(2)}) collective-permute-start(bf16[320,480]{1,0:T(8,128)(2,1)} %get-tuple-element.93), channel_id=1, source_target_pairs={{0,16},{1,17},{2,18},{3,19},{4,20},{5,21},{6,22},{7,23},{8,24},{9,... | collective-permute-start | bytes 921608 | tf_op jit(solution)/shard_map/ppermute | solution.py:491
  332.4 36.6 %collective-permute-start.34 = (bf16[320,480]{1,0:T(8,128)(2,1)}, bf16[320,480]{1,0:T(8,128)(2,1)}, u32[]{:S(2)}, u32[]{:S(2)}) collective-permute-start(bf16[320,480]{1,0:T(8,128)(2,1)} %get-tuple-element.92), channel_id=1, source_target_pairs={{0,8},{1,9},{2,10},{3,11},{4,12},{5,13},{6,14},{7,15},{8,0},{9,1},... | collective-permute-start | bytes 921608 | tf_op jit(solution)/shard_map/ppermute | solution.py:491
  369.0 39.1 %collective-permute-start.14 = (bf16[480,1280]{1,0:T(8,128)(2,1)}, bf16[480,1280]{1,0:T(8,128)(2,1)S(1)}, u32[]{:S(2)}, u32[]{:S(2)}) collective-permute-start(bf16[480,1280]{1,0:T(8,128)(2,1)} %convolution_convert_fusion.3), channel_id=1, source_target_pairs={{0,1},{1,0},{2,3},{3,2},{4,5},{5,4},{6,7},{7,6},{8,9},{9,8},{10,11... | collective-permute-start | bytes 3686408 | tf_op jit(solution)/shard_map/ppermute | solution.py:491
  371.0 35.2 %collective-permute-start.37 = (bf16[320,480]{1,0:T(8,128)(2,1)S(1)}, bf16[320,480]{1,0:T(8,128)(2,1)S(1)}, u32[]{:S(2)}, u32[]{:S(2)}) collective-permute-start(bf16[320,480]{1,0:T(8,128)(2,1)S(1)} %add_convert_fusion.1), channel_id=1, source_target_pairs={{0,3},{1,2},{2,1},{3,0},{4,7},{5,6},{6,5},{7,4},{8,11},{9,10},{10,... | collective-permute-start | bytes 921608 | tf_op jit(solution)/shard_map/ppermute | solution.py:491
  377.0 29.2 %collective-permute-start.11 = (bf16[320,480]{1,0:T(8,128)(2,1)}, bf16[320,480]{1,0:T(8,128)(2,1)S(1)}, u32[]{:S(2)}, u32[]{:S(2)}) collective-permute-start(bf16[320,480]{1,0:T(8,128)(2,1)} %get-tuple-element.69), channel_id=1, source_target_pairs={{0,8},{1,9},{2,10},{3,11},{4,12},{5,13},{6,14},{7,15},{8,0},{9,1},... | collective-permute-start | bytes 921608 | tf_op jit(solution)/shard_map/ppermute | solution.py:491
  455.1 44.9 %collective-permute-start.15 = (bf16[1024,1280]{1,0:T(8,128)(2,1)}, bf16[1024,1280]{1,0:T(8,128)(2,1)}, u32[]{:S(2)}, u32[]{:S(2)}) collective-permute-start(bf16[1024,1280]{1,0:T(8,128)(2,1)} %fusion.18), channel_id=1, source_target_pairs={{0,4},{1,5},{2,6},{3,7},{4,0},{5,1},{6,2},{7,3},{8,12},{9,13},{10,... | collective-permute-start | bytes 7864328 | tf_op jit(solution)/shard_map/ppermute | solution.py:491
  483.5 41.9 %collective-permute-start.25 = (bf16[480,1280]{1,0:T(8,128)(2,1)}, bf16[480,1280]{1,0:T(8,128)(2,1)S(1)}, u32[]{:S(2)}, u32[]{:S(2)}) collective-permute-start(bf16[480,1280]{1,0:T(8,128)(2,1)} %convolution_convert_fusion.2), channel_id=1, source_target_pairs={{0,2},{1,3},{2,0},{3,1},{4,6},{5,7},{6,4},{7,5},{8,10},{9,11},{10,... | collective-permute-start | bytes 3686408 | tf_op jit(solution)/shard_map/ppermute | solution.py:491
  498.6 70.4 %collective-permute-start.32 = (bf16[320,480]{1,0:T(8,128)(2,1)}, bf16[320,480]{1,0:T(8,128)(2,1)}, u32[]{:S(2)}, u32[]{:S(2)}) collective-permute-start(bf16[320,480]{1,0:T(8,128)(2,1)} %convert_add_fusion.3), channel_id=1, source_target_pairs={{0,3},{1,2},{2,1},{3,0},{4,7},{5,6},{6,5},{7,4},{8,11},{9,10},{10,... | collective-permute-start | bytes 921608 | tf_op jit(solution)/shard_map/ppermute | solution.py:491
  530.8 38.1 %collective-permute-start.28 = (bf16[320,480]{1,0:T(8,128)(2,1)}, bf16[320,480]{1,0:T(8,128)(2,1)S(1)}, u32[]{:S(2)}, u32[]{:S(2)}) collective-permute-start(bf16[320,480]{1,0:T(8,128)(2,1)} %get-tuple-element.84), channel_id=1, source_target_pairs={{0,24},{1,25},{2,26},{3,27},{4,28},{5,29},{6,30},{7,31},{8,16},{9,... | collective-permute-start | bytes 921608 | tf_op jit(solution)/shard_map/ppermute | solution.py:491
  533.8 35.2 %collective-permute-start.27 = (bf16[320,480]{1,0:T(8,128)(2,1)}, bf16[320,480]{1,0:T(8,128)(2,1)S(1)}, u32[]{:S(2)}, u32[]{:S(2)}) collective-permute-start(bf16[320,480]{1,0:T(8,128)(2,1)} %get-tuple-element.83), channel_id=1, source_target_pairs={{0,16},{1,17},{2,18},{3,19},{4,20},{5,21},{6,22},{7,23},{8,24},{9,... | collective-permute-start | bytes 921608 | tf_op jit(solution)/shard_map/ppermute | solution.py:491
  534.3 34.7 %collective-permute-start.26 = (bf16[320,480]{1,0:T(8,128)(2,1)}, bf16[320,480]{1,0:T(8,128)(2,1)S(1)}, u32[]{:S(2)}, u32[]{:S(2)}) collective-permute-start(bf16[320,480]{1,0:T(8,128)(2,1)} %get-tuple-element.82), channel_id=1, source_target_pairs={{0,8},{1,9},{2,10},{3,11},{4,12},{5,13},{6,14},{7,15},{8,0},{9,1},... | collective-permute-start | bytes 921608 | tf_op jit(solution)/shard_map/ppermute | solution.py:491
  572.4 31.3 %collective-permute-start.17 = (bf16[256,1280]{1,0:T(8,128)(2,1)S(1)}, bf16[256,1280]{1,0:T(8,128)(2,1)S(1)}, u32[]{:S(2)}, u32[]{:S(2)}) collective-permute-start(bf16[256,1280]{1,0:T(8,128)(2,1)S(1)} %get-tuple-element.140), channel_id=1, source_target_pairs={{0,2},{1,3},{2,4},{3,5},{4,0},{5,1},{6,6},{7,7},{8,10},{9,11},{10,... | collective-permute-start | bytes 1966088 | tf_op jit(solution)/shard_map/ppermute | solution.py:491
  574.5 29.2 %collective-permute-start.18 = (bf16[256,1280]{1,0:T(8,128)(2,1)S(1)}, bf16[256,1280]{1,0:T(8,128)(2,1)S(1)}, u32[]{:S(2)}, u32[]{:S(2)}) collective-permute-start(bf16[256,1280]{1,0:T(8,128)(2,1)S(1)} %get-tuple-element.138), channel_id=1, source_target_pairs={{0,1},{1,0},{2,7},{3,6},{4,3},{5,2},{6,5},{7,4},{8,9},{9,8},{10,15... | collective-permute-start | bytes 1966088 | tf_op jit(solution)/shard_map/ppermute | solution.py:491
  574.6 30.1 %collective-permute-start.19 = (bf16[256,1280]{1,0:T(8,128)(2,1)S(1)}, bf16[256,1280]{1,0:T(8,128)(2,1)S(1)}, u32[]{:S(2)}, u32[]{:S(2)}) collective-permute-start(bf16[256,1280]{1,0:T(8,128)(2,1)S(1)} %get-tuple-element.141), channel_id=1, source_target_pairs={{0,0},{1,1},{2,6},{3,7},{4,2},{5,3},{6,4},{7,5},{8,8},{9,9},{10,14... | collective-permute-start | bytes 1966088 | tf_op jit(solution)/shard_map/ppermute | solution.py:491
  (69 other events, 682.7 us)
where the time goes:
time: 611 us; the launch traced here: 608 us
  Pallas kernels  260 us (43%)
  matrix products  109 us (18%)
  waiting for transfers between devices  76.6 us (13%)
  local copies, waits for them, and re-layouts  60.8 us (10%)
  starting transfers between devices  58.3 us (10%)
  other arithmetic  41.1 us (7%)
    pallas_call x1, Pallas kernels, forward(): pl.pallas_call(functools.partial(fwd_kernel, Z, C, n), out_shape=(B(NB, n...  144 us
    dot_general x15, matrix products, dot(): return lax.dot_general(a, b, dims, preferred_element_type=f32)  109 us
    pallas_call x4, Pallas kernels, attn_bwd(): pl.pallas_call(functools.partial(bwd_kernel, hb), out_shape=(jax.ShapeDty...  100 us
    ppermute x44, waiting for transfers between devices, pp(): return lax.ppermute(x, AXES, [(lin[c], lin[fn(*c)]) for c in coords])  76.6 us
    ppermute x44, starting transfers between devices, pp(): return lax.ppermute(x, AXES, [(lin[c], lin[fn(*c)]) for c in coords])  58.3 us
    unnamed x116, local copies, waits for them, and re-layouts  18.9 us
    pallas_call x4, Pallas kernels, split(): pl.pallas_call(functools.partial(split_kernel, Z, len(recvs)), out_shape=...  15.3 us
  transfers between devices with their start and end apart: 44, of which 12 were waited for; matrix products, arithmetic and copies ran while one was open for 18% of the time, Pallas kernels for 15%

commit v1 on v0

--- a/solution.py
+++ b/solution.py
@@ -275,8 +275,8 @@
     rcopy(ref,ref,sem,sem,(z,1-k,q,s)).wait_recv()
 
 def fwd_kernel(Z, C, n, x_ref, w1_ref, w2_ref, cot_ref, gain_ref, pd_ref, segk_ref, segq_ref,
-               xo_ref, ain_ref, wts_ref, w2o_ref, coto_ref, mix_ref, qt_ref, kt_ref, k_ref, v_ref, ot_ref, lse_ref,
-               wa_scr, wb_scr, wc_scr, wd_scr, d3_scr, o3_scr, w2_scr, vt_scr, s_scr,
+               xo_ref, ain_ref, wts_ref, w2o_ref, coto_ref, mix_ref, qkv_ref, ot_ref, lse_ref,
+               wa_scr, wb_scr, wc_scr, wd_scr, d3_scr, o3_scr, w2_scr, k_scr, s_scr,
                tok_s, tok_r, ain_s, ain_r, a_s, a_r, b_s, b_r, c_s, c_r, dd_s, dd_r, d3_s, o3_s, do_r,
                wt_s, wt_r, w2_s, w2_r, gr_s, gr_r, loc_s, cot_s, cot_r, mix_s, mix_r):
     z,k,q,s=[lax.axis_index(a) for a in AXES]
@@ -351,21 +351,19 @@
         for c in range(L//CH):
             cs=slice(c*CH,(c+1)*CH)
             r=dot(wts_ref[m],ain_ref[c*per:(c+1)*per].reshape(CH,D),NT)
-            qt_ref[m,:,cs]=(r[:W]*pd_ref[:,:1]).astype(bf16)
-            kt_ref[m,:,cs]=r[W:2*W].astype(bf16)
-            vt_scr[:,cs]=r[2*W:].astype(bf16)
+            qkv_ref[m,:W,cs]=(r[:W]*pd_ref[:,:1]).astype(bf16)
+            qkv_ref[m,W:,cs]=r[W:].astype(bf16)
             for h in range(hb):
-                k_ref[m*hb+h,cs,:]=r[W+h*HD:W+(h+1)*HD].T.astype(bf16)
-                v_ref[m*hb+h,cs,:]=r[2*W+h*HD:2*W+(h+1)*HD].T.astype(bf16)
+                k_scr[h,cs,:]=r[W+h*HD:W+(h+1)*HD].T.astype(bf16)
         units=[(i,h) for i in range(nb) for h in range(hb)]
         st={}
         def phase_a(u):
             i,h=units[u]; c0=i*BQ
-            qi=qt_ref[m,hs[h],c0:c0+BQ]
+            qi=qkv_ref[m,hs[h],c0:c0+BQ]
             sq=segq_ref[:,c0:c0+BQ]
             m8=None
             for j in range(i+1):
-                t=dot(k_ref[m*hb+h,j*BQ:(j+1)*BQ,:],qi)
+                t=dot(k_scr[h,j*BQ:(j+1)*BQ,:],qi)
                 sk=segk_ref[j*BQ:(j+1)*BQ,:]
                 ok=jnp.concatenate([sk]*(BQ//128),axis=1)==sq
                 if j==i: ok=ok&(rowi<=coli)
@@ -382,7 +380,7 @@
                 p=jnp.exp(s_scr[u%2,j*BQ:(j+1)*BQ,:]-mx)
                 ll=p.reshape(BQ//8,8,BQ).sum(0)
                 l8=ll if l8 is None else l8+ll
-                pv=dot(vt_scr[hs[h],j*BQ:(j+1)*BQ],p.astype(bf16))
+                pv=dot(qkv_ref[m,2*W+h*HD:2*W+(h+1)*HD,j*BQ:(j+1)*BQ],p.astype(bf16))
                 acc=pv if acc is None else acc+pv
                 yield
             l=l8.sum(0,keepdims=True)
@@ -429,10 +427,10 @@
     B=lambda *sh: jax.ShapeDtypeStruct(sh,bf16)
     col=pltpu.VMEM((2*Z,Dd,nC),bf16); half=pltpu.VMEM((2,Dd,nC),bf16)
     return pl.pallas_call(functools.partial(fwd_kernel,Z,C,n),
-        out_shape=(B(NB,n,D),B(NB*G,n,D),B(4,nC,D),B(G,4,nC,D),B(NB,n,D),B(NB,G,4,W,n),B(4,W,L),B(4,W,L),
-                   B(4*hb,L,HD),B(4*hb,L,HD),B(NB*G,4,W,n),jax.ShapeDtypeStruct((4*hb,1,L),f32)),
-        in_specs=[A,A,A,A,V,V,V,V],out_specs=(V,V,V,A,A,V,V,V,V,V,V,V),
-        scratch_shapes=[col,col,col,col,half,half,pltpu.VMEM((4,nC,D),bf16),pltpu.VMEM((W,L),bf16),pltpu.VMEM((2,L,BQ),f32),
+        out_shape=(B(NB,n,D),B(NB*G,n,D),B(4,nC,D),B(G,4,nC,D),B(NB,n,D),B(NB,G,4,W,n),B(4,nC,L),
+                   B(NB*G,4,W,n),jax.ShapeDtypeStruct((4*hb,1,L),f32)),
+        in_specs=[A,A,A,A,V,V,V,V],out_specs=(V,V,V,A,A,V,V,V,V),
+        scratch_shapes=[col,col,col,col,half,half,pltpu.VMEM((4,nC,D),bf16),pltpu.VMEM((hb,L,HD),bf16),pltpu.VMEM((2,L,BQ),f32),
             S(NB),S(NB),S(G-1,NB),S(NB*G),S(2*Z),S(2*Z),S(2*Z),S(2*Z),S(2*Z),S(2*Z),S(2*Z),S(2*Z),S(),S(),S(2),
             S(4),S(4),S(4),S(4),S(G-1,4),S(G,4),S(4),S(NB),S(NB),S(G-1,NB,4),S(G,NB,4)],
         compiler_params=pltpu.CompilerParams(collective_id=0,has_side_effects=True,vmem_limit_bytes=60*2**20),
@@ -440,40 +438,262 @@
         name="forward")(tokens,w1h,w2h,cot,gain[None],pd,segk,segq)
 
 
-def assemble_kernel(Z, zi_ref, *refs):
-    parts,out,scr=refs[:Z],refs[Z],refs[Z+1]
-    for j in range(Z):
-        scr[zi_ref[0]^j]=parts[j][...]
-    transpose_rows(scr,out)
-
-def assemble(zi, parts):
-    Z=len(parts); rows,nC=parts[0].shape
-    V=pl.BlockSpec(memory_space=pltpu.VMEM)
-    return pl.pallas_call(functools.partial(assemble_kernel,Z),out_shape=jax.ShapeDtypeStruct((nC,Z*rows),bf16),
-        in_specs=[pl.BlockSpec(memory_space=pltpu.SMEM)]+[V]*Z,out_specs=V,
-        scratch_shapes=[pltpu.VMEM((Z,rows,nC),bf16)],
-        compiler_params=pltpu.CompilerParams(vmem_limit_bytes=56*2**20),name="assemble")(zi[None],*parts)
-
-def split_kernel(Z, nr, zi_ref, own_ref, *refs):
-    recvs,outs,scr=refs[:nr],refs[nr:nr+Z],refs[nr+Z]
-    nC,D=own_ref.shape; rows=D//Z
-    per=max(1,640//rows)
-    for i in range(Z//per):
-        ls=slice(i*per*rows,(i+1)*per*rows)
-        t=own_ref[:,ls].astype(f32)
-        for r in recvs: t=t+r[:,ls].astype(f32)
-        scr[i*per:(i+1)*per]=t.T.reshape(per,rows,nC)
-    for j in range(Z):
-        outs[j][...]=scr[zi_ref[0]^j].astype(outs[j].dtype)
-
-def split(zi, Z, own, recvs):
-    nC,D=own.shape
-    V=pl.BlockSpec(memory_space=pltpu.VMEM)
-    return pl.pallas_call(functools.partial(split_kernel,Z,len(recvs)),
-        out_shape=tuple(jax.ShapeDtypeStruct((D//Z,nC),f32 if j==0 else bf16) for j in range(Z)),
-        in_specs=[pl.BlockSpec(memory_space=pltpu.SMEM)]+[V]*(1+len(recvs)),out_specs=(V,)*Z,
-        scratch_shapes=[pltpu.VMEM((Z,D//Z,nC),f32)],
-        compiler_params=pltpu.CompilerParams(vmem_limit_bytes=56*2**20),name="split")(zi[None],own,*recvs)
+def bwd_kernel(Z, C, n, qkv_ref, ot_ref, do_ref, lse_ref, pd_ref, segk_ref, segq_ref, ain_ref, wts_ref,
+               xo_ref, gmid_ref, gain_ref, vec_ref, fb_ref,
+               gi_ref, gwm_ref, gwq_ref, vo_ref,
+               kv_scr, k_scr, v_scr, p_scr, ds_scr, dq_scr, dl_scr, dv_scr, dk_scr, a_scr, st_scr, dw_scr, qr_scr, fr_scr, zs_scr, zr_scr, t3_scr, t3r_scr, ot_scr, do_scr,
+               dx_scr, dxr_scr, own_scr, xb_scr, gb_scr, va_scr, vb_scr, vs_scr, sc_scr,
+               fs, frs, qs, qrs, zss, zrs, t3s, t3rs, cs_, crs, dxs, dxrs, gis, girs, ld, al, otl, dol, kvl, xl, vas, vars_, vbs, vbrs):
+    z,k,q,s=[lax.axis_index(a) for a in AXES]
+    G=2*C; g0=k*C+s; NB=4*C
+    D=gain_ref.shape[1]; L=segq_ref.shape[1]; W=pd_ref.shape[0]; hb=W//HD; nb=L//BQ; sub=BQ//n
+    nC=3*W; Dd=gwm_ref.shape[1]
+    peers=list(itertools.product(range(2),range(C)))[1:]
+    pdev=[(z,lax.rem(k+gc,2),q,lax.rem(s+gs,C)) for gc,gs in peers]
+    pidx=[lax.rem(k+gc,2)*C+lax.rem(s+gs,C) for gc,gs in peers]
+    back=[gc*C+(C-gs)%C for gc,gs in peers]
+    fore=[gc*C+gs for gc,gs in peers]
+    chipdev=[(z,k,partner(q,m),s) for m in range(4)]
+    core=(z,1-k,q,s)
+    zdev=[lax.rem(z+j,Z) for j in range(Z)]
+    fcp={m: rcopy(fb_ref.at[m],fr_scr.at[m-1],fs.at[m],frs.at[m],chipdev[m]) for m in (1,2)}
+    qcp={m: rcopy(dw_scr.at[m-1],qr_scr.at[m-1],qs.at[m],qrs.at[m],chipdev[m]) for m in (1,2)}
+    zcp=[[rcopy(zs_scr.at[e%2,zdev[j]],zr_scr.at[e,z],zss.at[e,j],zrs.at[e,z],(zdev[j],k,q,s)) for j in range(1,Z)] for e in range(4)]
+    t3cp=[rcopy(t3_scr.at[e],t3r_scr.at[e],t3s.at[e],t3rs.at[e],chipdev[3]) for e in range(2)]
+    gws=(gwm_ref,gwq_ref)
+    ccp=[rcopy(t3_scr.at[e,pl.ds(pl.multiple_of((1-k)*Dd,Dd),Dd),:],gws[e].at[k],cs_.at[e],crs.at[e],core) for e in range(2)]
+    def load(src,dst,i):
+        cp=pltpu.make_async_copy(src,dst,ld.at[i]); cp.start(); return cp
+    def zsend(e, value):
+        rows=D//Z; per=max(1,640//rows)
+        for i in range(Z//per):
+            ls=slice(i*per*rows,(i+1)*per*rows)
+            zs_scr[e%2,i*per:(i+1)*per]=value(ls).T.reshape(per,rows,nC).astype(bf16)
+        for cp in zcp[e]: cp.start()
+    def zsum(e):
+        for cp in zcp[e]: cp.wait_send()
+        t=zs_scr[e%2,z].astype(f32)
+        for j in range(1,Z):
+            arrived(zr_scr.at[e,zdev[j]],zrs.at[e,zdev[j]])
+            t=t+zr_scr[e,zdev[j]].astype(f32)
+        return t
+    def diag(e):
+        t3_scr[e]=zsum(e)
+        t3cp[e].start()
+    def final(e):
+        t=zsum(2+e)
+        arrived(t3r_scr.at[e],t3rs.at[e])
+        t=t+t3r_scr[e]
+        t3cp[e].wait_send()
+        t3_scr[e]=t
+        ccp[e].start()
+        gws[e][k]=t3_scr[e,pl.ds(pl.multiple_of(k*Dd,Dd),Dd),:]
+    kvcp=[pltpu.make_async_copy(qkv_ref.at[m],kv_scr.at[m],kvl.at[m]) for m in range(4)]
+    for m in (3,2,1,0): kvcp[m].start()
+    acp=pltpu.make_async_copy(ain_ref,a_scr,al)
+    acp.start()
+    def otcp(m): return pltpu.make_async_copy(ot_ref.at[:,m],ot_scr,otl)
+    otcp(3).start()
+    def docp(idx): return pltpu.make_async_copy(do_ref.at[:,3-idx],do_scr.at[lax.rem(idx,2)],dol.at[lax.rem(idx,2)])
+    docp(0).start()
+    greet(Z,C)
+    for m in (1,2): fcp[m].start()
+    load(fb_ref.at[3],st_scr,0).wait()
+    zsend(0,lambda ls: st_scr[:,ls].astype(f32))
+    sc_scr[...]=jnp.zeros_like(sc_scr)
+    rowi=lax.broadcasted_iota(jnp.int32,(BQ,BQ),0)
+    coli=lax.broadcasted_iota(jnp.int32,(BQ,BQ),1)
+    hs=[slice(h*HD,(h+1)*HD) for h in range(hb)]
+    H2=BQ//2
+
+    def block(idx,_):
+        m=3-idx
+        pltpu.make_async_copy(qkv_ref.at[m],kv_scr.at[m],kvl.at[m]).wait()
+        for h in range(hb):
+            k_scr[h]=kv_scr[m,W+h*HD:W+(h+1)*HD,:].T
+            v_scr[h]=kv_scr[m,2*W+h*HD:2*W+(h+1)*HD,:].T
+        slot=lax.rem(idx,2)
+        docp(idx).wait()
+        @pl.when(idx<3)
+        def _(): docp(idx+1).start()
+        def tile(h,i):
+            return jnp.concatenate([do_scr[slot,i*sub+t,hs[h],:] for t in range(sub)],1) if sub>1 else do_scr[slot,i,hs[h],:]
+        otcp(m).wait()
+        for i in range(nb):
+            for h in range(hb):
+                for t in range(sub):
+                    B_=i*sub+t
+                    dl_scr[h,:,B_*n:(B_+1)*n]=(do_scr[slot,B_,hs[h],:].astype(f32)*ot_scr[B_,hs[h],:].astype(f32)).sum(0,keepdims=True)
+        @pl.when(m>0)
+        def _(): otcp(m-1).start()
+        units=[(j,h,i) for j in range(nb) for h in range(hb) for i in range(j,nb)]
+        def phase_a(u):
+            j,h,i=units[u]; cs=slice(i*BQ,(i+1)*BQ)
+            for a in range(2):
+                ks=slice(j*BQ+a*H2,j*BQ+(a+1)*H2)
+                t=dot(k_scr[h,ks,:],kv_scr[m,hs[h],cs])
+                dp=dot(v_scr[h,ks,:],tile(h,i))
+                sk=segk_ref[ks,:]
+                ok=jnp.concatenate([sk]*(BQ//128),axis=1)==segq_ref[:,cs]
+                if j==i: ok=ok&(rowi[a*H2:(a+1)*H2]<=coli[a*H2:(a+1)*H2])
+                p=jnp.exp(jnp.where(ok,t-lse_ref[m*hb+h,:,cs],NEG))
+                p_scr[u%2,a*H2:(a+1)*H2,:]=p.astype(bf16)
+                ds_scr[u%2,a*H2:(a+1)*H2,:]=(p*(dp-dl_scr[h,:,cs])).astype(bf16)
+                yield
+        def phase_b(u):
+            j,h,i=units[u]; js=slice(j*BQ,(j+1)*BQ); cs=slice(i*BQ,(i+1)*BQ)
+            p=p_scr[u%2]; ds=ds_scr[u%2]
+            dv=dot(tile(h,i),p,NT); dk=dot(kv_scr[m,hs[h],cs],ds,NT)
+            if i==j: dv_scr[h]=dv; dk_scr[h]=dk
+            else: dv_scr[h]+=dv; dk_scr[h]+=dk
+            yield
+            dq=dot(kv_scr[m,W+h*HD:W+(h+1)*HD,js],ds)
+            if j==0: dq_scr[hs[h],cs]=dq
+            else: dq_scr[hs[h],cs]+=dq
+            if i==nb-1:
+                kv_scr[m,W+h*HD:W+(h+1)*HD,js]=dk_scr[h].astype(bf16)
+                kv_scr[m,2*W+h*HD:2*W+(h+1)*HD,js]=dv_scr[h].astype(bf16)
+            yield
+        merge(phase_a(0))
+        for u in range(len(units)):
+            gs=[phase_b(u)]
+            if u+1<len(units): gs=[phase_a(u+1)]+gs
+            merge(*gs)
+        dq=dq_scr[...]
+        sc_scr[...]+=(dq*kv_scr[m,:W,:].astype(f32)).sum(1,keepdims=True)/pd_ref[:,:1]
+        kv_scr[m,:W,:]=(dq*pd_ref[:,:1]).astype(bf16)
+        @pl.when(idx==0)
+        def _():
+            acp.wait()
+            zsend(1,lambda ls: dwt(3,ls))
+        @pl.when((idx==1)|(idx==2))
+        def _():
+            for c in range(D//256):
+                ls=slice(c*256,(c+1)*256)
+                dw_scr[m-1,:,ls]=dwt(m,ls).astype(bf16)
+        @pl.when(idx==1)
+        def _():
+            qcp[2].start()
+            diag(0)
+            ld0=load(fb_ref.at[0],st_scr,0)
+            for m2 in (1,2): arrived(fr_scr.at[m2-1],frs.at[m2])
+            ld0.wait()
+            zsend(2,lambda ls: st_scr[:,ls].astype(f32)+fr_scr[0,:,ls].astype(f32)+fr_scr[1,:,ls].astype(f32))
+        @pl.when(idx==2)
+        def _():
+            qcp[1].start()
+            diag(1)
+        return 0
+    def dwt(m,ls):
+        return dot(kv_scr[m],a_scr[:,ls])
+    lax.fori_loop(0,4,block,0)
+    for m2 in (1,2): arrived(qr_scr.at[m2-1],qrs.at[m2])
+    zsend(3,lambda ls: dwt(0,ls)+qr_scr[0,:,ls].astype(f32)+qr_scr[1,:,ls].astype(f32))
+    wcp=[pltpu.make_async_copy(wts_ref.at[m],a_scr.at[pl.ds(m*nC,nC),:],kvl.at[m]) for m in range(4)]
+    for cp in wcp: cp.start()
+    for cp in wcp: cp.wait()
+
+    def chunk(i):
+        gl=kv_scr[:,:,pl.ds(pl.multiple_of(i*BQ,BQ),BQ)].reshape(4*nC,BQ)
+        return dot(gl,a_scr[:4*nC,:],TN)
+    def xload(b):
+        return [pltpu.make_async_copy(xo_ref.at[b],xb_scr.at[b%2],xl.at[0,b%2]),pltpu.make_async_copy(gmid_ref.at[b],gb_scr.at[b%2],xl.at[1,b%2])]
+    for cp in xload(0): cp.start()
+    dxcp=[[rcopy(dx_scr.at[i,b],dxr_scr.at[back[i]-1,b],dxs.at[i,b],dxrs.at[back[i],b],pdev[i]) for b in range(NB)] for i in range(G-1)]
+    for b in range(NB):
+        if sub==1:
+            for i in range(G-1):
+                dx_scr[i,b]=chunk(b*G+pidx[i]).astype(bf16)
+                dxcp[i][b].start()
+        else:
+            own_scr[...]=chunk(b)
+            for i in range(G-1):
+                dx_scr[i,b]=own_scr[pl.ds(pl.multiple_of(pidx[i]*n,n),n),:].astype(bf16)
+                dxcp[i][b].start()
+    gicp=[]
+    gpart=None
+    for b in range(NB):
+        if b+1<NB:
+            for cp in xload(b+1): cp.start()
+        if sub==1:
+            gain=chunk(b*G+g0)
+        else:
+            own_scr[...]=chunk(b)
+            gain=own_scr[pl.ds(pl.multiple_of(g0*n,n),n),:]
+        for i in range(G-1):
+            arrived(dxr_scr.at[fore[i]-1,b],dxrs.at[fore[i],b])
+            gain=gain+dxr_scr[fore[i]-1,b].astype(f32)
+        for cp in xload(b): cp.wait()
+        x=xb_scr[b%2].astype(f32)
+        inv=lax.rsqrt(jnp.mean(x*x,axis=-1,keepdims=True)+norm_eps)
+        nx=x*inv
+        dn=gain*gain_ref[...]
+        gin=gb_scr[b%2]+inv*(dn-nx*jnp.mean(dn*nx,axis=-1,keepdims=True))
+        gp=(gain*nx).reshape(n//8,8,D).sum(0)
+        gpart=gp if gpart is None else gpart+gp
+        dxcp[0][b].wait_send()
+        dx_scr[0,b]=gin.astype(bf16)
+        dst=gi_ref.at[lax.rem(q,2),pl.ds(pl.multiple_of((k*C+s)*n,n),n),:]
+        rs=girs.at[(lax.rem(q,2)*2+k)*C+s]
+        mine=(lax.div(q,2)==k)&(q==b//C)&(s==b%C)
+        gicp.append((mine,pltpu.make_async_copy(dx_scr.at[0,b],dst,rs),rcopy(dx_scr.at[0,b],dst,gis.at[b],rs,(z,lax.div(q,2),b//C,b%C))))
+        spread_start(gicp[-1:])
+    vs_scr[...]=jnp.zeros_like(vs_scr)
+    vs_scr[0:1,:]=gpart.sum(0,keepdims=True)
+    vs_scr[1:2,:]=vec_ref[...]
+    sc=sc_scr[0:HD,:]
+    for h in range(1,hb): sc=sc+sc_scr[h*HD:(h+1)*HD,:]
+    vs_scr[2:3,0:HD]=sc.T[0:1,:]
+    me=(k*4+q)*C+s
+    va_scr[me]=vs_scr[...]
+    plane=list(itertools.product(range(2),range(4),range(C)))[1:]
+    vacp=[rcopy(vs_scr,va_scr.at[me],vas.at[i],vars_.at[me],(z,lax.rem(k+a,2),lax.rem(q+b,4),lax.rem(s+c,C))) for i,(a,b,c) in enumerate(plane)]
+    for cp in vacp: cp.start()
+    final(0)
+    for a,b,c in plane:
+        o=(lax.rem(k+a,2)*4+lax.rem(q+b,4))*C+lax.rem(s+c,C)
+        arrived(va_scr.at[o],vars_.at[o])
+    t=va_scr[0]
+    for i in range(1,8*C): t=t+va_scr[i]
+    vb_scr[z]=t
+    vbcp=[rcopy(vb_scr.at[z],vb_scr.at[z],vbs.at[j],vbrs.at[z],(zdev[j],k,q,s)) for j in range(1,Z)]
+    for cp in vbcp: cp.start()
+    final(1)
+    for j in range(1,Z): arrived(vb_scr.at[zdev[j]],vbrs.at[zdev[j]])
+    t=vb_scr[0]
+    for i in range(1,Z): t=t+vb_scr[i]
+    vo_ref[...]=t
+    for e in range(2):
+        arrived(gws[e].at[1-k],crs.at[e])
+        ccp[e].wait_send()
+    for r in range(2):
+        for h in range(2):
+            for s2 in range(C):
+                arrived(gi_ref.at[r,pl.ds((h*C+s2)*n,n),:],girs.at[(r*2+h)*C+s2])
+    spread_sent(gicp)
+    for i in range(1,G-1):
+        for b in range(NB): dxcp[i][b].wait_send()
+    for m in (1,2):
+        fcp[m].wait_send(); qcp[m].wait_send()
+    for cp in vacp+vbcp: cp.wait_send()
+
+def backward(Z, C, qkv, ot, do, lse, pd, segk, segq, ain, wts, xo, gmid, gain, vec, fb, R, Pn, Dd):
+    NB,n,D=xo.shape; G=2*C; nC=wts.shape[1]; W=pd.shape[0]; hb=W//HD; L=segq.shape[1]
+    V=pl.BlockSpec(memory_space=pltpu.VMEM); A=pl.BlockSpec(memory_space=pl.ANY)
+    S=lambda *sh: pltpu.SemaphoreType.DMA(sh) if sh else pltpu.SemaphoreType.DMA
+    M=lambda *sh: pltpu.VMEM(sh,bf16)
+    F=lambda *sh: pltpu.VMEM(sh,f32)
+    gw=jax.ShapeDtypeStruct((2,Dd,nC),f32)
+    return pl.pallas_call(functools.partial(bwd_kernel,Z,C,n),
+        out_shape=(jax.ShapeDtypeStruct((R,Pn,D),bf16),gw,gw,jax.ShapeDtypeStruct((8,D),f32)),
+        in_specs=[A,A,A,V,V,V,V,A,A,A,A,V,V,A],out_specs=(A,V,V,V),
+        scratch_shapes=[M(4,nC,L),M(hb,L,HD),M(hb,L,HD),M(2,BQ,BQ),M(2,BQ,BQ),F(W,L),F(hb,1,L),F(hb,HD,BQ),F(hb,HD,BQ),M(L,D),
+            M(nC,D),M(2,nC,D),M(2,nC,D),M(2,nC,D),M(2,Z,D//Z,nC),M(4,Z,D//Z,nC),F(2,D//Z,nC),F(2,D//Z,nC),M(NB*G,W,n),M(2,NB*G,W,n),
+            M(G-1,NB,n,D),M(G-1,NB,n,D),F(BQ,D) if n<BQ else F(8,128),M(2,n,D),F(2,n,D),F(8*C,8,D),F(Z,8,D),F(8,D),F(W,1),
+            S(4),S(4),S(4),S(4),S(4,Z),S(4,Z),S(2),S(2),S(2),S(2),S(G,NB),S(G,NB),S(NB),S(4*C),S(4),S(),S(),S(2),S(4),S(2,2),S(8*C),S(8*C),S(Z),S(Z)],
+        compiler_params=pltpu.CompilerParams(collective_id=1,has_side_effects=True,vmem_limit_bytes=58*2**20),
+        cost_estimate=pl.CostEstimate(flops=6*10**10,bytes_accessed=10**8,transcendentals=0),
+        name="backward")(qkv,ot,do,lse,pd,segk,segq,ain.reshape(L,D),wts,xo,gmid,gain[None],vec[None],fb)
 
 
 scale_base = 1.442695041
@@ -572,10 +792,8 @@
         per_dim=scale_base/math.sqrt(HD)*jax.nn.softplus(query_scale)
         pd=jnp.broadcast_to(jnp.tile(per_dim,hb)[:,None],(W,128))
         w1h=halves([w_query,w_key,w_value]); w2h=halves([w_out.T,w_up,w_down.T])
-        xo,ain,wts,w2o,cot,mix,qt,kt,kn,vn,ot,lse=forward(Z,C,tokens,w1h,w2h,cotangent,attn_gain,pd,segk,segq)
-        x=xo.reshape(N,D).astype(f32); ain=ain.reshape(L,D); cot=cot.reshape(N,D)
-        otT=jnp.concatenate([ot[i] for i in range(4*C*G)],-1)
-        saved=[(qt[m],kt[m],kn[m*hb:(m+1)*hb],vn[m*hb:(m+1)*hb],otT[m],lse[m*hb:(m+1)*hb]) for m in range(4)]
+        xo,ain,wts,w2o,cot,mix,qkv,ot,lse=forward(Z,C,tokens,w1h,w2h,cotangent,attn_gain,pd,segk,segq)
+        x=xo.reshape(N,D).astype(f32); cot=cot.reshape(N,D)
         mixT_own=jnp.concatenate([mix[b].reshape(G*4*W,n) for b in range(4*C)],1)
         wo,wu,wd=[w2o[:,:,i*Ch:(i+1)*Ch].reshape(G*4*Ch,D) for i in range(3)]
 
@@ -597,7 +815,8 @@
         gattn=gmid.astype(bf16)
         gmixT=dot(wo,gattn,NT).astype(bf16)
         K=gmixT.shape[0]//G
-        doT=tok_lanes_join(unxor([gmixT[:K]]+[gsend(gmixT[g*K:(g+1)*K],g) for g in range(1,G)],g0))
+        gparts=unxor([gmixT[:K]]+[gsend(gmixT[g*K:(g+1)*K],g) for g in range(1,G)],g0)
+        do=jnp.stack([gparts[g][:,b*n:(b+1)*n].reshape(4,W,n) for b in range(4*C) for g in range(G)],0)
         g3=[dot(mixT_own,gattn),dot(gup,mlp_in,TN),dot(hid,cot,TN)]
 
         K4=4*Ch
@@ -607,49 +826,15 @@
             for i,t in enumerate(g3):
                 mine[i]=mine[i]+gsend(t[g*K4:(g+1)*K4].astype(bf16),g).astype(f32)
         fb=[jnp.concatenate([t[m*Ch:(m+1)*Ch] for t in mine],0) for m in range(4)]
-        gT=[None]*4; dW=[None]*4; sc=0.0
-        def bwd(m,*deps):
-            qt,kt,kn,vn,ot,lse=saved[m]
-            qt=after(qt,*deps)
-            gT[m],s_=attn_bwd(first,last,qt,kt,kn,vn,ot,doT[m*W:(m+1)*W],lse,pd,segk,segq)
-            return s_[:,0]
-        sc=sc+bwd(3)
-        dW[3]=dot(gT[3],ain).astype(bf16)
-        fr=[chip(fb[m].astype(bf16),m) for m in (1,2)]
-        f3=reduceZ(split(zi,Z,fb[3],[]))
-        sc=sc+bwd(1,gT[3],fb[0])
-        dW[1]=dot(gT[1],ain).astype(bf16)
-        q1=chip(dW[1],1)
-        f0=reduceZ(split(zi,Z,fb[0],fr))
-        f3=chip(f3.astype(bf16),3)
-        sc=sc+bwd(2,gT[1],fr[0],fr[1])
-        dW[2]=dot(gT[2],ain).astype(bf16)
-        q2=chip(dW[2],2)
-        q3=reduceZ(split(zi,Z,after(dW[3],f0),[]))
-        sc=sc+bwd(0,gT[2],f0,q1)
-        q3=chip(after(q3,gT[0]).astype(bf16),3)
-        g_out,g_up,g_down=finish(f0+f3.astype(f32),3)
-        grad_out=g_out.T; grad_up=g_up; grad_down=g_down.T
-        gTall=jnp.concatenate(gT,0); wtall=jnp.concatenate(wts,0)
-        grel=unxor(tok_lanes(gTall),g0)
-        gain=0.0
-        for g in range(1,G):
-            gain=gain+gsend(dot(grel[g],wtall,TN).astype(bf16),g).astype(f32)
-        gain=gain+dot(grel[0],wtall,TN)
-        norm1=x*inv1
-        dn1=gain*attn_gain
-        gin=gmid+inv1*(dn1-norm1*jnp.mean(dn1*norm1,axis=-1,keepdims=True))
-        attn_gain_part=jnp.sum(gain*norm1,axis=0)
-        ginb=gin.astype(bf16)
-        input_grad=collect(ginb).astype(f32)
-        dW[0]=dot(after(gT[0],ginb),ain)
-        q0s=reduceZ(split(zi,Z,dW[0],[q1,q2]))
-        grad_query,grad_key,grad_value=finish(q0s+q3.astype(f32),3)
-
-        scale_part=jnp.sum(sc.reshape(hb,HD),axis=0)*(scale_base/math.sqrt(HD))*jax.nn.sigmoid(query_scale)
-        grad_mlp_gain=allsum(mlp_gain_part)
-        late=allsum(jnp.concatenate([attn_gain_part,scale_part]))
-        return (block_out,input_grad,late[:D],grad_query,grad_key,grad_value,grad_out,late[D:],grad_mlp_gain,grad_up,grad_down)
+        fbb=jnp.stack(fb,0).astype(bf16)
+        gi,gwm,gwq,vo=backward(Z,C,qkv,ot,do,lse,pd,segk,segq,ain,wts,xo,gmid.reshape(4*C,n,D),attn_gain,mlp_gain_part,fbb,R,Pn,Dd)
+        input_grad=gi.astype(f32)
+        def cols(gw,i):
+            return jnp.concatenate([gw[0,:,i*Ch:(i+1)*Ch],gw[1,:,i*Ch:(i+1)*Ch]],1)
+        grad_query,grad_key,grad_value=[cols(gwq,i) for i in range(3)]
+        grad_out=cols(gwm,0).T; grad_up=cols(gwm,1); grad_down=cols(gwm,2).T
+        grad_query_scale=vo[2,:HD]*(scale_base/math.sqrt(HD))*jax.nn.sigmoid(query_scale)
+        return (block_out,input_grad,vo[0],grad_query,grad_key,grad_value,grad_out,grad_query_scale,vo[1],grad_up,grad_down)
     return local
 
 def solution(mesh):

time: 611 us -> 432 us (0.71)
  matrix products: 109 us -> 38.2 us
  waiting for transfers between devices: 76.6 us -> 7.71 us
  Pallas kernels: 260 us -> 317 us
  starting transfers between devices: 58.3 us -> 12 us
  local copies, waits for them, and re-layouts: 60.8 us -> 25.9 us
  other arithmetic: 41.1 us -> 26.1 us
    dot_general x15 -> x9, matrix products: 109 us -> 38.2 us  [dot(): return lax.dot_general(a, b, dims, preferred_element_type=f32)]
    ppermute x44 -> x9, waiting for transfers between devices: 76.6 us -> 7.71 us  [pp(): return lax.ppermute(x, AXES, [(lin[c], lin[fn(*c)]) for c in coords])]
    pallas_call x8 -> x1, Pallas kernels: 116 us -> 174 us  [backward(): pl.pallas_call(functools.partial(bwd_kernel, Z, C, n), out_shape=(jax.Sha...]
    ppermute x44 -> x9, starting transfers between devices: 58.3 us -> 12 us  [pp(): return lax.ppermute(x, AXES, [(lin[c], lin[fn(*c)]) for c in coords])]
    unnamed x116 -> x43, local copies, waits for them, and re-layouts: 18.9 us -> 0.83 us
    slice x12 -> x3, local copies, waits for them, and re-layouts: 11.4 us -> 1.66 us  [the longest x1 1.48 us: local(): vo[1]]
    slice x3, local copies, waits for them, and re-layouts: 9.78 us -> 1.75 us  [local(): t[g * K4:(g + 1) * K4].astype(bf16)]
  transfers between devices with their start and end apart: 44 -> 9, of which waited for: 12 -> 2; matrix products, arithmetic and copies ran while one was open for 18% -> 7% of each run, Pallas kernels for 15% -> 0%
where the time goes in v1:
time: 432 us; the launch traced here: 428 us
  Pallas kernels  317 us (73%)
  matrix products  38.2 us (9%)
  other arithmetic  26.1 us (6%)
  local copies, waits for them, and re-layouts  25.9 us (6%)
  starting transfers between devices  12 us (3%)
  waiting for transfers between devices  7.71 us (2%)
    pallas_call x1, Pallas kernels, backward(): pl.pallas_call(functools.partial(bwd_kernel, Z, C, n), out_shape=(jax.Sha...  174 us
    pallas_call x1, Pallas kernels, forward(): pl.pallas_call(functools.partial(fwd_kernel, Z, C, n), out_shape=(B(NB, n...  143 us
    dot_general x9, matrix products, dot(): return lax.dot_general(a, b, dims, preferred_element_type=f32)  38.2 us
    ppermute x9, starting transfers between devices, pp(): return lax.ppermute(x, AXES, [(lin[c], lin[fn(*c)]) for c in coords])  12 us
  transfers between devices with their start and end apart: 9, of which 2 were waited for; matrix products, arithmetic and copies ran while one was open for 7% of the time, Pallas kernels for 0%

profile of v1, /device:TPU:6, one launch (start us, length us, event | category | flops | bytes accessed | tf_op | source)
XLA Modules:
  0.0 428.0 jit_solution(14531777721775341452)
XLA Ops:
  12.5 142.6 %forward.1 = (bf16[4,256,1280]{2,1,0:T(8,128)(2,1)}, bf16[8,256,1280]{2,1,0:T(8,128)(2,1)}, bf16[4,480,1280]{2,1,0:T(8,128)(2,1)}, bf16[2,4,480,1280]{3,2,1,0:T(...) custom-call(bf16[2,512,1280]{2,1,0:T(8,128)(2,1)} %x_ref.1, ...), custom_call_target="tpu_custom_call" | custom-call | flops 30000001024 | bytes 100000000 | tf_op jit(solution)/shard_map/forward/pallas_call | solution.py:429
  155.1 1.9 fusion.13
  157.0 5.6 %fusion.12 = (bf16[2,4,160,1280]{3,2,1,0:T(8,128)(2,1)S(1)}, bf16[2,4,160,1280]{3,2,1,0:T(8,128)(2,1)S(1)}, bf16[2,4,160,1280]{3,2,1,0:T(8,128)(2,1)S(1)}) fusion(bf16[2,4,480,1280]{3,2,1,0:T(8,128)(2,1)} %get-tuple-element.26), kind=kLoop, calls=%fused_computation.96 | loop fusion | bytes 19660800 | tf_op jit(solution)/shard_map/slice | solution.py:798
  162.7 4.1 multiply_reduce_fusion.2
  166.8 3.6 fusion.10
  170.5 4.5 %add_convert_fusion = bf16[1024,1280]{1,0:T(8,128)(2,1)S(1)} fusion(f32[1024,1280]{1,0:T(8,128)S(1)} %get-tuple-element.103, bf16[1280,1280]{1,0:T(8,128)(2,1)S(1)} %bitcast.89, f32[1024,1280]{1,0:T(8,128)S(1)} %fusion.10), kind=kOutput, calls=%fused_computation.5 | convolution fusion | flops 3364618240 | bytes 16384000 | tf_op jit(solution)/shard_map/dot_general | solution.py:19
  175.0 4.6 %multiply_convert_fusion = bf16[1024,1280]{1,0:T(8,128)(2,1)S(1)} fusion(f32[1024,1280]{1,0:T(8,128)S(1)} %fusion.10, bf16[1024,1280]{1,0:T(8,128)(2,1)S(1)} %bitcast.91, bf16[1280,1280]{1,0:T(8,128)(2,1)S(1)} %bitcast.90), kind=kOutput, calls=%fused_computation.4 | convolution fusion | flops 3367239680 | bytes 13762560 | tf_op jit(solution)/shard_map/dot_general | solution.py:19
  179.6 5.9 %fusion.11 = f32[1280,1280]{1,0:T(8,128)S(1)} fusion(bf16[1024,1280]{1,0:T(8,128)(2,1)S(1)} %bitcast.92, f32[1024,1280]{1,0:T(8,128)} %copy-done.17), kind=kOutput, calls=%fused_computation.95 | convolution fusion | flops 3361996800 | bytes 14417920 | tf_op jit(solution)/shard_map/dot_general | solution.py:19
  185.5 4.0 multiply_reduce_fusion
  189.5 3.9 fusion.9
  193.5 1.9 broadcast_select_fusion.15
  195.4 4.2 collective-permute-start.2
  199.6 3.5 collective-permute-start.4
  205.1 3.6 collective-permute-start.8
  209.2 1.9 multiply_add_fusion
  211.1 3.9 convolution_convert_fusion
  217.0 3.6 fusion.3
  220.9 6.6 %collective-permute-done.2 = bf16[256,1280]{1,0:T(8,128)(2,1)} collective-permute-done((bf16[256,1280]{1,0:T(8,128)(2,1)}, bf16[256,1280]{1,0:T(8,128)(2,1)}, u32[]{:S(2)}, u32[]{:S(2)}) %collective-permute-start.2) | collective-permute-done | bytes 655392 | tf_op jit(solution)/shard_map/ppermute | solution.py:711
  228.6 1.9 broadcast_select_fusion.13
  230.7 1.7 pad_maximum_fusion.2
  233.0 2.8 fusion
  237.5 2.8 pad_maximum_fusion.fb_ref
  240.2 173.9 %backward.1 = (bf16[2,512,1280]{2,1,0:T(8,128)(2,1)}, f32[2,160,480]{2,1,0:T(8,128)}, f32[2,160,480]{2,1,0:T(8,128)}, f32[8,1280]{1,0:T(8,128)}) custom-call(bf16[4,480,2048]{2,1,0:T(8,128)(2,1)} %get-tuple-element.27.qkv_ref, bf16[8,4,160,256]{3,2,1,0:T(8,128)(2,1)} %get-tuple-element.28.ot_ref, bf16[8,4,160,256]{3,2,1,0:T(8,128)(2,1)} %copy-done.10, ...), custom_call_target="tpu_custom_call" | custom-call | flops 60000002048 | bytes 100000000 | tf_op jit(solution)/shard_map/backward/pallas_call | solution.py:687
  420.2 2.8 convert_element_type.55
  (107 shorter events, 30.6 us)
Async XLA Ops:
  0.6 9.8 %copy-start.12 = (s32[2,2048]{1,0:T(2,128)S(1)}, s32[2,2048]{1,0:T(2,128)}, u32[]{:S(2)}) copy-start(s32[2,2048]{1,0:T(2,128)} %param.13) | copy-start | bytes 49156
  0.7 9.1 %copy-start.14 = (f32[1280]{0:T(1024)S(1)}, f32[1280]{0:T(1024)}, u32[]{:S(2)}) copy-start(f32[1280]{0:T(1024)} %param.14) | copy-start | bytes 15364
  0.7 9.7 %collective-permute-start = (s32[2,2048]{1,0:T(2,128)}, s32[2,2048]{1,0:T(2,128)S(1)}, u32[]{:S(2)}, u32[]{:S(2)}) collective-permute-start(s32[2,2048]{1,0:T(2,128)} %param.13), channel_id=1, source_target_pairs={{0,4},{1,5},{2,6},{3,7},{4,0},{5,1},{6,2},{7,3},{8,12},{9,13},{10,... | collective-permute-start | bytes 49160 | tf_op jit(solution)/shard_map/ppermute | solution.py:711
  10.4 2.0 copy-start.11
  157.0 5.7 %copy-start.4 = (bf16[1,2,4,160,256]{4,3,2,1,0:T(8,128)(2,1)}, bf16[1,2,4,160,256]{4,3,2,1,0:T(8,128)(2,1)S(1)}, u32[]{:S(2)}) copy-start(bf16[1,2,4,160,256]{4,3,2,1,0:T(8,128)(2,1)S(1)} %get-tuple-element.55) | copy-start | bytes 1966084
  157.0 5.7 %copy-start.6 = (bf16[1,2,4,160,256]{4,3,2,1,0:T(8,128)(2,1)}, bf16[1,2,4,160,256]{4,3,2,1,0:T(8,128)(2,1)S(1)}, u32[]{:S(2)}) copy-start(bf16[1,2,4,160,256]{4,3,2,1,0:T(8,128)(2,1)S(1)} %get-tuple-element.56) | copy-start | bytes 1966084
  157.0 5.7 %copy-start.8 = (bf16[1,2,4,160,256]{4,3,2,1,0:T(8,128)(2,1)}, bf16[1,2,4,160,256]{4,3,2,1,0:T(8,128)(2,1)S(1)}, u32[]{:S(2)}) copy-start(bf16[1,2,4,160,256]{4,3,2,1,0:T(8,128)(2,1)S(1)} %get-tuple-element.57) | copy-start | bytes 1966084
  157.0 5.7 %copy-start.16 = (bf16[4,256,1280]{2,1,0:T(8,128)(2,1)S(1)}, bf16[4,256,1280]{2,1,0:T(8,128)(2,1)}, u32[]{:S(2)}) copy-start(bf16[4,256,1280]{2,1,0:T(8,128)(2,1)} %get-tuple-element.24.xo_ref) | copy-start | bytes 7864324
  162.7 4.1 copy-start.13
  170.5 4.5 %copy-start.17 = (f32[1024,1280]{1,0:T(8,128)}, f32[1024,1280]{1,0:T(8,128)S(1)}, u32[]{:S(2)}) copy-start(f32[1024,1280]{1,0:T(8,128)S(1)} %fusion.10) | copy-start | bytes 15728644
  170.5 4.5 %copy-start.2 = (bf16[4,256,1280]{2,1,0:T(8,128)(2,1)S(1)}, bf16[4,256,1280]{2,1,0:T(8,128)(2,1)}, u32[]{:S(2)}) copy-start(bf16[4,256,1280]{2,1,0:T(8,128)(2,1)} %get-tuple-element.29) | copy-start | bytes 7864324
  195.3 13.9 %copy-start.3 = (bf16[4,256,1280]{2,1,0:T(8,128)(2,1)S(1)}, bf16[4,256,1280]{2,1,0:T(8,128)(2,1)}, u32[]{:S(2)}) copy-start(bf16[4,256,1280]{2,1,0:T(8,128)(2,1)} %get-tuple-element.29) | copy-start | bytes 7864324
  195.3 25.5 %collective-permute-start.3 = (bf16[256,1280]{1,0:T(8,128)(2,1)}, bf16[256,1280]{1,0:T(8,128)(2,1)}, u32[]{:S(2)}, u32[]{:S(2)}) collective-permute-start(bf16[256,1280]{1,0:T(8,128)(2,1)} %get-tuple-element.50), channel_id=1, source_target_pairs={{0,1},{1,0},{2,7},{3,6},{4,3},{5,2},{6,5},{7,4},{8,9},{9,8},{10,15... | collective-permute-start | bytes 1966088 | tf_op jit(solution)/shard_map/ppermute | solution.py:711
  195.4 32.2 %collective-permute-start.2 = (bf16[256,1280]{1,0:T(8,128)(2,1)}, bf16[256,1280]{1,0:T(8,128)(2,1)}, u32[]{:S(2)}, u32[]{:S(2)}) collective-permute-start(bf16[256,1280]{1,0:T(8,128)(2,1)} %get-tuple-element.51), channel_id=1, source_target_pairs={{0,2},{1,3},{2,4},{3,5},{4,0},{5,1},{6,6},{7,7},{8,10},{9,11},{10,... | collective-permute-start | bytes 1966088 | tf_op jit(solution)/shard_map/ppermute | solution.py:711
  199.6 29.0 %collective-permute-start.4 = (bf16[256,1280]{1,0:T(8,128)(2,1)}, bf16[256,1280]{1,0:T(8,128)(2,1)}, u32[]{:S(2)}, u32[]{:S(2)}) collective-permute-start(bf16[256,1280]{1,0:T(8,128)(2,1)} %get-tuple-element.52), channel_id=1, source_target_pairs={{0,0},{1,1},{2,6},{3,7},{4,2},{5,3},{6,4},{7,5},{8,8},{9,9},{10,14... | collective-permute-start | bytes 1966088 | tf_op jit(solution)/shard_map/ppermute | solution.py:711
  203.1 25.5 %collective-permute-start.1 = (bf16[256,1280]{1,0:T(8,128)(2,1)}, bf16[256,1280]{1,0:T(8,128)(2,1)}, u32[]{:S(2)}, u32[]{:S(2)}) collective-permute-start(bf16[256,1280]{1,0:T(8,128)(2,1)} %get-tuple-element.53), channel_id=1, source_target_pairs={{0,3},{1,2},{2,5},{3,4},{4,1},{5,0},{6,7},{7,6},{8,11},{9,10},{10,... | collective-permute-start | bytes 1966088 | tf_op jit(solution)/shard_map/ppermute | solution.py:711
  205.1 28.0 %collective-permute-start.8 = (bf16[640,1280]{1,0:T(8,128)(2,1)}, bf16[640,1280]{1,0:T(8,128)(2,1)}, u32[]{:S(2)}, u32[]{:S(2)}) collective-permute-start(bf16[640,1280]{1,0:T(8,128)(2,1)} %slice.396), channel_id=1, source_target_pairs={{0,4},{1,5},{2,6},{3,7},{4,0},{5,1},{6,2},{7,3},{8,12},{9,13},{10,... | collective-permute-start | bytes 4915208 | tf_op jit(solution)/shard_map/ppermute | solution.py:711
  211.1 5.3 %copy-start = (f32[1024,1280]{1,0:T(8,128)}, f32[1024,1280]{1,0:T(8,128)S(1)}, u32[]{:S(2)}) copy-start(f32[1024,1280]{1,0:T(8,128)S(1)} %multiply_add_fusion) | copy-start | bytes 15728644
  220.8 11.6 %collective-permute-start.5 = (bf16[640,1024]{1,0:T(8,128)(2,1)}, bf16[640,1024]{1,0:T(8,128)(2,1)S(1)}, u32[]{:S(2)}, u32[]{:S(2)}) collective-permute-start(bf16[640,1024]{1,0:T(8,128)(2,1)} %slice.297), channel_id=1, source_target_pairs={{0,4},{1,5},{2,6},{3,7},{4,0},{5,1},{6,2},{7,3},{8,12},{9,13},{10,... | collective-permute-start | bytes 3932168 | tf_op jit(solution)/shard_map/ppermute | solution.py:711
  227.5 8.5 %collective-permute-start.7 = (bf16[640,1280]{1,0:T(8,128)(2,1)S(1)}, bf16[640,1280]{1,0:T(8,128)(2,1)S(1)}, u32[]{:S(2)}, u32[]{:S(2)}) collective-permute-start(bf16[640,1280]{1,0:T(8,128)(2,1)S(1)} %slice.397), channel_id=1, source_target_pairs={{0,4},{1,5},{2,6},{3,7},{4,0},{5,1},{6,2},{7,3},{8,12},{9,13},{10,... | collective-permute-start | bytes 4915208 | tf_op jit(solution)/shard_map/ppermute | solution.py:711
  228.6 8.0 %collective-permute-start.6 = (bf16[640,1280]{1,0:T(8,128)(2,1)S(1)}, bf16[640,1280]{1,0:T(8,128)(2,1)S(1)}, u32[]{:S(2)}, u32[]{:S(2)}) collective-permute-start(bf16[640,1280]{1,0:T(8,128)(2,1)S(1)} %slice.398), channel_id=1, source_target_pairs={{0,4},{1,5},{2,6},{3,7},{4,0},{5,1},{6,2},{7,3},{8,12},{9,13},{10,... | collective-permute-start | bytes 4915208 | tf_op jit(solution)/shard_map/ppermute | solution.py:711
  233.0 2.8 copy-start.10
  240.2 173.9 %copy-start.15 = (f32[80]{0:T(128)S(1)}, f32[80]{0:T(128)}, u32[]{:S(2)}) copy-start(f32[80]{0:T(128)} %param.19) | copy-start | bytes 964
  414.2 6.0 %copy-start.1 = (bf16[2,512,1280]{2,1,0:T(8,128)(2,1)S(1)}, bf16[2,512,1280]{2,1,0:T(8,128)(2,1)}, u32[]{:S(2)}) copy-start(bf16[2,512,1280]{2,1,0:T(8,128)(2,1)} %get-tuple-element.33) | copy-start | bytes 7864324
  (3 other events, 5.1 us)

commit v2 on v1

v2 whole, which is shorter than its diff:
```python
import functools
import itertools
import math
import jax, jax.numpy as jnp
from jax import lax
from jax.experimental import pallas as pl
from jax.experimental.pallas import tpu as pltpu
from jax.sharding import Mesh, PartitionSpec as P

AXES=("zz","core","q","s")
norm_eps = 1e-06
HD=80
BQ=256
NEG=-1e30
f32=jnp.float32; bf16=jnp.bfloat16
NT=(((1,),(1,)),((),()))
NN=(((1,),(0,)),((),()))
TN=(((0,),(0,)),((),()))
def dot(a,b,dims=NN): return lax.dot_general(a,b,dims,preferred_element_type=f32)

def merge(*gens):
    gens=list(gens)
    while gens:
        for g in list(gens):
            try: next(g)
            except StopIteration: gens.remove(g)


MESH=pl.DeviceIdType.MESH
scale_base = 1.442695041

def rcopy(src,dst,ss,rs,dev):
    return pltpu.make_async_remote_copy(src_ref=src,dst_ref=dst,send_sem=ss,recv_sem=rs,device_id=dev,device_id_type=MESH)

def transpose_rows(src, dst):
    P_,rows,cols=src.shape
    per=max(1,640//rows)
    for i in range(P_//per):
        dst[:,i*per*rows:(i+1)*per*rows]=src[i*per:(i+1)*per].reshape(per*rows,cols).T

def partner(q, m):
    return (q,q+1-2*lax.rem(q,2),lax.rem(q+2,4),3-q)[m]

def greet(Z, C):
    z,k,q,s=[lax.axis_index(a) for a in AXES]
    bar=pltpu.get_barrier_semaphore()
    plane=list(itertools.product(range(2),range(4),range(C)))[1:]
    column=[(j,a) for j in range(1,Z) for a in range(2)]
    for a,b,c in plane:
        pl.semaphore_signal(bar,inc=1,device_id=(z,lax.rem(k+a,2),lax.rem(q+b,4),lax.rem(s+c,C)),device_id_type=MESH)
    for j,a in column:
        pl.semaphore_signal(bar,inc=1,device_id=(lax.rem(z+j,Z),lax.rem(k+a,2),q,s),device_id_type=MESH)
    pl.semaphore_wait(bar,len(plane)+len(column))

def col_copies(Z, src, dst, ss, rs):
    z,k,q,s=[lax.axis_index(a) for a in AXES]
    out=[]
    for j in range(Z):
        for a in range(2):
            kk=lax.rem(k+a,2)
            if j==0 and a==0: out.append(pltpu.make_async_copy(src.at[k],dst.at[2*z+k],rs.at[2*z+k]))
            else: out.append(rcopy(src.at[kk],dst.at[2*z+k],ss.at[j*2+a],rs.at[2*z+k],(lax.rem(z+j,Z),kk,q,s)))
    return out

def spread_copies(C, n, src, dst, ss, rs):
    z,k,q,s=[lax.axis_index(a) for a in AXES]
    out=[]
    for rr in range(2):
        r=lax.rem(q+rr,2)
        for h in range(2):
            for s2 in range(C):
                i=(rr*2+h)*C+s2
                piece=src.at[r,pl.ds((h*C+s2)*n,n),:]
                out.append((rr,(k==h)&(q==2*k+r)&(s==s2),pltpu.make_async_copy(piece,dst.at[q*C+s],rs.at[q*C+s]),
                            rcopy(piece,dst.at[q*C+s],ss.at[i],rs.at[q*C+s],(z,h,2*k+r,s2))))
    return out

def is_home(): return lax.axis_index("core")==lax.div(lax.axis_index("q"),2)

def spread_near(cps, do):
    for rr,mine,loc,cp in cps:
        if rr==0:
            @pl.when(mine)
            def _(loc=loc):
                if do=="start": loc.start()
            @pl.when(jnp.logical_not(mine))
            def _(cp=cp): cp.start() if do=="start" else cp.wait_send()
        else:
            @pl.when(is_home())
            def _(cp=cp): cp.start() if do=="start" else cp.wait_send()

def spread_far(cps, do):
    for rr,mine,loc,cp in cps:
        if rr==1:
            @pl.when(jnp.logical_not(is_home()))
            def _(cp=cp): cp.start() if do=="start" else cp.wait_send()

def near_blocks(C):
    q=lax.axis_index("q")
    return [partner(q,m)*C+t for m in range(3) for t in range(C)]

def far_blocks(C):
    q=lax.axis_index("q")
    return [partner(q,3)*C+t for t in range(C)]

def spread_start(cps):
    for mine,loc,cp in cps:
        @pl.when(mine)
        def _(loc=loc): loc.start()
        @pl.when(jnp.logical_not(mine))
        def _(cp=cp): cp.start()

def spread_sent(cps):
    for mine,loc,cp in cps:
        @pl.when(jnp.logical_not(mine))
        def _(cp=cp): cp.wait_send()

def home_copies(C, n, src, dst, ss, rs):
    z,k,q,s=[lax.axis_index(a) for a in AXES]
    out=[]
    for b in range(4*C):
        to=dst.at[lax.rem(q,2),pl.ds(pl.multiple_of((k*C+s)*n,n),n),:]
        sem=rs.at[(lax.rem(q,2)*2+k)*C+s]
        out.append(((lax.div(q,2)==k)&(q==b//C)&(s==b%C),pltpu.make_async_copy(src.at[b],to,sem),
                    rcopy(src.at[b],to,ss.at[b],sem,(z,lax.div(q,2),b//C,b%C))))
    return out

def home_arrived(C, n, dst, rs):
    for r in range(2):
        for h in range(2):
            for s2 in range(C):
                arrived(dst.at[r,pl.ds((h*C+s2)*n,n),:],rs.at[(r*2+h)*C+s2])

def arrived(ref, sem):
    z,k,q,s=[lax.axis_index(a) for a in AXES]
    rcopy(ref,ref,sem,sem,(z,1-k,q,s)).wait_recv()

def fwd_kernel(Z, C, n, x_ref, w1_ref, w2_ref, cot_ref, gain_ref, pd_ref, seg_ref,
               xo_ref, ain_ref, wts_ref, w2o_ref, mix_ref, qkv_ref, ot_ref, lse_ref, segk_ref, segq_ref, coto_ref,
               xo_scr, ain_scr, wts_scr, qkv_scr, ot_scr, wa_scr, wb_scr, wd_scr, o3_scr, w2_scr, k_scr, s_scr, so_scr,
               tok_s, tok_r, ain_s, ain_r, a_s, a_r, b_s, b_r, dd_s, dd_r, o3_s, o3_r,
               wt_s, wt_r, hf_s, hf_r, w2_s, w2_r, gr_s, gr_r, loc_s, mix_s, mix_r, mixl, sg_s, sg_r, out_s, qo_s, cot_s, cot_r):
    z,k,q,s=[lax.axis_index(a) for a in AXES]
    G=2*C; g0=k*C+s; NB=4*C
    D=gain_ref.shape[1]; L=seg_ref.shape[1]; W=pd_ref.shape[0]; hb=W//HD; nb=L//BQ; nC=3*W
    peers=list(itertools.product(range(2),range(C)))[1:]
    pdev=[(z,lax.rem(k+gc,2),q,lax.rem(s+gs,C)) for gc,gs in peers]
    pidx=[lax.rem(k+gc,2)*C+lax.rem(s+gs,C) for gc,gs in peers]
    back=[gc*C+(C-gs)%C for gc,gs in peers]
    fore=[gc*C+gs for gc,gs in peers]
    chipdev=[(z,k,partner(q,m),s) for m in range(4)]
    toks=spread_copies(C,n,x_ref,xo_scr,tok_s,tok_r)
    cots=spread_copies(C,n,cot_ref,coto_ref,cot_s,cot_r)
    ca=col_copies(Z,w1_ref,wa_scr,a_s,a_r)
    cb=col_copies(Z,w2_ref,wb_scr,b_s,b_r)
    cd=col_copies(Z,o3_scr,wd_scr,dd_s,dd_r)
    o3=rcopy(w2_ref,o3_scr,o3_s,o3_r,chipdev[3])
    wcp=[rcopy(wts_scr.at[0],wts_scr.at[m],wt_s.at[m],wt_r.at[m],chipdev[m]) for m in (1,2)]
    h1=nC//32*16; half=[pl.ds(0,h1),pl.ds(h1,nC-h1)]
    hcp=[rcopy(wts_scr.at[1,half[0]],wts_scr.at[3,half[0]],hf_s.at[0],hf_r.at[0],chipdev[2]),
         rcopy(wts_scr.at[2,half[1]],wts_scr.at[3,half[1]],hf_s.at[1],hf_r.at[1],chipdev[1])]
    save=[pltpu.make_async_copy(xo_scr,xo_ref,out_s.at[0]),pltpu.make_async_copy(ain_scr,ain_ref,out_s.at[1])]
    wsave=[pltpu.make_async_copy(wts_scr.at[m],wts_ref.at[m],out_s.at[2+m]) for m in range(4)]
    def qsave(m): return [pltpu.make_async_copy(qkv_scr.at[m],qkv_ref.at[m],qo_s.at[0,m]),pltpu.make_async_copy(ot_scr.at[:,m],ot_ref.at[:,m],qo_s.at[1,m])]
    w2cp=[rcopy(w2_scr.at[0],w2_scr.at[m],w2_s.at[m],w2_r.at[m],chipdev[m]) for m in (1,2)]
    grp=[[rcopy(w2_scr.at[m],w2o_ref.at[back[i],m],gr_s.at[i,m],gr_r.at[back[i],m],pdev[i]) for i in range(G-1)] for m in range(4)]
    loc=[pltpu.make_async_copy(w2_scr.at[m],w2o_ref.at[0,m],loc_s.at[m]) for m in range(4)]
    def share(m):
        loc[m].start()
        for cp in grp[m]: cp.start()
    sgc=rcopy(seg_ref,so_scr,sg_s,sg_r,(z,1-k,q,s))
    greet(Z,C)
    sgc.start()
    for cp in ca: cp.start()
    spread_near(toks,"start"); spread_far(toks,"start")
    o3.start()
    sgc.wait_recv()
    sg=jnp.where(k==lax.div(q,2),seg_ref[...],so_scr[...])
    sg=jnp.where(lax.rem(q,2)==0,sg[0:1],sg[1:2]).astype(f32)
    segq_ref[...]=sg
    for c in range(L//BQ):
        segk_ref[c*BQ:(c+1)*BQ,:]=jnp.broadcast_to(sg[:,c*BQ:(c+1)*BQ],(128,BQ)).T
    for i in range(2*Z): arrived(wa_scr.at[i],a_r.at[i])
    for cp in cb: cp.start()
    transpose_rows(wa_scr,wts_scr.at[0])
    for cp in wcp: cp.start()
    wsave[0].start()
    ains=[]
    for j in range(NB):
        arrived(xo_scr.at[j],tok_r.at[j])
        x=xo_scr[j].astype(f32)
        inv=lax.rsqrt(jnp.mean(x*x,axis=-1,keepdims=True)+norm_eps)
        slot=j*G+g0
        ain_scr[slot]=(x*inv*gain_ref[...]).astype(bf16)
        for i in range(G-1):
            cp=rcopy(ain_scr.at[slot],ain_scr.at[slot],ain_s.at[i,j],ain_r.at[slot],pdev[i])
            cp.start(); ains.append(cp)
    for j in range(NB):
        for i in range(G-1): arrived(ain_scr.at[j*G+pidx[i]],ain_r.at[j*G+pidx[i]])
    for cp in save: cp.start()
    rowi=lax.broadcasted_iota(jnp.int32,(BQ,BQ),0)
    coli=lax.broadcasted_iota(jnp.int32,(BQ,BQ),1)
    hs=[slice(h*HD,(h+1)*HD) for h in range(hb)]
    CH=512; per=CH//n; sub=BQ//n

    def block(m,_):
        @pl.when(m==1)
        def _():
            for i in range(2*Z): arrived(wb_scr.at[i],b_r.at[i])
            arrived(o3_scr,o3_r)
            for cp in cd: cp.start()
            transpose_rows(wb_scr,w2_scr.at[0])
            for i in (1,2): arrived(wts_scr.at[i],wt_r.at[i])
            for cp in hcp+wsave[1:3]: cp.start()
            share(0)
        @pl.when(m==2)
        def _():
            for cp in w2cp: cp.start()
        @pl.when(m==3)
        def _():
            for i in range(2): arrived(wts_scr.at[3,half[i]],hf_r.at[i])
            wsave[3].start()
            spread_near(cots,"start")
        for c in range(L//CH):
            cs=slice(c*CH,(c+1)*CH)
            r=dot(wts_scr[m],ain_scr[c*per:(c+1)*per].reshape(CH,D),NT)
            qkv_scr[m,:W,cs]=(r[:W]*pd_ref[:,:1]).astype(bf16)
            qkv_scr[m,W:,cs]=r[W:].astype(bf16)
            for h in range(hb):
                k_scr[h,cs,:]=r[W+h*HD:W+(h+1)*HD].T.astype(bf16)
        units=[(i,h) for i in range(nb) for h in range(hb)]
        st={}
        def phase_a(u):
            i,h=units[u]; c0=i*BQ
            qi=qkv_scr[m,hs[h],c0:c0+BQ]
            sq=segq_ref[:,c0:c0+BQ]
            m8=None
            for j in range(i+1):
                t=dot(k_scr[h,j*BQ:(j+1)*BQ,:],qi)
                sk=segk_ref[j*BQ:(j+1)*BQ,:]
                ok=jnp.concatenate([sk]*(BQ//128),axis=1)==sq
                if j==i: ok=ok&(rowi<=coli)
                t=jnp.where(ok,t,NEG)
                s_scr[u%2,j*BQ:(j+1)*BQ,:]=t
                mm=t.reshape(BQ//8,8,BQ).max(0)
                m8=mm if m8 is None else jnp.maximum(m8,mm)
                yield
            st[u]=m8.max(0,keepdims=True)
        def phase_b(u):
            i,h=units[u]; c0=i*BQ
            mx=st[u]; l8=None; acc=None
            for j in range(i+1):
                p=jnp.exp(s_scr[u%2,j*BQ:(j+1)*BQ,:]-mx)
                ll=p.reshape(BQ//8,8,BQ).sum(0)
                l8=ll if l8 is None else l8+ll
                pv=dot(qkv_scr[m,2*W+h*HD:2*W+(h+1)*HD,j*BQ:(j+1)*BQ],p.astype(bf16))
                acc=pv if acc is None else acc+pv
                yield
            l=l8.sum(0,keepdims=True)
            o=(acc*(1.0/l)).astype(bf16)
            for t in range(sub): ot_scr[i*sub+t,m,hs[h],:]=o[:,t*n:(t+1)*n]
            lse_ref[m*hb+h,:,c0:c0+BQ]=mx+jnp.log(l)
        merge(phase_a(0))
        for u in range(len(units)):
            gs=[phase_b(u)]
            if u+1<len(units): gs=[phase_a(u+1)]+gs
            merge(*gs)
        for b in range(NB):
            pltpu.make_async_copy(ot_scr.at[b*G+g0,m],mix_ref.at[b,0,m],mixl.at[b,m]).start()
            for i in range(G-1):
                rcopy(ot_scr.at[b*G+pidx[i],m],mix_ref.at[b,back[i],m],mix_s.at[i,b,m],mix_r.at[back[i],b,m],pdev[i]).start()
        for cp in qsave(m): cp.start()
        return 0
    lax.fori_loop(0,4,block,0)
    for m in (1,2):
        arrived(w2_scr.at[m],w2_r.at[m])
        share(m)
    for i in range(2*Z): arrived(wd_scr.at[i],dd_r.at[i])
    transpose_rows(wd_scr,w2_scr.at[3])
    share(3)
    for i in range(G-1):
        for b in range(NB):
            for m in range(4):
                arrived(mix_ref.at[b,fore[i],m],mix_r.at[fore[i],b,m])
                rcopy(ot_scr.at[b*G+pidx[i],m],mix_ref.at[b,back[i],m],mix_s.at[i,b,m],mix_r.at[back[i],b,m],pdev[i]).wait_send()
        for m in range(4): arrived(w2o_ref.at[fore[i],m],gr_r.at[fore[i],m])
    for m in range(4):
        loc[m].wait()
        for cp in grp[m]: cp.wait_send()
    for cps in (ca,cb,cd):
        for cp in cps[1:]: cp.wait_send()
    for cp in wcp+hcp+w2cp+ains+[o3,sgc]: cp.wait_send()
    spread_near(toks,"sent"); spread_far(toks,"sent"); spread_near(cots,"sent")
    for b in near_blocks(C): arrived(coto_ref.at[b],cot_r.at[b])
    for cp in save+wsave: cp.wait()
    for m in range(4):
        for cp in qsave(m): cp.wait()
        for b in range(NB): pltpu.make_async_copy(ot_scr.at[b*G+g0,m],mix_ref.at[b,0,m],mixl.at[b,m]).wait()

def forward(Z, C, tokens, w1h, w2h, cot, gain, pd, seg):
    R,Pn,D=tokens.shape; G=2*C; n=Pn//G; _,Dd,nC=w1h.shape; NB=4*C
    L=seg.shape[1]; W=pd.shape[0]; hb=W//HD
    V=pl.BlockSpec(memory_space=pltpu.VMEM); A=pl.BlockSpec(memory_space=pl.ANY)
    S=lambda *sh: pltpu.SemaphoreType.DMA(sh) if sh else pltpu.SemaphoreType.DMA
    B=lambda *sh: jax.ShapeDtypeStruct(sh,bf16)
    F=lambda *sh: jax.ShapeDtypeStruct(sh,f32)
    M=lambda *sh: pltpu.VMEM(sh,bf16)
    col=M(2*Z,Dd,nC)
    return pl.pallas_call(functools.partial(fwd_kernel,Z,C,n),
        out_shape=(B(NB,n,D),B(NB*G,n,D),B(4,nC,D),B(G,4,nC,D),B(NB,G,4,W,n),B(4,nC,L),B(NB*G,4,W,n),F(4*hb,1,L),F(L,128),F(1,L),B(NB,n,D)),
        in_specs=[A,A,A,A,V,V,V],out_specs=(A,A,A,A,A,A,A,V,V,V,A),
        scratch_shapes=[M(NB,n,D),M(NB*G,n,D),M(4,nC,D),M(4,nC,L),M(NB*G,4,W,n),col,col,col,M(2,Dd,nC),M(4,nC,D),M(hb,L,HD),
            pltpu.VMEM((2,L,BQ),f32),pltpu.VMEM((R,L),jnp.int32),
            S(NB),S(NB),S(G-1,NB),S(NB*G),S(2*Z),S(2*Z),S(2*Z),S(2*Z),S(2*Z),S(2*Z),S(),S(),
            S(4),S(4),S(2),S(2),S(4),S(4),S(G-1,4),S(G,4),S(4),S(G-1,NB,4),S(G,NB,4),S(NB,4),S(),S(),S(6),S(2,4),S(NB),S(NB)],
        compiler_params=pltpu.CompilerParams(collective_id=0,has_side_effects=True,vmem_limit_bytes=60*2**20),
        cost_estimate=pl.CostEstimate(flops=3*10**10,bytes_accessed=10**8,transcendentals=0),
        name="forward")(tokens,w1h,w2h,cot,gain.reshape(1,D),pd,seg)

def prep_kernel(Ch, wq_ref, wk_ref, wv_ref, wo_ref, wu_ref, wd_ref, qs_ref, w1_ref, w2_ref, pd_ref):
    for ref,three in ((w1_ref,(wq_ref[...],wk_ref[...],wv_ref[...])),(w2_ref,(wo_ref[...],wu_ref[...],wd_ref[...]))):
        for i,w in enumerate(three):
            for h in range(2): ref[h,:,i*Ch:(i+1)*Ch]=w[:,h*Ch:(h+1)*Ch]
    v=qs_ref[...]
    per_dim=scale_base/math.sqrt(HD)*(jnp.maximum(v,0.0)+jnp.log(1.0+jnp.exp(-jnp.abs(v))))
    col=jnp.broadcast_to(per_dim,(128,HD)).T
    for h in range(pd_ref.shape[0]//HD): pd_ref[h*HD:(h+1)*HD,:]=col

def prep(wq, wk, wv, wo, wu, wd, qs):
    Dd,Ct=wq.shape; Ch=Ct//2
    B=jax.ShapeDtypeStruct((2,Dd,3*Ch),bf16)
    return pl.pallas_call(functools.partial(prep_kernel,Ch),out_shape=(B,B,jax.ShapeDtypeStruct((Ch,128),f32)),
        compiler_params=pltpu.CompilerParams(vmem_limit_bytes=60*2**20),name="prep")(wq,wk,wv,wo.T,wu,wd.T,qs.reshape(1,-1))


def mid_kernel(Z, C, n, mix_ref, w2_ref, xo_ref, cot_ref, coto_ref, gain_ref,
               bo_ref, bh_ref, do_ref, gm_ref, fb_ref, vec_ref,
               wo_scr, wu_scr, wd_scr, mi_scr, hid_scr, gup_scr, ga_scr, gt_scr, gs_scr, gr_scr, co_scr, up_scr, mid_scr,
               wl, dos, dors, dol, gss, grs, cot_s, cot_r, out_s, fo_s, bos, bors):
    z,k,q,s=[lax.axis_index(a) for a in AXES]
    G=2*C; g0=k*C+s; NB=4*C
    D=gain_ref.shape[1]; K4=wo_scr.shape[0]//G; Ch=K4//4; N=NB*n
    peers=list(itertools.product(range(2),range(C)))[1:]
    pdev=[(z,lax.rem(k+gc,2),q,lax.rem(s+gs,C)) for gc,gs in peers]
    pidx=[lax.rem(k+gc,2)*C+lax.rem(s+gs,C) for gc,gs in peers]
    back=[gc*C+(C-gs)%C for gc,gs in peers]
    fore=[gc*C+gs for gc,gs in peers]
    wcp=[]
    for i,dst in enumerate((wo_scr,wu_scr,wd_scr)):
        wcp.append([pltpu.make_async_copy(w2_ref.at[g,m,pl.ds(i*Ch,Ch),:],dst.at[pl.ds((g*4+m)*Ch,Ch),:],wl.at[i,g,m]) for g in range(G) for m in range(4)])
        for cp in wcp[i]: cp.start()
    cots=spread_copies(C,n,cot_ref,co_scr,cot_s,cot_r)
    greet(Z,C)
    spread_far(cots,"start")
    for b in near_blocks(C): pltpu.make_async_copy(coto_ref.at[b],co_scr.at[b],cot_r.at[b]).start()
    order=[partner(q,m)*C+(lax.rem(s+t,C)) for m in range(4) for t in range(C)]
    def rows(b): return pl.ds(pl.multiple_of(b*n,n),n)
    outs=[]
    def put(src,dst,sem):
        cp=pltpu.make_async_copy(src,dst,sem); cp.start(); outs.append(cp)
    vec_ref[...]=jnp.zeros_like(vec_ref)
    for cp in wcp[0]: cp.wait()
    for e,b in enumerate(order):
        attn=dot(mix_ref[b].reshape(G*K4,n),wo_scr[...],TN)
        middle=xo_ref[b].astype(f32)+attn
        mid_scr[b]=middle
        inv=lax.rsqrt(jnp.mean(middle*middle,axis=-1,keepdims=True)+norm_eps)
        mi_scr[rows(b),:]=(middle*inv*gain_ref[...]).astype(bf16)
        if e==0:
            for cp in wcp[1]+wcp[2]: cp.wait()
        up=dot(mi_scr[rows(b),:],wu_scr[...],NT)
        up_scr[b]=up
        hid_scr[rows(b),:]=(up*(1.0/(1.0+jnp.exp(-up)))).astype(bf16)
        gs_scr[rows(b),:]=(middle+dot(hid_scr[rows(b),:],wd_scr[...])).astype(bf16)
        put(gs_scr.at[rows(b)],bo_ref.at[b],out_s.at[0,e])
    exch=[]
    home=[]
    boouts=list(outs); outs=[]
    for e,b in enumerate(order):
        if e<3*C: pltpu.make_async_copy(coto_ref.at[b],co_scr.at[b],cot_r.at[b]).wait()
        else: arrived(co_scr.at[b],cot_r.at[b])
        boouts[e].wait()
        dst=bh_ref.at[lax.rem(q,2),pl.ds(pl.multiple_of((k*C+s)*n,n),n),:]
        rs=bors.at[(lax.rem(q,2)*2+k)*C+s]
        mine=is_home()&(b==q*C+s)
        home.append((mine,pltpu.make_async_copy(bo_ref.at[b],dst,rs),rcopy(bo_ref.at[b],dst,bos.at[e],rs,(z,lax.div(q,2),lax.div(b,C),lax.rem(b,C)))))
        spread_start(home[-1:])
        gh=dot(co_scr[b],wd_scr[...],NT)
        up=up_scr[b]
        sg=1.0/(1.0+jnp.exp(-up))
        gup_scr[rows(b),:]=(gh*(sg*(1.0+up*(1.0-sg)))).astype(bf16)
        gmlp=dot(gup_scr[rows(b),:],wu_scr[...])
        middle=mid_scr[b]
        inv=lax.rsqrt(jnp.mean(middle*middle,axis=-1,keepdims=True)+norm_eps)
        n2=middle*inv
        dn=gmlp*gain_ref[...]
        gm=co_scr[b].astype(f32)+inv*(dn-n2*jnp.mean(dn*n2,axis=-1,keepdims=True))
        vec_ref[...]+=(gmlp*n2).reshape(n//8,8,D).sum(0)
        mid_scr[b]=gm
        put(mid_scr.at[b],gm_ref.at[b],out_s.at[1,e])
        ga_scr[rows(b),:]=gm.astype(bf16)
        gt_scr[b]=dot(wo_scr[...],ga_scr[rows(b),:],NT).astype(bf16).reshape(G,4,Ch,n)
        lc=pltpu.make_async_copy(gt_scr.at[b,0],do_ref.at[b*G+g0],dol.at[e])
        lc.start(); exch.append(lc)
        for i in range(G-1):
            cp=rcopy(gt_scr.at[b,fore[i]],do_ref.at[b*G+g0],dos.at[i,e],dors.at[b*G+g0],pdev[i])
            cp.start(); exch.append(cp)
    def wgrad(i,g):
        cs=slice(g*K4,(g+1)*K4)
        if i==0: return dot(jnp.concatenate([mix_ref[b,g].reshape(K4,n) for b in range(NB)],1),ga_scr[...])
        if i==1: return dot(gup_scr[:,cs],mi_scr[...],TN)
        return dot(hid_scr[:,cs],co_scr[...].reshape(N,D),TN)
    for cp in outs: cp.wait()
    outs=[]
    def part(j,i): return pl.ds((j*3+i)*K4,K4)
    gcp=[[None]*3 for j in range(G-1)]
    for j in range(G-1):
        for i in range(3):
            gs_scr[part(j,i),:]=wgrad(i,fore[j]).astype(bf16)
            gcp[j][i]=rcopy(gs_scr.at[part(j,i)],gr_scr.at[back[j]-1,i],gss.at[j,i],grs.at[back[j]-1,i],pdev[j])
            gcp[j][i].start()
    for i in range(3):
        t=wgrad(i,0)
        for j in range(G-1):
            arrived(gr_scr.at[fore[j]-1,i],grs.at[fore[j]-1,i])
            t=t+gr_scr[fore[j]-1,i].astype(f32)
        gcp[0][i].wait_send()
        gs_scr[part(0,i),:]=t.astype(bf16)
        for m in range(4):
            put(gs_scr.at[pl.ds(i*K4+m*Ch,Ch)],fb_ref.at[m,pl.ds(i*Ch,Ch)],fo_s.at[i,m])
    for b in range(NB):
        for i in range(G-1): arrived(do_ref.at[b*G+pidx[i]],dors.at[b*G+pidx[i]])
    for i,cp in enumerate(exch):
        if i%G==0: cp.wait()
        else: cp.wait_send()
    for cps in gcp[1:]:
        for cp in cps: cp.wait_send()
    spread_far(cots,"sent")
    home_arrived(C,n,bh_ref,bors)
    spread_sent(home)
    for cp in outs: cp.wait()

def middle(Z, C, mix, w2o, xo, cot, coto, gain):
    NB,n,D=xo.shape; G=2*C; nC=w2o.shape[2]; Ch=nC//3; K4=4*Ch; N=NB*n
    V=pl.BlockSpec(memory_space=pltpu.VMEM); A=pl.BlockSpec(memory_space=pl.ANY)
    S=lambda *sh: pltpu.SemaphoreType.DMA(sh)
    M=lambda *sh: pltpu.VMEM(sh,bf16)
    B=lambda *sh: jax.ShapeDtypeStruct(sh,bf16)
    return pl.pallas_call(functools.partial(mid_kernel,Z,C,n),
        out_shape=(B(NB,n,D),B(*cot.shape),B(NB*G,4,Ch,n),jax.ShapeDtypeStruct((NB,n,D),f32),B(4,nC,D),jax.ShapeDtypeStruct((8,D),f32)),
        in_specs=[V,A,V,A,A,V],out_specs=(A,A,A,A,A,V),
        scratch_shapes=[M(G*K4,D)]*3+[M(N,G*K4) if i in (1,2) else M(N,D) for i in range(4)]+[M(NB,G,4,Ch,n),M((G-1)*3*K4,D),M(G-1,3,K4,D),M(NB,n,D),pltpu.VMEM((NB,n,G*K4),f32),pltpu.VMEM((NB,n,D),f32),
            S(3,G,4),S(G-1,NB),S(NB*G),S(NB),S(G-1,3),S(G-1,3),S(NB),S(NB),S(2,NB),S(3,4),S(NB),S(4*C)],
        compiler_params=pltpu.CompilerParams(collective_id=2,has_side_effects=True,vmem_limit_bytes=60*2**20),
        cost_estimate=pl.CostEstimate(flops=3*10**10,bytes_accessed=10**8,transcendentals=0),
        name="middle")(mix,w2o,xo,cot,coto,gain.reshape(1,D))

def bwd_kernel(Z, C, n, qkv_ref, ot_ref, do_ref, lse_ref, pd_ref, segk_ref, segq_ref, ain_ref, wts_ref,
               xo_ref, gmid_ref, gain_ref, vec_ref, fb_ref,
               gi_ref, gwm_ref, gwq_ref, vo_ref,
               kv_scr, k_scr, v_scr, p_scr, ds_scr, dq_scr, dl_scr, dv_scr, dk_scr, a_scr, st_scr, dw_scr, qr_scr, fr_scr, zs_scr, zr_scr, t3_scr, t3r_scr, tb_scr, ot_scr, do_scr,
               dx_scr, dxr_scr, own_scr, xb_scr, gb_scr, va_scr, vb_scr, vs_scr, sc_scr,
               fs, frs, qs, qrs, zss, zrs, t3s, t3rs, cs_, crs, dxs, dxrs, gis, girs, ld, al, otl, dol, kvl, xl, vas, vars_, vbs, vbrs):
    z,k,q,s=[lax.axis_index(a) for a in AXES]
    G=2*C; g0=k*C+s; NB=4*C
    D=gain_ref.shape[1]; L=segq_ref.shape[1]; W=pd_ref.shape[0]; hb=W//HD; nb=L//BQ; sub=BQ//n
    nC=3*W; Dd=gwm_ref.shape[1]
    peers=list(itertools.product(range(2),range(C)))[1:]
    pdev=[(z,lax.rem(k+gc,2),q,lax.rem(s+gs,C)) for gc,gs in peers]
    pidx=[lax.rem(k+gc,2)*C+lax.rem(s+gs,C) for gc,gs in peers]
    back=[gc*C+(C-gs)%C for gc,gs in peers]
    fore=[gc*C+gs for gc,gs in peers]
    chipdev=[(z,k,partner(q,m),s) for m in range(4)]
    core=(z,1-k,q,s)
    zdev=[lax.rem(z+j,Z) for j in range(Z)]
    fcp={m: rcopy(fb_ref.at[m],fr_scr.at[m-1],fs.at[m],frs.at[m],chipdev[m]) for m in (1,2)}
    qcp={m: rcopy(dw_scr.at[m-1],qr_scr.at[m-1],qs.at[m],qrs.at[m],chipdev[m]) for m in (1,2)}
    zcp=[[rcopy(zs_scr.at[e%2,zdev[j]],zr_scr.at[e,z],zss.at[e,j],zrs.at[e,z],(zdev[j],k,q,s)) for j in range(1,Z)] for e in range(4)]
    t3cp=[rcopy(tb_scr.at[e],t3r_scr.at[e],t3s.at[e],t3rs.at[e],chipdev[3]) for e in range(2)]
    gws=(gwm_ref,gwq_ref)
    ccp=[rcopy(t3_scr.at[e,pl.ds(pl.multiple_of((1-k)*Dd,Dd),Dd),:],gws[e].at[k],cs_.at[e],crs.at[e],core) for e in range(2)]
    def load(src,dst,i):
        cp=pltpu.make_async_copy(src,dst,ld.at[i]); cp.start(); return cp
    def zsend(e, value):
        rows=D//Z; per=max(1,640//rows)
        for i in range(Z//per):
            ls=slice(i*per*rows,(i+1)*per*rows)
            zs_scr[e%2,i*per:(i+1)*per]=value(ls).T.reshape(per,rows,nC).astype(bf16)
        for cp in zcp[e]: cp.start()
    def zsum(e):
        for cp in zcp[e]: cp.wait_send()
        t=zs_scr[e%2,z].astype(f32)
        for j in range(1,Z):
            arrived(zr_scr.at[e,zdev[j]],zrs.at[e,zdev[j]])
            t=t+zr_scr[e,zdev[j]].astype(f32)
        return t
    def diag(e):
        tb_scr[e]=zsum(e).astype(bf16)
        t3cp[e].start()
    def final(e):
        t=zsum(2+e)
        arrived(t3r_scr.at[e],t3rs.at[e])
        t=t+t3r_scr[e].astype(f32)
        t3cp[e].wait_send()
        t3_scr[e]=t
        ccp[e].start()
        gws[e][k]=t3_scr[e,pl.ds(pl.multiple_of(k*Dd,Dd),Dd),:]
    kvcp=[pltpu.make_async_copy(qkv_ref.at[m],kv_scr.at[m],kvl.at[m]) for m in range(4)]
    for m in (3,2,1,0): kvcp[m].start()
    acp=pltpu.make_async_copy(ain_ref,a_scr,al)
    acp.start()
    def otcp(m): return pltpu.make_async_copy(ot_ref.at[:,m],ot_scr,otl)
    otcp(3).start()
    def docp(idx): return pltpu.make_async_copy(do_ref.at[:,3-idx],do_scr.at[lax.rem(idx,2)],dol.at[lax.rem(idx,2)])
    docp(0).start()
    greet(Z,C)
    for m in (1,2): fcp[m].start()
    load(fb_ref.at[3],st_scr,0).wait()
    zsend(0,lambda ls: st_scr[:,ls].astype(f32))
    sc_scr[...]=jnp.zeros_like(sc_scr)
    rowi=lax.broadcasted_iota(jnp.int32,(BQ,BQ),0)
    coli=lax.broadcasted_iota(jnp.int32,(BQ,BQ),1)
    hs=[slice(h*HD,(h+1)*HD) for h in range(hb)]
    H2=BQ//2

    def block(idx,_):
        m=3-idx
        pltpu.make_async_copy(qkv_ref.at[m],kv_scr.at[m],kvl.at[m]).wait()
        for h in range(hb):
            k_scr[h]=kv_scr[m,W+h*HD:W+(h+1)*HD,:].T
            v_scr[h]=kv_scr[m,2*W+h*HD:2*W+(h+1)*HD,:].T
        slot=lax.rem(idx,2)
        docp(idx).wait()
        @pl.when(idx<3)
        def _(): docp(idx+1).start()
        def tile(h,i):
            return jnp.concatenate([do_scr[slot,i*sub+t,hs[h],:] for t in range(sub)],1) if sub>1 else do_scr[slot,i,hs[h],:]
        otcp(m).wait()
        for i in range(nb):
            for h in range(hb):
                for t in range(sub):
                    B_=i*sub+t
                    dl_scr[h,:,B_*n:(B_+1)*n]=(do_scr[slot,B_,hs[h],:].astype(f32)*ot_scr[B_,hs[h],:].astype(f32)).sum(0,keepdims=True)
        @pl.when(m>0)
        def _(): otcp(m-1).start()
        units=[(j,h,i) for j in range(nb) for h in range(hb) for i in range(j,nb)]
        def phase_a(u):
            j,h,i=units[u]; cs=slice(i*BQ,(i+1)*BQ)
            for a in range(2):
                ks=slice(j*BQ+a*H2,j*BQ+(a+1)*H2)
                t=dot(k_scr[h,ks,:],kv_scr[m,hs[h],cs])
                dp=dot(v_scr[h,ks,:],tile(h,i))
                sk=segk_ref[ks,:]
                ok=jnp.concatenate([sk]*(BQ//128),axis=1)==segq_ref[:,cs]
                if j==i: ok=ok&(rowi[a*H2:(a+1)*H2]<=coli[a*H2:(a+1)*H2])
                p=jnp.exp(jnp.where(ok,t-lse_ref[m*hb+h,:,cs],NEG))
                p_scr[u%2,a*H2:(a+1)*H2,:]=p.astype(bf16)
                ds_scr[u%2,a*H2:(a+1)*H2,:]=(p*(dp-dl_scr[h,:,cs])).astype(bf16)
                yield
        def phase_b(u):
            j,h,i=units[u]; js=slice(j*BQ,(j+1)*BQ); cs=slice(i*BQ,(i+1)*BQ)
            p=p_scr[u%2]; ds=ds_scr[u%2]
            dv=dot(tile(h,i),p,NT); dk=dot(kv_scr[m,hs[h],cs],ds,NT)
            if i==j: dv_scr[h]=dv; dk_scr[h]=dk
            else: dv_scr[h]+=dv; dk_scr[h]+=dk
            yield
            dq=dot(kv_scr[m,W+h*HD:W+(h+1)*HD,js],ds)
            if j==0: dq_scr[hs[h],cs]=dq
            else: dq_scr[hs[h],cs]+=dq
            if i==nb-1:
                kv_scr[m,W+h*HD:W+(h+1)*HD,js]=dk_scr[h].astype(bf16)
                kv_scr[m,2*W+h*HD:2*W+(h+1)*HD,js]=dv_scr[h].astype(bf16)
            yield
        merge(phase_a(0))
        for u in range(len(units)):
            gs=[phase_b(u)]
            if u+1<len(units): gs=[phase_a(u+1)]+gs
            merge(*gs)
        dq=dq_scr[...]
        sc_scr[...]+=(dq*kv_scr[m,:W,:].astype(f32)).sum(1,keepdims=True)/pd_ref[:,:1]
        kv_scr[m,:W,:]=(dq*pd_ref[:,:1]).astype(bf16)
        @pl.when(idx==0)
        def _():
            acp.wait()
            zsend(1,lambda ls: dwt(3,ls))
        @pl.when((idx==1)|(idx==2))
        def _():
            for c in range(D//256):
                ls=slice(c*256,(c+1)*256)
                dw_scr[m-1,:,ls]=dwt(m,ls).astype(bf16)
        @pl.when(idx==1)
        def _():
            qcp[2].start()
            diag(0)
            ld0=load(fb_ref.at[0],st_scr,0)
            for m2 in (1,2): arrived(fr_scr.at[m2-1],frs.at[m2])
            ld0.wait()
            zsend(2,lambda ls: st_scr[:,ls].astype(f32)+fr_scr[0,:,ls].astype(f32)+fr_scr[1,:,ls].astype(f32))
        @pl.when(idx==2)
        def _():
            qcp[1].start()
            diag(1)
        return 0
    def dwt(m,ls):
        return dot(kv_scr[m],a_scr[:,ls])
    lax.fori_loop(0,4,block,0)
    for m2 in (1,2): arrived(qr_scr.at[m2-1],qrs.at[m2])
    zsend(3,lambda ls: dwt(0,ls)+qr_scr[0,:,ls].astype(f32)+qr_scr[1,:,ls].astype(f32))
    wcp=[pltpu.make_async_copy(wts_ref.at[m],a_scr.at[pl.ds(m*nC,nC),:],kvl.at[m]) for m in range(4)]
    for cp in wcp: cp.start()
    for cp in wcp: cp.wait()

    def chunk(i):
        gl=kv_scr[:,:,pl.ds(pl.multiple_of(i*BQ,BQ),BQ)].reshape(4*nC,BQ)
        return dot(gl,a_scr[:4*nC,:],TN)
    def xload(b):
        return [pltpu.make_async_copy(xo_ref.at[b],xb_scr.at[b%2],xl.at[0,b%2]),pltpu.make_async_copy(gmid_ref.at[b],gb_scr.at[b%2],xl.at[1,b%2])]
    for cp in xload(0): cp.start()
    dxcp=[[rcopy(dx_scr.at[i,b],dxr_scr.at[back[i]-1,b],dxs.at[i,b],dxrs.at[back[i],b],pdev[i]) for b in range(NB)] for i in range(G-1)]
    for b in range(NB):
        if sub==1:
            for i in range(G-1):
                dx_scr[i,b]=chunk(b*G+pidx[i]).astype(bf16)
                dxcp[i][b].start()
        else:
            own_scr[...]=chunk(b)
            for i in range(G-1):
                dx_scr[i,b]=own_scr[pl.ds(pl.multiple_of(pidx[i]*n,n),n),:].astype(bf16)
                dxcp[i][b].start()
    gicp=home_copies(C,n,dx_scr.at[0],gi_ref,gis,girs)
    gpart=None
    for b in range(NB):
        if b+1<NB:
            for cp in xload(b+1): cp.start()
        if sub==1:
            gain=chunk(b*G+g0)
        else:
            own_scr[...]=chunk(b)
            gain=own_scr[pl.ds(pl.multiple_of(g0*n,n),n),:]
        for i in range(G-1):
            arrived(dxr_scr.at[fore[i]-1,b],dxrs.at[fore[i],b])
            gain=gain+dxr_scr[fore[i]-1,b].astype(f32)
        for cp in xload(b): cp.wait()
        x=xb_scr[b%2].astype(f32)
        inv=lax.rsqrt(jnp.mean(x*x,axis=-1,keepdims=True)+norm_eps)
        nx=x*inv
        dn=gain*gain_ref[...]
        gin=gb_scr[b%2]+inv*(dn-nx*jnp.mean(dn*nx,axis=-1,keepdims=True))
        gp=(gain*nx).reshape(n//8,8,D).sum(0)
        gpart=gp if gpart is None else gpart+gp
        dxcp[0][b].wait_send()
        dx_scr[0,b]=gin.astype(bf16)
        spread_start(gicp[b:b+1])
    vs_scr[...]=jnp.zeros_like(vs_scr)
    vs_scr[0:1,:]=gpart.sum(0,keepdims=True)
    vs_scr[1:2,:]=vec_ref[...].sum(0,keepdims=True)
    sc=sc_scr[0:HD,:]
    for h in range(1,hb): sc=sc+sc_scr[h*HD:(h+1)*HD,:]
    vs_scr[2:3,0:HD]=sc.T[0:1,:]
    me=(k*4+q)*C+s
    va_scr[me]=vs_scr[...]
    plane=list(itertools.product(range(2),range(4),range(C)))[1:]
    vacp=[rcopy(vs_scr,va_scr.at[me],vas.at[i],vars_.at[me],(z,lax.rem(k+a,2),lax.rem(q+b,4),lax.rem(s+c,C))) for i,(a,b,c) in enumerate(plane)]
    for cp in vacp: cp.start()
    final(0)
    for a,b,c in plane:
        o=(lax.rem(k+a,2)*4+lax.rem(q+b,4))*C+lax.rem(s+c,C)
        arrived(va_scr.at[o],vars_.at[o])
    t=va_scr[0]
    for i in range(1,8*C): t=t+va_scr[i]
    vb_scr[z]=t
    vbcp=[rcopy(vb_scr.at[z],vb_scr.at[z],vbs.at[j],vbrs.at[z],(zdev[j],k,q,s)) for j in range(1,Z)]
    for cp in vbcp: cp.start()
    final(1)
    for j in range(1,Z): arrived(vb_scr.at[zdev[j]],vbrs.at[zdev[j]])
    t=vb_scr[0]
    for i in range(1,Z): t=t+vb_scr[i]
    vo_ref[...]=t
    for e in range(2):
        arrived(gws[e].at[1-k],crs.at[e])
        ccp[e].wait_send()
    home_arrived(C,n,gi_ref,girs)
    spread_sent(gicp)
    for i in range(1,G-1):
        for b in range(NB): dxcp[i][b].wait_send()
    for m in (1,2):
        fcp[m].wait_send(); qcp[m].wait_send()
    for cp in vacp+vbcp: cp.wait_send()

def backward(Z, C, qkv, ot, do, lse, pd, segk, segq, ain, wts, xo, gmid, gain, vec, fb, R, Pn, Dd):
    NB,n,D=xo.shape; G=2*C; nC=wts.shape[1]; W=pd.shape[0]; hb=W//HD; L=segq.shape[1]
    V=pl.BlockSpec(memory_space=pltpu.VMEM); A=pl.BlockSpec(memory_space=pl.ANY)
    S=lambda *sh: pltpu.SemaphoreType.DMA(sh) if sh else pltpu.SemaphoreType.DMA
    M=lambda *sh: pltpu.VMEM(sh,bf16)
    F=lambda *sh: pltpu.VMEM(sh,f32)
    gw=jax.ShapeDtypeStruct((2,Dd,nC),f32)
    return pl.pallas_call(functools.partial(bwd_kernel,Z,C,n),
        out_shape=(jax.ShapeDtypeStruct((R,Pn,D),bf16),gw,gw,jax.ShapeDtypeStruct((8,D),f32)),
        in_specs=[A,A,A,V,V,V,V,A,A,A,A,V,V,A],out_specs=(A,V,V,V),
        scratch_shapes=[M(4,nC,L),M(hb,L,HD),M(hb,L,HD),M(2,BQ,BQ),M(2,BQ,BQ),F(W,L),F(hb,1,L),F(hb,HD,BQ),F(hb,HD,BQ),M(L,D),
            M(nC,D),M(2,nC,D),M(2,nC,D),M(2,nC,D),M(2,Z,D//Z,nC),M(4,Z,D//Z,nC),F(2,D//Z,nC),M(2,D//Z,nC),M(2,D//Z,nC),M(NB*G,W,n),M(2,NB*G,W,n),
            M(G-1,NB,n,D),M(G-1,NB,n,D),F(BQ,D) if n<BQ else F(8,128),M(2,n,D),F(2,n,D),F(8*C,8,D),F(Z,8,D),F(8,D),F(W,1),
            S(4),S(4),S(4),S(4),S(4,Z),S(4,Z),S(2),S(2),S(2),S(2),S(G,NB),S(G,NB),S(NB),S(4*C),S(4),S(),S(),S(2),S(4),S(2,2),S(8*C),S(8*C),S(Z),S(Z)],
        compiler_params=pltpu.CompilerParams(collective_id=1,has_side_effects=True,vmem_limit_bytes=58*2**20),
        cost_estimate=pl.CostEstimate(flops=6*10**10,bytes_accessed=10**8,transcendentals=0),
        name="backward")(qkv,ot,do,lse,pd,segk,segq,ain.reshape(L,D),wts,xo,gmid,gain.reshape(1,D),vec,fb)

def finish_kernel(Ch, gi_ref, gwm_ref, gwq_ref, vo_ref, sf_ref, ig_ref, gq_ref, gk_ref, gv_ref, go_ref, gu_ref, gd_ref, ga_ref, gs_ref, gm_ref):
    ig_ref[...]=gi_ref[...].astype(f32)
    @pl.when(pl.program_id(0)==0)
    def _():
        def cols(ref,i):
            return jnp.concatenate([ref[0,:,i*Ch:(i+1)*Ch],ref[1,:,i*Ch:(i+1)*Ch]],1)
        for i,o in enumerate((gq_ref,gk_ref,gv_ref)): o[...]=cols(gwq_ref,i)
        go_ref[...]=cols(gwm_ref,0)
        gu_ref[...]=cols(gwm_ref,1)
        gd_ref[...]=cols(gwm_ref,2)
        ga_ref[...]=vo_ref[0,:]
        gm_ref[...]=vo_ref[1,:]
        gs_ref[...]=vo_ref[2,0:HD]*sf_ref[0,:]

def finish(gi, gwm, gwq, vo, sf):
    R,Pn,D=gi.shape; _,Dd,nC=gwm.shape; Ch=nC//3; T=4
    F=lambda *sh: jax.ShapeDtypeStruct(sh,f32)
    full=lambda *sh: pl.BlockSpec(sh,lambda i: (0,)*len(sh))
    row=pl.BlockSpec((R,Pn//T,D),lambda i:(0,i,0))
    shapes=[(Dd,2*Ch)]*6+[(D,),(HD,),(D,)]
    return pl.pallas_call(functools.partial(finish_kernel,Ch),grid=(T,),
        out_shape=(F(R,Pn,D),)+tuple(F(*sh) for sh in shapes),
        in_specs=[row,full(2,Dd,nC),full(2,Dd,nC),full(8,D),full(1,HD)],
        out_specs=(row,)+tuple(full(*sh) for sh in shapes),
        compiler_params=pltpu.CompilerParams(vmem_limit_bytes=60*2**20),
        name="finish")(gi,gwm,gwq,vo,sf.reshape(1,HD))


def make_local(Z, C):
    def local(tokens, segments, attn_gain, w_query, w_key, w_value, w_out, query_scale, mlp_gain, w_up, w_down, cotangent):
        R,Pn,D=tokens.shape
        Dd=w_query.shape[0]

        w1h,w2h,pd=prep(w_query,w_key,w_value,w_out,w_up,w_down,query_scale)
        xo,ain,wts,w2o,mix,qkv,ot,lse,segk,segq,coto=forward(Z,C,tokens,w1h,w2h,cotangent,attn_gain,pd,segments)
        _,block_out,do,gmid,fb,vec=middle(Z,C,mix,w2o,xo,cotangent,coto,mlp_gain)
        gi,gwm,gwq,vo=backward(Z,C,qkv,ot,do,lse,pd,segk,segq,ain,wts,xo,gmid,attn_gain,vec,fb,R,Pn,Dd)
        sf=(scale_base/math.sqrt(HD))*jax.nn.sigmoid(query_scale)
        ig,gq,gk,gv,go,gu,gd,ga,gs,gm=finish(gi,gwm,gwq,vo,sf)
        return (block_out,ig,ga,gq,gk,gv,go.T,gs,gm,gu,gd.T)
    return local

def solution(mesh):
    dp,T=mesh.shape["dp"],mesh.shape["tensor"]
    Z,C=dp//2,T//4
    fine=Mesh(mesh.devices.reshape(Z,2,4,C),AXES)
    dpx=("zz","core"); tx=("q","s")
    in_specs=(P(dpx,tx,None),P(dpx,None),P(),P(dpx,tx),P(dpx,tx),P(dpx,tx),P(tx,dpx),P(),P(),P(dpx,tx),P(tx,dpx),P(dpx,tx,None))
    out_specs=(P(dpx,tx,None),P(dpx,tx,None),P(),P(dpx,tx),P(dpx,tx),P(dpx,tx),P(tx,dpx),P(),P(),P(dpx,tx),P(tx,dpx))
    return jax.shard_map(make_local(Z,C),mesh=fine,in_specs=in_specs,out_specs=out_specs,check_vma=False)
```

time: 432 us -> 364 us (0.84)
  Pallas kernels: 317 us -> 357 us
  matrix products: 38.2 us -> 0 us
  other arithmetic: 26.1 us -> 0.53 us
  local copies, waits for them, and re-layouts: 25.9 us -> 3.4 us
  starting transfers between devices: 12 us -> 0 us
  waiting for transfers between devices: 7.71 us -> 0 us
    pallas_call x0 -> x3, Pallas kernels: none -> 68.2 us  [the longest x1 59.5 us: middle(): pl.pallas_call(functools.partial(mid_kernel, Z, C, n), out_shape=(B(NB, n...]
    dot_general x9 -> x0, matrix products: 38.2 us -> none  [dot(): return lax.dot_general(a, b, dims, preferred_element_type=f32)]
    slice x18 -> x0, local copies, waits for them, and re-layouts: 18.7 us -> none  [the longest x6 6.32 us: halves(): w[:, h * Ch:(h + 1) * Ch]]
    pallas_call x1, Pallas kernels: 143 us -> 125 us  [forward(): pl.pallas_call(functools.partial(fwd_kernel, Z, C, n), out_shape=(B(NB, n...]
    ppermute x9 -> x0, starting transfers between devices: 12 us -> none  [pp(): return lax.ppermute(x, AXES, [(lin[c], lin[fn(*c)]) for c in coords])]
    another operation x15 -> x0, other arithmetic: 10.6 us -> none
    pallas_call x1, Pallas kernels: 174 us -> 164 us  [backward(): pl.pallas_call(functools.partial(bwd_kernel, Z, C, n), out_shape=(jax.Sha...]
    ppermute x9 -> x0, waiting for transfers between devices: 7.71 us -> none  [pp(): return lax.ppermute(x, AXES, [(lin[c], lin[fn(*c)]) for c in coords])]
  transfers between devices with their start and end apart: 9 -> 0, of which waited for: 2 -> 0; matrix products, arithmetic and copies ran while one was open for 7% -> 0% of each run, Pallas kernels for 0% -> 0%
where the time goes in v2:
time: 364 us; the launch traced here: 362 us
  Pallas kernels  357 us (98%)
    pallas_call x1, Pallas kernels, backward(): pl.pallas_call(functools.partial(bwd_kernel, Z, C, n), out_shape=(jax.Sha...  164 us
    pallas_call x1, Pallas kernels, forward(): pl.pallas_call(functools.partial(fwd_kernel, Z, C, n), out_shape=(B(NB, n...  125 us
    pallas_call x1, Pallas kernels, middle(): pl.pallas_call(functools.partial(mid_kernel, Z, C, n), out_shape=(B(NB, n...  59.5 us

profile of v2, /device:TPU:6, one launch (start us, length us, event | category | flops | bytes accessed | tf_op | source)
XLA Modules:
  0.0 361.6 jit_solution(14694024900339765416)
XLA Ops:
  0.6 2.6 prep.1
  3.3 1.3 reshape.39.gain_ref
  4.6 0.0 copy-start.1
  4.6 124.6 %forward.1 = (bf16[4,256,1280]{2,1,0:T(8,128)(2,1)}, bf16[8,256,1280]{2,1,0:T(8,128)(2,1)}, bf16[4,480,1280]{2,1,0:T(8,128)(2,1)}, bf16[2,4,480,1280]{3,2,1,0:T(...) custom-call(bf16[2,512,1280]{2,1,0:T(8,128)(2,1)} %x_ref.1, ...), custom_call_target="tpu_custom_call" | custom-call | flops 30000001024 | bytes 100000000 | tf_op jit(solution)/shard_map/forward/pallas_call | solution.py:309
  129.2 0.0 copy-done.1
  129.2 0.6 reshape.40.gain_ref
  129.8 59.5 %middle.1 = (bf16[4,256,1280]{2,1,0:T(8,128)(2,1)}, bf16[2,512,1280]{2,1,0:T(8,128)(2,1)}, bf16[8,4,160,256]{3,2,1,0:T(8,128)(2,1)}, f32[4,256,1280]{2,1,0:T(8,1...) custom-call(bf16[4,2,4,160,256]{4,3,2,1,0:T(8,128)(2,1)} %get-tuple-element.47.mix_ref, ...), custom_call_target="tpu_custom_call" | custom-call | flops 30000001024 | bytes 100000000 | tf_op jit(solution)/shard_map/middle/pallas_call | solution.py:449
  189.3 0.0 copy-start.2
  189.3 163.7 %backward.1 = (bf16[2,512,1280]{2,1,0:T(8,128)(2,1)}, f32[2,160,480]{2,1,0:T(8,128)}, f32[2,160,480]{2,1,0:T(8,128)}, f32[8,1280]{1,0:T(8,128)}) custom-call(bf16[4,480,2048]{2,1,0:T(8,128)(2,1)} %get-tuple-element.52.qkv_ref, bf16[8,4,160,256]{3,2,1,0:T(8,128)(2,1)} %get-tuple-element.53.ot_ref, bf16[8,4,160,256]{3,2,1,0:T(8,128)(2,1)} %get-tuple-element.54.do_ref, ...), custom_call_target="tpu_custom_call" | custom-call | flops 60000002048 | bytes 100000000 | tf_op jit(solution)/shard_map/backward/pallas_call | solution.py:697
  353.0 0.0 copy-start
  353.0 0.0 copy-done.2
  353.0 0.5 multiply_bitcast_fusion.sf_ref
  353.5 6.1 %finish.1 = (f32[2,512,1280]{2,1,0:T(8,128)}, f32[160,320]{1,0:T(8,128)}, f32[160,320]{1,0:T(8,128)}, f32[160,320]{1,0:T(8,128)}, f32[160,320]{1,0:T(8,128)}, /*...) custom-call(bf16[2,512,1280]{2,1,0:T(8,128)(2,1)} %get-tuple-element.63.gi_ref, ...), custom_call_target="tpu_custom_call" | custom-call | tf_op jit(solution)/shard_map/finish/pallas_call | solution.py:728
  359.7 0.0 copy-done
  359.7 1.5 copy.24
Async XLA Ops:
  4.6 124.6 %copy-start.1 = (f32[1280]{0:T(1024)S(1)}, f32[1280]{0:T(1024)}, u32[]{:S(2)}) copy-start(f32[1280]{0:T(1024)} %param.20) | copy-start | bytes 15364
  189.3 163.7 %copy-start.2 = (f32[80]{0:T(128)S(1)}, f32[80]{0:T(128)}, u32[]{:S(2)}) copy-start(f32[80]{0:T(128)} %param.19) | copy-start | bytes 964
  353.0 6.7 %copy-start = (bf16[2,512,1280]{2,1,0:T(8,128)(2,1)S(1)}, bf16[2,512,1280]{2,1,0:T(8,128)(2,1)}, u32[]{:S(2)}) copy-start(bf16[2,512,1280]{2,1,0:T(8,128)(2,1)} %get-tuple-element.88) | copy-start | bytes 7864324

commit v3 on v2

--- a/solution.py
+++ b/solution.py
@@ -458,8 +458,8 @@
 def bwd_kernel(Z, C, n, qkv_ref, ot_ref, do_ref, lse_ref, pd_ref, segk_ref, segq_ref, ain_ref, wts_ref,
                xo_ref, gmid_ref, gain_ref, vec_ref, fb_ref,
                gi_ref, gwm_ref, gwq_ref, vo_ref,
-               kv_scr, k_scr, v_scr, p_scr, ds_scr, dq_scr, dl_scr, dv_scr, dk_scr, a_scr, st_scr, dw_scr, qr_scr, fr_scr, zs_scr, zr_scr, t3_scr, t3r_scr, tb_scr, ot_scr, do_scr,
-               dx_scr, dxr_scr, own_scr, xb_scr, gb_scr, va_scr, vb_scr, vs_scr, sc_scr,
+               kv_scr, k_scr, v_scr, p_scr, ds_scr, dq_scr, dl_scr, a_scr, dw_scr, qr_scr, big_scr, zs_scr, zr_scr, t3_scr, t3r_scr, tb_scr, ot_scr, do_scr,
+               dxr_scr, own_scr, xb_scr, gb_scr, va_scr, vb_scr, vs_scr, sc_scr,
                fs, frs, qs, qrs, zss, zrs, t3s, t3rs, cs_, crs, dxs, dxrs, gis, girs, ld, al, otl, dol, kvl, xl, vas, vars_, vbs, vbrs):
     z,k,q,s=[lax.axis_index(a) for a in AXES]
     G=2*C; g0=k*C+s; NB=4*C
@@ -473,7 +473,9 @@
     chipdev=[(z,k,partner(q,m),s) for m in range(4)]
     core=(z,1-k,q,s)
     zdev=[lax.rem(z+j,Z) for j in range(Z)]
-    fcp={m: rcopy(fb_ref.at[m],fr_scr.at[m-1],fs.at[m],frs.at[m],chipdev[m]) for m in (1,2)}
+    def frow(m): return big_scr.at[pl.ds((m-1)*nC,nC)]
+    def dxat(i,e): return big_scr.at[pl.ds((i*NB+e)*n,n)]
+    fcp={m: rcopy(fb_ref.at[m],frow(m),fs.at[m],frs.at[m],chipdev[m]) for m in (1,2)}
     qcp={m: rcopy(dw_scr.at[m-1],qr_scr.at[m-1],qs.at[m],qrs.at[m],chipdev[m]) for m in (1,2)}
     zcp=[[rcopy(zs_scr.at[e%2,zdev[j]],zr_scr.at[e,z],zss.at[e,j],zrs.at[e,z],(zdev[j],k,q,s)) for j in range(1,Z)] for e in range(4)]
     t3cp=[rcopy(tb_scr.at[e],t3r_scr.at[e],t3s.at[e],t3rs.at[e],chipdev[3]) for e in range(2)]
@@ -515,13 +517,12 @@
     docp(0).start()
     greet(Z,C)
     for m in (1,2): fcp[m].start()
-    load(fb_ref.at[3],st_scr,0).wait()
-    zsend(0,lambda ls: st_scr[:,ls].astype(f32))
+    load(fb_ref.at[3],dw_scr.at[0],0).wait()
+    zsend(0,lambda ls: dw_scr[0,:,ls].astype(f32))
     sc_scr[...]=jnp.zeros_like(sc_scr)
     rowi=lax.broadcasted_iota(jnp.int32,(BQ,BQ),0)
     coli=lax.broadcasted_iota(jnp.int32,(BQ,BQ),1)
     hs=[slice(h*HD,(h+1)*HD) for h in range(hb)]
-    H2=BQ//2
 
     def block(idx,_):
         m=3-idx
@@ -543,38 +544,39 @@
                     dl_scr[h,:,B_*n:(B_+1)*n]=(do_scr[slot,B_,hs[h],:].astype(f32)*ot_scr[B_,hs[h],:].astype(f32)).sum(0,keepdims=True)
         @pl.when(m>0)
         def _(): otcp(m-1).start()
-        units=[(j,h,i) for j in range(nb) for h in range(hb) for i in range(j,nb)]
-        def phase_a(u):
-            j,h,i=units[u]; cs=slice(i*BQ,(i+1)*BQ)
-            for a in range(2):
-                ks=slice(j*BQ+a*H2,j*BQ+(a+1)*H2)
+        rows=[(j,h) for j in range(nb) for h in range(hb)]
+        def phase_a(r):
+            j,h=rows[r]; ks=slice(j*BQ,(j+1)*BQ)
+            for i in range(j,nb):
+                cs=slice(i*BQ,(i+1)*BQ)
                 t=dot(k_scr[h,ks,:],kv_scr[m,hs[h],cs])
                 dp=dot(v_scr[h,ks,:],tile(h,i))
                 sk=segk_ref[ks,:]
                 ok=jnp.concatenate([sk]*(BQ//128),axis=1)==segq_ref[:,cs]
-                if j==i: ok=ok&(rowi[a*H2:(a+1)*H2]<=coli[a*H2:(a+1)*H2])
+                if j==i: ok=ok&(rowi<=coli)
                 p=jnp.exp(jnp.where(ok,t-lse_ref[m*hb+h,:,cs],NEG))
-                p_scr[u%2,a*H2:(a+1)*H2,:]=p.astype(bf16)
-                ds_scr[u%2,a*H2:(a+1)*H2,:]=(p*(dp-dl_scr[h,:,cs])).astype(bf16)
+                p_scr[r%2,:,cs]=p.astype(bf16)
+                ds_scr[r%2,:,cs]=(p*(dp-dl_scr[h,:,cs])).astype(bf16)
                 yield
-        def phase_b(u):
-            j,h,i=units[u]; js=slice(j*BQ,(j+1)*BQ); cs=slice(i*BQ,(i+1)*BQ)
-            p=p_scr[u%2]; ds=ds_scr[u%2]
-            dv=dot(tile(h,i),p,NT); dk=dot(kv_scr[m,hs[h],cs],ds,NT)
-            if i==j: dv_scr[h]=dv; dk_scr[h]=dk
-            else: dv_scr[h]+=dv; dk_scr[h]+=dk
+        def phase_b(r):
+            j,h=rows[r]; js=slice(j*BQ,(j+1)*BQ); rs=slice(j*BQ,L)
+            dos=jnp.concatenate([tile(h,i) for i in range(j,nb)],1)
+            dv=dot(dos,p_scr[r%2,:,rs],NT)
             yield
-            dq=dot(kv_scr[m,W+h*HD:W+(h+1)*HD,js],ds)
-            if j==0: dq_scr[hs[h],cs]=dq
-            else: dq_scr[hs[h],cs]+=dq
-            if i==nb-1:
-                kv_scr[m,W+h*HD:W+(h+1)*HD,js]=dk_scr[h].astype(bf16)
-                kv_scr[m,2*W+h*HD:2*W+(h+1)*HD,js]=dv_scr[h].astype(bf16)
+            dk=dot(kv_scr[m,hs[h],rs],ds_scr[r%2,:,rs],NT)
             yield
+            for i in range(j,nb):
+                cs=slice(i*BQ,(i+1)*BQ)
+                dq=dot(kv_scr[m,W+h*HD:W+(h+1)*HD,js],ds_scr[r%2,:,cs])
+                if j==0: dq_scr[hs[h],cs]=dq
+                else: dq_scr[hs[h],cs]+=dq
+                yield
+            kv_scr[m,W+h*HD:W+(h+1)*HD,js]=dk.astype(bf16)
+            kv_scr[m,2*W+h*HD:2*W+(h+1)*HD,js]=dv.astype(bf16)
         merge(phase_a(0))
-        for u in range(len(units)):
+        for u in range(len(rows)):
             gs=[phase_b(u)]
-            if u+1<len(units): gs=[phase_a(u+1)]+gs
+            if u+1<len(rows): gs=[phase_a(u+1)]+gs
             merge(*gs)
         dq=dq_scr[...]
         sc_scr[...]+=(dq*kv_scr[m,:W,:].astype(f32)).sum(1,keepdims=True)/pd_ref[:,:1]
@@ -592,10 +594,10 @@
         def _():
             qcp[2].start()
             diag(0)
-            ld0=load(fb_ref.at[0],st_scr,0)
-            for m2 in (1,2): arrived(fr_scr.at[m2-1],frs.at[m2])
+            ld0=load(fb_ref.at[0],dw_scr.at[0],0)
+            for m2 in (1,2): arrived(frow(m2),frs.at[m2])
             ld0.wait()
-            zsend(2,lambda ls: st_scr[:,ls].astype(f32)+fr_scr[0,:,ls].astype(f32)+fr_scr[1,:,ls].astype(f32))
+            zsend(2,lambda ls: dw_scr[0,:,ls].astype(f32)+big_scr[0:nC,ls].astype(f32)+big_scr[nC:2*nC,ls].astype(f32))
         @pl.when(idx==2)
         def _():
             qcp[1].start()
@@ -613,44 +615,51 @@
     def chunk(i):
         gl=kv_scr[:,:,pl.ds(pl.multiple_of(i*BQ,BQ),BQ)].reshape(4*nC,BQ)
         return dot(gl,a_scr[:4*nC,:],TN)
-    def xload(b):
-        return [pltpu.make_async_copy(xo_ref.at[b],xb_scr.at[b%2],xl.at[0,b%2]),pltpu.make_async_copy(gmid_ref.at[b],gb_scr.at[b%2],xl.at[1,b%2])]
-    for cp in xload(0): cp.start()
-    dxcp=[[rcopy(dx_scr.at[i,b],dxr_scr.at[back[i]-1,b],dxs.at[i,b],dxrs.at[back[i],b],pdev[i]) for b in range(NB)] for i in range(G-1)]
-    for b in range(NB):
-        if sub==1:
-            for i in range(G-1):
-                dx_scr[i,b]=chunk(b*G+pidx[i]).astype(bf16)
-                dxcp[i][b].start()
-        else:
-            own_scr[...]=chunk(b)
-            for i in range(G-1):
-                dx_scr[i,b]=own_scr[pl.ds(pl.multiple_of(pidx[i]*n,n),n),:].astype(bf16)
-                dxcp[i][b].start()
-    gicp=home_copies(C,n,dx_scr.at[0],gi_ref,gis,girs)
-    gpart=None
-    for b in range(NB):
-        if b+1<NB:
-            for cp in xload(b+1): cp.start()
+    order=[partner(q,m)*C+t for m in (3,1,2,0) for t in range(C)]
+    def xload(e):
+        b=order[e]
+        return [pltpu.make_async_copy(xo_ref.at[b],xb_scr.at[0],xl.at[0,0]),pltpu.make_async_copy(gmid_ref.at[b],gb_scr.at[0],xl.at[1,0])]
+    dxcp=[[rcopy(dxat(i,e),dxr_scr.at[back[i]-1,e],dxs.at[i,e],dxrs.at[back[i],e],pdev[i]) for e in range(NB)] for i in range(G-1)]
+    def give(e):
+        b=order[e]
+        if sub>1: own_scr[...]=chunk(b)
+        for i in range(G-1):
+            if sub==1: big_scr[(i*NB+e)*n:(i*NB+e+1)*n,:]=chunk(b*G+pidx[i]).astype(bf16)
+            else: big_scr[(i*NB+e)*n:(i*NB+e+1)*n,:]=own_scr[pl.ds(pl.multiple_of(pidx[i]*n,n),n),:].astype(bf16)
+            dxcp[i][e].start()
+    gicp=[]
+    gparts=[]
+    def take(e):
+        b=order[e]
+        for cp in xload(e): cp.start()
         if sub==1:
             gain=chunk(b*G+g0)
         else:
             own_scr[...]=chunk(b)
             gain=own_scr[pl.ds(pl.multiple_of(g0*n,n),n),:]
         for i in range(G-1):
-            arrived(dxr_scr.at[fore[i]-1,b],dxrs.at[fore[i],b])
-            gain=gain+dxr_scr[fore[i]-1,b].astype(f32)
-        for cp in xload(b): cp.wait()
-        x=xb_scr[b%2].astype(f32)
+            arrived(dxr_scr.at[fore[i]-1,e],dxrs.at[fore[i],e])
+            gain=gain+dxr_scr[fore[i]-1,e].astype(f32)
+        for cp in xload(e): cp.wait()
+        x=xb_scr[0].astype(f32)
         inv=lax.rsqrt(jnp.mean(x*x,axis=-1,keepdims=True)+norm_eps)
         nx=x*inv
         dn=gain*gain_ref[...]
-        gin=gb_scr[b%2]+inv*(dn-nx*jnp.mean(dn*nx,axis=-1,keepdims=True))
-        gp=(gain*nx).reshape(n//8,8,D).sum(0)
-        gpart=gp if gpart is None else gpart+gp
-        dxcp[0][b].wait_send()
-        dx_scr[0,b]=gin.astype(bf16)
-        spread_start(gicp[b:b+1])
+        gin=gb_scr[0]+inv*(dn-nx*jnp.mean(dn*nx,axis=-1,keepdims=True))
+        gparts.append((gain*nx).reshape(n//8,8,D).sum(0))
+        dxcp[0][e].wait_send()
+        big_scr[e*n:(e+1)*n,:]=gin.astype(bf16)
+        dst=gi_ref.at[lax.rem(q,2),pl.ds(pl.multiple_of((k*C+s)*n,n),n),:]
+        rs=girs.at[(lax.rem(q,2)*2+k)*C+s]
+        gicp.append((is_home()&(b==q*C+s),pltpu.make_async_copy(dxat(0,e),dst,rs),
+                     rcopy(dxat(0,e),dst,gis.at[e],rs,(z,lax.div(q,2),lax.div(b,C),lax.rem(b,C)))))
+        spread_start(gicp[-1:])
+    give(0)
+    for e in range(NB):
+        if e+1<NB: give(e+1)
+        take(e)
+    gpart=gparts[0]
+    for t in gparts[1:]: gpart=gpart+t
     vs_scr[...]=jnp.zeros_like(vs_scr)
     vs_scr[0:1,:]=gpart.sum(0,keepdims=True)
     vs_scr[1:2,:]=vec_ref[...].sum(0,keepdims=True)
@@ -682,7 +691,7 @@
     home_arrived(C,n,gi_ref,girs)
     spread_sent(gicp)
     for i in range(1,G-1):
-        for b in range(NB): dxcp[i][b].wait_send()
+        for e in range(NB): dxcp[i][e].wait_send()
     for m in (1,2):
         fcp[m].wait_send(); qcp[m].wait_send()
     for cp in vacp+vbcp: cp.wait_send()
@@ -697,9 +706,9 @@
     return pl.pallas_call(functools.partial(bwd_kernel,Z,C,n),
         out_shape=(jax.ShapeDtypeStruct((R,Pn,D),bf16),gw,gw,jax.ShapeDtypeStruct((8,D),f32)),
         in_specs=[A,A,A,V,V,V,V,A,A,A,A,V,V,A],out_specs=(A,V,V,V),
-        scratch_shapes=[M(4,nC,L),M(hb,L,HD),M(hb,L,HD),M(2,BQ,BQ),M(2,BQ,BQ),F(W,L),F(hb,1,L),F(hb,HD,BQ),F(hb,HD,BQ),M(L,D),
-            M(nC,D),M(2,nC,D),M(2,nC,D),M(2,nC,D),M(2,Z,D//Z,nC),M(4,Z,D//Z,nC),F(2,D//Z,nC),M(2,D//Z,nC),M(2,D//Z,nC),M(NB*G,W,n),M(2,NB*G,W,n),
-            M(G-1,NB,n,D),M(G-1,NB,n,D),F(BQ,D) if n<BQ else F(8,128),M(2,n,D),F(2,n,D),F(8*C,8,D),F(Z,8,D),F(8,D),F(W,1),
+        scratch_shapes=[M(4,nC,L),M(hb,L,HD),M(hb,L,HD),M(2,BQ,L),M(2,BQ,L),F(W,L),F(hb,1,L),M(L,D),
+            M(2,nC,D),M(2,nC,D),M(max(2*nC,(G-1)*NB*n),D),M(2,Z,D//Z,nC),M(4,Z,D//Z,nC),F(2,D//Z,nC),M(2,D//Z,nC),M(2,D//Z,nC),M(NB*G,W,n),M(2,NB*G,W,n),
+            M(G-1,NB,n,D),F(BQ,D) if n<BQ else F(8,128),M(1,n,D),F(1,n,D),F(8*C,8,D),F(Z,8,D),F(8,D),F(W,1),
             S(4),S(4),S(4),S(4),S(4,Z),S(4,Z),S(2),S(2),S(2),S(2),S(G,NB),S(G,NB),S(NB),S(4*C),S(4),S(),S(),S(2),S(4),S(2,2),S(8*C),S(8*C),S(Z),S(Z)],
         compiler_params=pltpu.CompilerParams(collective_id=1,has_side_effects=True,vmem_limit_bytes=58*2**20),
         cost_estimate=pl.CostEstimate(flops=6*10**10,bytes_accessed=10**8,transcendentals=0),

time: 364 us -> 351 us (0.964)
  Pallas kernels: 357 us -> 341 us
    pallas_call x1, Pallas kernels: 164 us -> 148 us  [backward(): pl.pallas_call(functools.partial(bwd_kernel, Z, C, n), out_shape=(jax.Sha...]
where the time goes in v3:
time: 351 us; the launch traced here: 346 us
  Pallas kernels  341 us (97%)
    pallas_call x1, Pallas kernels, backward(): pl.pallas_call(functools.partial(bwd_kernel, Z, C, n), out_shape=(jax.Sha...  148 us
    pallas_call x1, Pallas kernels, forward(): pl.pallas_call(functools.partial(fwd_kernel, Z, C, n), out_shape=(B(NB, n...  125 us
    pallas_call x1, Pallas kernels, middle(): pl.pallas_call(functools.partial(mid_kernel, Z, C, n), out_shape=(B(NB, n...  59.5 us

profile of v3, /device:TPU:6, one launch (start us, length us, event | category | flops | bytes accessed | tf_op | source)
XLA Modules:
  0.0 346.3 jit_solution(17862102946211948260)
XLA Ops:
  0.6 2.6 prep.1
  3.3 1.3 reshape.39.gain_ref
  4.6 0.0 copy-start.1
  4.6 124.6 %forward.1 = (bf16[4,256,1280]{2,1,0:T(8,128)(2,1)}, bf16[8,256,1280]{2,1,0:T(8,128)(2,1)}, bf16[4,480,1280]{2,1,0:T(8,128)(2,1)}, bf16[2,4,480,1280]{3,2,1,0:T(...) custom-call(bf16[2,512,1280]{2,1,0:T(8,128)(2,1)} %x_ref.1, ...), custom_call_target="tpu_custom_call" | custom-call | flops 30000001024 | bytes 100000000 | tf_op jit(solution)/shard_map/forward/pallas_call | solution.py:309
  129.2 0.0 copy-done.1
  129.2 0.6 reshape.40.gain_ref
  129.8 59.5 %middle.1 = (bf16[4,256,1280]{2,1,0:T(8,128)(2,1)}, bf16[2,512,1280]{2,1,0:T(8,128)(2,1)}, bf16[8,4,160,256]{3,2,1,0:T(8,128)(2,1)}, f32[4,256,1280]{2,1,0:T(8,1...) custom-call(bf16[4,2,4,160,256]{4,3,2,1,0:T(8,128)(2,1)} %get-tuple-element.47.mix_ref, ...), custom_call_target="tpu_custom_call" | custom-call | flops 30000001024 | bytes 100000000 | tf_op jit(solution)/shard_map/middle/pallas_call | solution.py:449
  189.3 0.0 copy-start.2
  189.3 148.4 %backward.1 = (bf16[2,512,1280]{2,1,0:T(8,128)(2,1)}, f32[2,160,480]{2,1,0:T(8,128)}, f32[2,160,480]{2,1,0:T(8,128)}, f32[8,1280]{1,0:T(8,128)}) custom-call(bf16[4,480,2048]{2,1,0:T(8,128)(2,1)} %get-tuple-element.52.qkv_ref, bf16[8,4,160,256]{3,2,1,0:T(8,128)(2,1)} %get-tuple-element.53.ot_ref, bf16[8,4,160,256]{3,2,1,0:T(8,128)(2,1)} %get-tuple-element.54.do_ref, ...), custom_call_target="tpu_custom_call" | custom-call | flops 60000002048 | bytes 100000000 | tf_op jit(solution)/shard_map/backward/pallas_call | solution.py:706
  337.7 0.0 copy-start
  337.7 0.0 copy-done.2
  337.7 0.5 multiply_bitcast_fusion.sf_ref
  338.3 6.1 %finish.1 = (f32[2,512,1280]{2,1,0:T(8,128)}, f32[160,320]{1,0:T(8,128)}, f32[160,320]{1,0:T(8,128)}, f32[160,320]{1,0:T(8,128)}, f32[160,320]{1,0:T(8,128)}, /*...) custom-call(bf16[2,512,1280]{2,1,0:T(8,128)(2,1)} %get-tuple-element.63.gi_ref, ...), custom_call_target="tpu_custom_call" | custom-call | tf_op jit(solution)/shard_map/finish/pallas_call | solution.py:737
  344.4 0.0 copy-done
  344.4 1.5 copy.24
Async XLA Ops:
  4.6 124.6 %copy-start.1 = (f32[1280]{0:T(1024)S(1)}, f32[1280]{0:T(1024)}, u32[]{:S(2)}) copy-start(f32[1280]{0:T(1024)} %param.20) | copy-start | bytes 15364
  189.3 148.4 %copy-start.2 = (f32[80]{0:T(128)S(1)}, f32[80]{0:T(128)}, u32[]{:S(2)}) copy-start(f32[80]{0:T(128)} %param.19) | copy-start | bytes 964
  337.7 6.7 %copy-start = (bf16[2,512,1280]{2,1,0:T(8,128)(2,1)S(1)}, bf16[2,512,1280]{2,1,0:T(8,128)(2,1)}, u32[]{:S(2)}) copy-start(bf16[2,512,1280]{2,1,0:T(8,128)(2,1)} %get-tuple-element.88) | copy-start | bytes 7864324

commit v4 on v3

--- a/solution.py
+++ b/solution.py
@@ -354,62 +354,78 @@
     spread_far(cots,"start")
     for b in near_blocks(C): pltpu.make_async_copy(coto_ref.at[b],co_scr.at[b],cot_r.at[b]).start()
     order=[partner(q,m)*C+(lax.rem(s+t,C)) for m in range(4) for t in range(C)]
-    def rows(b): return pl.ds(pl.multiple_of(b*n,n),n)
     outs=[]
     def put(src,dst,sem):
         cp=pltpu.make_async_copy(src,dst,sem); cp.start(); outs.append(cp)
     vec_ref[...]=jnp.zeros_like(vec_ref)
     for cp in wcp[0]: cp.wait()
-    for e,b in enumerate(order):
+    def slot(e): return slice(e*n,(e+1)*n)
+    def ahead(e):
+        b=order[e]
         attn=dot(mix_ref[b].reshape(G*K4,n),wo_scr[...],TN)
         middle=xo_ref[b].astype(f32)+attn
-        mid_scr[b]=middle
+        mid_scr[e]=middle
         inv=lax.rsqrt(jnp.mean(middle*middle,axis=-1,keepdims=True)+norm_eps)
-        mi_scr[rows(b),:]=(middle*inv*gain_ref[...]).astype(bf16)
+        mi_scr[slot(e),:]=(middle*inv*gain_ref[...]).astype(bf16)
+        yield
         if e==0:
             for cp in wcp[1]+wcp[2]: cp.wait()
-        up=dot(mi_scr[rows(b),:],wu_scr[...],NT)
-        up_scr[b]=up
-        hid_scr[rows(b),:]=(up*(1.0/(1.0+jnp.exp(-up)))).astype(bf16)
-        gs_scr[rows(b),:]=(middle+dot(hid_scr[rows(b),:],wd_scr[...])).astype(bf16)
-        put(gs_scr.at[rows(b)],bo_ref.at[b],out_s.at[0,e])
+        up=dot(mi_scr[slot(e),:],wu_scr[...],NT)
+        up_scr[e]=up
+        hid_scr[slot(e),:]=(up*(1.0/(1.0+jnp.exp(-up)))).astype(bf16)
+        yield
+        gs_scr[slot(e),:]=(mid_scr[e]+dot(hid_scr[slot(e),:],wd_scr[...])).astype(bf16)
+        yield
+    for e in range(0,NB,2):
+        merge(ahead(e),ahead(e+1))
+        for i in (e,e+1): put(gs_scr.at[slot(i)],bo_ref.at[order[i]],out_s.at[0,i])
     exch=[]
     home=[]
     boouts=list(outs); outs=[]
-    for e,b in enumerate(order):
-        if e<3*C: pltpu.make_async_copy(coto_ref.at[b],co_scr.at[b],cot_r.at[b]).wait()
-        else: arrived(co_scr.at[b],cot_r.at[b])
-        boouts[e].wait()
-        dst=bh_ref.at[lax.rem(q,2),pl.ds(pl.multiple_of((k*C+s)*n,n),n),:]
-        rs=bors.at[(lax.rem(q,2)*2+k)*C+s]
-        mine=is_home()&(b==q*C+s)
-        home.append((mine,pltpu.make_async_copy(bo_ref.at[b],dst,rs),rcopy(bo_ref.at[b],dst,bos.at[e],rs,(z,lax.div(q,2),lax.div(b,C),lax.rem(b,C)))))
-        spread_start(home[-1:])
+    def behind(e):
+        b=order[e]
         gh=dot(co_scr[b],wd_scr[...],NT)
-        up=up_scr[b]
+        up=up_scr[e]
         sg=1.0/(1.0+jnp.exp(-up))
-        gup_scr[rows(b),:]=(gh*(sg*(1.0+up*(1.0-sg)))).astype(bf16)
-        gmlp=dot(gup_scr[rows(b),:],wu_scr[...])
-        middle=mid_scr[b]
+        gup_scr[slot(e),:]=(gh*(sg*(1.0+up*(1.0-sg)))).astype(bf16)
+        yield
+        gmlp=dot(gup_scr[slot(e),:],wu_scr[...])
+        middle=mid_scr[e]
         inv=lax.rsqrt(jnp.mean(middle*middle,axis=-1,keepdims=True)+norm_eps)
         n2=middle*inv
         dn=gmlp*gain_ref[...]
         gm=co_scr[b].astype(f32)+inv*(dn-n2*jnp.mean(dn*n2,axis=-1,keepdims=True))
         vec_ref[...]+=(gmlp*n2).reshape(n//8,8,D).sum(0)
-        mid_scr[b]=gm
-        put(mid_scr.at[b],gm_ref.at[b],out_s.at[1,e])
-        ga_scr[rows(b),:]=gm.astype(bf16)
-        gt_scr[b]=dot(wo_scr[...],ga_scr[rows(b),:],NT).astype(bf16).reshape(G,4,Ch,n)
-        lc=pltpu.make_async_copy(gt_scr.at[b,0],do_ref.at[b*G+g0],dol.at[e])
-        lc.start(); exch.append(lc)
-        for i in range(G-1):
-            cp=rcopy(gt_scr.at[b,fore[i]],do_ref.at[b*G+g0],dos.at[i,e],dors.at[b*G+g0],pdev[i])
-            cp.start(); exch.append(cp)
+        mid_scr[e]=gm
+        ga_scr[slot(e),:]=gm.astype(bf16)
+        yield
+        gt_scr[e]=dot(wo_scr[...],ga_scr[slot(e),:],NT).astype(bf16).reshape(G,4,Ch,n)
+        yield
+    for e0 in range(0,NB,2):
+        for e in (e0,e0+1):
+            b=order[e]
+            if e<3*C: pltpu.make_async_copy(coto_ref.at[b],co_scr.at[b],cot_r.at[b]).wait()
+            else: arrived(co_scr.at[b],cot_r.at[b])
+            boouts[e].wait()
+            dst=bh_ref.at[lax.rem(q,2),pl.ds(pl.multiple_of((k*C+s)*n,n),n),:]
+            rs=bors.at[(lax.rem(q,2)*2+k)*C+s]
+            mine=is_home()&(b==q*C+s)
+            home.append((mine,pltpu.make_async_copy(bo_ref.at[b],dst,rs),rcopy(bo_ref.at[b],dst,bos.at[e],rs,(z,lax.div(q,2),lax.div(b,C),lax.rem(b,C)))))
+            spread_start(home[-1:])
+        merge(behind(e0),behind(e0+1))
+        for e in (e0,e0+1):
+            b=order[e]
+            put(mid_scr.at[e],gm_ref.at[b],out_s.at[1,e])
+            lc=pltpu.make_async_copy(gt_scr.at[e,0],do_ref.at[b*G+g0],dol.at[e])
+            lc.start(); exch.append(lc)
+            for i in range(G-1):
+                cp=rcopy(gt_scr.at[e,fore[i]],do_ref.at[b*G+g0],dos.at[i,e],dors.at[b*G+g0],pdev[i])
+                cp.start(); exch.append(cp)
     def wgrad(i,g):
         cs=slice(g*K4,(g+1)*K4)
-        if i==0: return dot(jnp.concatenate([mix_ref[b,g].reshape(K4,n) for b in range(NB)],1),ga_scr[...])
+        if i==0: return dot(jnp.concatenate([mix_ref[b,g].reshape(K4,n) for b in order],1),ga_scr[...])
         if i==1: return dot(gup_scr[:,cs],mi_scr[...],TN)
-        return dot(hid_scr[:,cs],co_scr[...].reshape(N,D),TN)
+        return dot(hid_scr[:,cs],jnp.concatenate([co_scr[b] for b in order],0),TN)
     for cp in outs: cp.wait()
     outs=[]
     def part(j,i): return pl.ds((j*3+i)*K4,K4)

time: 351 us -> 348 us (level)
  Pallas kernels: 341 us -> 337 us
    pallas_call x1, Pallas kernels: 59.5 us -> 55 us  [middle(): pl.pallas_call(functools.partial(mid_kernel, Z, C, n), out_shape=(B(NB, n...]
where the time goes in v4:
time: 348 us; the launch traced here: 342 us
  Pallas kernels  337 us (97%)
    pallas_call x1, Pallas kernels, backward(): pl.pallas_call(functools.partial(bwd_kernel, Z, C, n), out_shape=(jax.Sha...  149 us
    pallas_call x1, Pallas kernels, forward(): pl.pallas_call(functools.partial(fwd_kernel, Z, C, n), out_shape=(B(NB, n...  125 us
    pallas_call x1, Pallas kernels, middle(): pl.pallas_call(functools.partial(mid_kernel, Z, C, n), out_shape=(B(NB, n...  55 us

profile of v4, /device:TPU:6, one launch (start us, length us, event | category | flops | bytes accessed | tf_op | source)
XLA Modules:
  0.0 341.9 jit_solution(6100570543659972345)
XLA Ops:
  0.6 2.6 prep.1
  3.3 1.3 reshape.39.gain_ref
  4.6 0.0 copy-start.1
  4.6 124.6 %forward.1 = (bf16[4,256,1280]{2,1,0:T(8,128)(2,1)}, bf16[8,256,1280]{2,1,0:T(8,128)(2,1)}, bf16[4,480,1280]{2,1,0:T(8,128)(2,1)}, bf16[2,4,480,1280]{3,2,1,0:T(...) custom-call(bf16[2,512,1280]{2,1,0:T(8,128)(2,1)} %x_ref.1, ...), custom_call_target="tpu_custom_call" | custom-call | flops 30000001024 | bytes 100000000 | tf_op jit(solution)/shard_map/forward/pallas_call | solution.py:309
  129.2 0.0 copy-done.1
  129.2 0.6 reshape.40.gain_ref
  129.8 55.0 %middle.1 = (bf16[4,256,1280]{2,1,0:T(8,128)(2,1)}, bf16[2,512,1280]{2,1,0:T(8,128)(2,1)}, bf16[8,4,160,256]{3,2,1,0:T(8,128)(2,1)}, f32[4,256,1280]{2,1,0:T(8,1...) custom-call(bf16[4,2,4,160,256]{4,3,2,1,0:T(8,128)(2,1)} %get-tuple-element.47.mix_ref, ...), custom_call_target="tpu_custom_call" | custom-call | flops 30000001024 | bytes 100000000 | tf_op jit(solution)/shard_map/middle/pallas_call | solution.py:465
  184.8 0.0 copy-start.2
  184.8 148.7 %backward.1 = (bf16[2,512,1280]{2,1,0:T(8,128)(2,1)}, f32[2,160,480]{2,1,0:T(8,128)}, f32[2,160,480]{2,1,0:T(8,128)}, f32[8,1280]{1,0:T(8,128)}) custom-call(bf16[4,480,2048]{2,1,0:T(8,128)(2,1)} %get-tuple-element.52.qkv_ref, bf16[8,4,160,256]{3,2,1,0:T(8,128)(2,1)} %get-tuple-element.53.ot_ref, bf16[8,4,160,256]{3,2,1,0:T(8,128)(2,1)} %get-tuple-element.54.do_ref, ...), custom_call_target="tpu_custom_call" | custom-call | flops 60000002048 | bytes 100000000 | tf_op jit(solution)/shard_map/backward/pallas_call | solution.py:722
  333.5 0.0 copy-start
  333.5 0.0 copy-done.2
  333.5 0.5 multiply_bitcast_fusion.sf_ref
  334.0 6.1 %finish.1 = (f32[2,512,1280]{2,1,0:T(8,128)}, f32[160,320]{1,0:T(8,128)}, f32[160,320]{1,0:T(8,128)}, f32[160,320]{1,0:T(8,128)}, f32[160,320]{1,0:T(8,128)}, /*...) custom-call(bf16[2,512,1280]{2,1,0:T(8,128)(2,1)} %get-tuple-element.63.gi_ref, ...), custom_call_target="tpu_custom_call" | custom-call | tf_op jit(solution)/shard_map/finish/pallas_call | solution.py:753
  340.2 0.0 copy-done
  340.2 1.5 copy.24
Async XLA Ops:
  4.6 124.6 %copy-start.1 = (f32[1280]{0:T(1024)S(1)}, f32[1280]{0:T(1024)}, u32[]{:S(2)}) copy-start(f32[1280]{0:T(1024)} %param.20) | copy-start | bytes 15364
  184.8 148.7 %copy-start.2 = (f32[80]{0:T(128)S(1)}, f32[80]{0:T(128)}, u32[]{:S(2)}) copy-start(f32[80]{0:T(128)} %param.19) | copy-start | bytes 964
  333.5 6.7 %copy-start = (bf16[2,512,1280]{2,1,0:T(8,128)(2,1)S(1)}, bf16[2,512,1280]{2,1,0:T(8,128)(2,1)}, u32[]{:S(2)}) copy-start(bf16[2,512,1280]{2,1,0:T(8,128)(2,1)} %get-tuple-element.88) | copy-start | bytes 7864324

commit v5 on v4

--- a/solution.py
+++ b/solution.py
@@ -475,8 +475,8 @@
                xo_ref, gmid_ref, gain_ref, vec_ref, fb_ref,
                gi_ref, gwm_ref, gwq_ref, vo_ref,
                kv_scr, k_scr, v_scr, p_scr, ds_scr, dq_scr, dl_scr, a_scr, dw_scr, qr_scr, big_scr, zs_scr, zr_scr, t3_scr, t3r_scr, tb_scr, ot_scr, do_scr,
-               dxr_scr, own_scr, xb_scr, gb_scr, va_scr, vb_scr, vs_scr, sc_scr,
-               fs, frs, qs, qrs, zss, zrs, t3s, t3rs, cs_, crs, dxs, dxrs, gis, girs, ld, al, otl, dol, kvl, xl, vas, vars_, vbs, vbrs):
+               dxr_scr, wx_scr, own_scr, xb_scr, gb_scr, va_scr, vb_scr, vs_scr, sc_scr,
+               fs, frs, qs, qrs, zss, zrs, t3s, t3rs, cs_, crs, dxs, dxrs, gis, girs, ld, al, otl, dol, kvl, wtl, xl, vas, vars_, vbs, vbrs):
     z,k,q,s=[lax.axis_index(a) for a in AXES]
     G=2*C; g0=k*C+s; NB=4*C
     D=gain_ref.shape[1]; L=segq_ref.shape[1]; W=pd_ref.shape[0]; hb=W//HD; nb=L//BQ; sub=BQ//n
@@ -493,55 +493,59 @@
     def dxat(i,e): return big_scr.at[pl.ds((i*NB+e)*n,n)]
     fcp={m: rcopy(fb_ref.at[m],frow(m),fs.at[m],frs.at[m],chipdev[m]) for m in (1,2)}
     qcp={m: rcopy(dw_scr.at[m-1],qr_scr.at[m-1],qs.at[m],qrs.at[m],chipdev[m]) for m in (1,2)}
-    zcp=[[rcopy(zs_scr.at[e%2,zdev[j]],zr_scr.at[e,z],zss.at[e,j],zrs.at[e,z],(zdev[j],k,q,s)) for j in range(1,Z)] for e in range(4)]
-    t3cp=[rcopy(tb_scr.at[e],t3r_scr.at[e],t3s.at[e],t3rs.at[e],chipdev[3]) for e in range(2)]
+    slot_of=(0,1,0,0)
+    zcp=[[rcopy(zs_scr.at[slot_of[e],zdev[j]],zr_scr.at[e%3,z],zss.at[e,j],zrs.at[e,z],(zdev[j],k,q,s)) for j in range(1,Z)] for e in range(4)]
+    t3cp=[rcopy(tb_scr,t3r_scr.at[e],t3s.at[e],t3rs.at[e],chipdev[3]) for e in range(2)]
     gws=(gwm_ref,gwq_ref)
-    ccp=[rcopy(t3_scr.at[e,pl.ds(pl.multiple_of((1-k)*Dd,Dd),Dd),:],gws[e].at[k],cs_.at[e],crs.at[e],core) for e in range(2)]
+    ccp=[rcopy(t3_scr.at[pl.ds(pl.multiple_of((1-k)*Dd,Dd),Dd),:],gws[e].at[k],cs_.at[e],crs.at[e],core) for e in range(2)]
+    def wcopy(m): return pltpu.make_async_copy(wts_ref.at[m],(dw_scr.at[m] if m<2 else wx_scr.at[m-2]),wtl.at[m])
     def load(src,dst,i):
         cp=pltpu.make_async_copy(src,dst,ld.at[i]); cp.start(); return cp
     def zsend(e, value):
         rows=D//Z; per=max(1,640//rows)
         for i in range(Z//per):
             ls=slice(i*per*rows,(i+1)*per*rows)
-            zs_scr[e%2,i*per:(i+1)*per]=value(ls).T.reshape(per,rows,nC).astype(bf16)
+            zs_scr[slot_of[e],i*per:(i+1)*per]=value(ls).T.reshape(per,rows,nC).astype(bf16)
         for cp in zcp[e]: cp.start()
     def zsum(e):
         for cp in zcp[e]: cp.wait_send()
-        t=zs_scr[e%2,z].astype(f32)
+        t=zs_scr[slot_of[e],z].astype(f32)
         for j in range(1,Z):
-            arrived(zr_scr.at[e,zdev[j]],zrs.at[e,zdev[j]])
-            t=t+zr_scr[e,zdev[j]].astype(f32)
+            arrived(zr_scr.at[e%3,zdev[j]],zrs.at[e,zdev[j]])
+            t=t+zr_scr[e%3,zdev[j]].astype(f32)
         return t
     def diag(e):
-        tb_scr[e]=zsum(e).astype(bf16)
+        tb_scr[...]=zsum(e).astype(bf16)
         t3cp[e].start()
     def final(e):
         t=zsum(2+e)
         arrived(t3r_scr.at[e],t3rs.at[e])
         t=t+t3r_scr[e].astype(f32)
         t3cp[e].wait_send()
-        t3_scr[e]=t
+        if e==1: ccp[0].wait_send()
+        t3_scr[...]=t
         ccp[e].start()
-        gws[e][k]=t3_scr[e,pl.ds(pl.multiple_of(k*Dd,Dd),Dd),:]
+        gws[e][k]=t3_scr[pl.ds(pl.multiple_of(k*Dd,Dd),Dd),:]
     kvcp=[pltpu.make_async_copy(qkv_ref.at[m],kv_scr.at[m],kvl.at[m]) for m in range(4)]
-    for m in (3,2,1,0): kvcp[m].start()
+    for m in (1,2,3,0): kvcp[m].start()
     acp=pltpu.make_async_copy(ain_ref,a_scr,al)
     acp.start()
     def otcp(m): return pltpu.make_async_copy(ot_ref.at[:,m],ot_scr,otl)
-    otcp(3).start()
-    def docp(idx): return pltpu.make_async_copy(do_ref.at[:,3-idx],do_scr.at[lax.rem(idx,2)],dol.at[lax.rem(idx,2)])
+    otcp(1).start()
+    def docp(idx): return pltpu.make_async_copy(do_ref.at[:,lax.rem(idx+1,4)],do_scr.at[lax.rem(idx,2)],dol.at[lax.rem(idx,2)])
     docp(0).start()
     greet(Z,C)
     for m in (1,2): fcp[m].start()
     load(fb_ref.at[3],dw_scr.at[0],0).wait()
     zsend(0,lambda ls: dw_scr[0,:,ls].astype(f32))
+    ld0=load(fb_ref.at[0],dw_scr.at[1],1)
     sc_scr[...]=jnp.zeros_like(sc_scr)
     rowi=lax.broadcasted_iota(jnp.int32,(BQ,BQ),0)
     coli=lax.broadcasted_iota(jnp.int32,(BQ,BQ),1)
     hs=[slice(h*HD,(h+1)*HD) for h in range(hb)]
 
     def block(idx,_):
-        m=3-idx
+        m=lax.rem(idx+1,4)
         pltpu.make_async_copy(qkv_ref.at[m],kv_scr.at[m],kvl.at[m]).wait()
         for h in range(hb):
             k_scr[h]=kv_scr[m,W+h*HD:W+(h+1)*HD,:].T
@@ -558,8 +562,8 @@
                 for t in range(sub):
                     B_=i*sub+t
                     dl_scr[h,:,B_*n:(B_+1)*n]=(do_scr[slot,B_,hs[h],:].astype(f32)*ot_scr[B_,hs[h],:].astype(f32)).sum(0,keepdims=True)
-        @pl.when(m>0)
-        def _(): otcp(m-1).start()
+        @pl.when(idx<3)
+        def _(): otcp(lax.rem(idx+2,4)).start()
         rows=[(j,h) for j in range(nb) for h in range(hb)]
         def phase_a(r):
             j,h=rows[r]; ks=slice(j*BQ,(j+1)*BQ)
@@ -589,48 +593,51 @@
                 yield
             kv_scr[m,W+h*HD:W+(h+1)*HD,js]=dk.astype(bf16)
             kv_scr[m,2*W+h*HD:2*W+(h+1)*HD,js]=dv.astype(bf16)
-        merge(phase_a(0))
-        for u in range(len(rows)):
-            gs=[phase_b(u)]
-            if u+1<len(rows): gs=[phase_a(u+1)]+gs
-            merge(*gs)
+        def attend(part):
+            merge(phase_a(part[0]))
+            for u in part:
+                gs=[phase_b(u)]
+                if u+1<=part[-1]: gs=[phase_a(u+1)]+gs
+                merge(*gs)
+        attend(range(2*hb))
+        @pl.when(idx==1)
+        def _():
+            diag(0)
+            for m2 in (1,2): arrived(frow(m2),frs.at[m2])
+            ld0.wait()
+            zsend(2,lambda ls: dw_scr[1,:,ls].astype(f32)+big_scr[0:nC,ls].astype(f32)+big_scr[nC:2*nC,ls].astype(f32))
+        @pl.when(idx==3)
+        def _():
+            final(0)
+            for m2 in (1,2): qcp[m2].wait_send()
+            for m2 in range(4): wcopy(m2).start()
+        attend(range(2*hb,len(rows)))
         dq=dq_scr[...]
         sc_scr[...]+=(dq*kv_scr[m,:W,:].astype(f32)).sum(1,keepdims=True)/pd_ref[:,:1]
         kv_scr[m,:W,:]=(dq*pd_ref[:,:1]).astype(bf16)
         @pl.when(idx==0)
-        def _():
-            acp.wait()
-            zsend(1,lambda ls: dwt(3,ls))
-        @pl.when((idx==1)|(idx==2))
+        def _(): acp.wait()
+        @pl.when(idx<2)
         def _():
             for c in range(D//256):
                 ls=slice(c*256,(c+1)*256)
                 dw_scr[m-1,:,ls]=dwt(m,ls).astype(bf16)
-        @pl.when(idx==1)
-        def _():
-            qcp[2].start()
-            diag(0)
-            ld0=load(fb_ref.at[0],dw_scr.at[0],0)
-            for m2 in (1,2): arrived(frow(m2),frs.at[m2])
-            ld0.wait()
-            zsend(2,lambda ls: dw_scr[0,:,ls].astype(f32)+big_scr[0:nC,ls].astype(f32)+big_scr[nC:2*nC,ls].astype(f32))
-        @pl.when(idx==2)
+        @pl.when(idx==0)
         def _():
             qcp[1].start()
-            diag(1)
+        @pl.when(idx==1)
+        def _(): qcp[2].start()
+        @pl.when(idx==2)
+        def _(): zsend(1,lambda ls: dwt(3,ls))
         return 0
     def dwt(m,ls):
         return dot(kv_scr[m],a_scr[:,ls])
     lax.fori_loop(0,4,block,0)
-    for m2 in (1,2): arrived(qr_scr.at[m2-1],qrs.at[m2])
-    zsend(3,lambda ls: dwt(0,ls)+qr_scr[0,:,ls].astype(f32)+qr_scr[1,:,ls].astype(f32))
-    wcp=[pltpu.make_async_copy(wts_ref.at[m],a_scr.at[pl.ds(m*nC,nC),:],kvl.at[m]) for m in range(4)]
-    for cp in wcp: cp.start()
-    for cp in wcp: cp.wait()
+    for m in range(4): wcopy(m).wait()
 
     def chunk(i):
         gl=kv_scr[:,:,pl.ds(pl.multiple_of(i*BQ,BQ),BQ)].reshape(4*nC,BQ)
-        return dot(gl,a_scr[:4*nC,:],TN)
+        return dot(gl,jnp.concatenate([dw_scr[...].reshape(2*nC,D),wx_scr[...].reshape(2*nC,D)],0),TN)
     order=[partner(q,m)*C+t for m in (3,1,2,0) for t in range(C)]
     def xload(e):
         b=order[e]
@@ -674,6 +681,10 @@
     for e in range(NB):
         if e+1<NB: give(e+1)
         take(e)
+        if e==0:
+            for m2 in (1,2): arrived(qr_scr.at[m2-1],qrs.at[m2])
+            zsend(3,lambda ls: dwt(0,ls)+qr_scr[0,:,ls].astype(f32)+qr_scr[1,:,ls].astype(f32))
+            diag(1)
     gpart=gparts[0]
     for t in gparts[1:]: gpart=gpart+t
     vs_scr[...]=jnp.zeros_like(vs_scr)
@@ -687,7 +698,6 @@
     plane=list(itertools.product(range(2),range(4),range(C)))[1:]
     vacp=[rcopy(vs_scr,va_scr.at[me],vas.at[i],vars_.at[me],(z,lax.rem(k+a,2),lax.rem(q+b,4),lax.rem(s+c,C))) for i,(a,b,c) in enumerate(plane)]
     for cp in vacp: cp.start()
-    final(0)
     for a,b,c in plane:
         o=(lax.rem(k+a,2)*4+lax.rem(q+b,4))*C+lax.rem(s+c,C)
         arrived(va_scr.at[o],vars_.at[o])
@@ -703,13 +713,13 @@
     vo_ref[...]=t
     for e in range(2):
         arrived(gws[e].at[1-k],crs.at[e])
-        ccp[e].wait_send()
+        if e==1: ccp[e].wait_send()
     home_arrived(C,n,gi_ref,girs)
     spread_sent(gicp)
     for i in range(1,G-1):
         for e in range(NB): dxcp[i][e].wait_send()
     for m in (1,2):
-        fcp[m].wait_send(); qcp[m].wait_send()
+        fcp[m].wait_send()
     for cp in vacp+vbcp: cp.wait_send()
 
 def backward(Z, C, qkv, ot, do, lse, pd, segk, segq, ain, wts, xo, gmid, gain, vec, fb, R, Pn, Dd):
@@ -723,10 +733,10 @@
         out_shape=(jax.ShapeDtypeStruct((R,Pn,D),bf16),gw,gw,jax.ShapeDtypeStruct((8,D),f32)),
         in_specs=[A,A,A,V,V,V,V,A,A,A,A,V,V,A],out_specs=(A,V,V,V),
         scratch_shapes=[M(4,nC,L),M(hb,L,HD),M(hb,L,HD),M(2,BQ,L),M(2,BQ,L),F(W,L),F(hb,1,L),M(L,D),
-            M(2,nC,D),M(2,nC,D),M(max(2*nC,(G-1)*NB*n),D),M(2,Z,D//Z,nC),M(4,Z,D//Z,nC),F(2,D//Z,nC),M(2,D//Z,nC),M(2,D//Z,nC),M(NB*G,W,n),M(2,NB*G,W,n),
-            M(G-1,NB,n,D),F(BQ,D) if n<BQ else F(8,128),M(1,n,D),F(1,n,D),F(8*C,8,D),F(Z,8,D),F(8,D),F(W,1),
-            S(4),S(4),S(4),S(4),S(4,Z),S(4,Z),S(2),S(2),S(2),S(2),S(G,NB),S(G,NB),S(NB),S(4*C),S(4),S(),S(),S(2),S(4),S(2,2),S(8*C),S(8*C),S(Z),S(Z)],
-        compiler_params=pltpu.CompilerParams(collective_id=1,has_side_effects=True,vmem_limit_bytes=58*2**20),
+            M(2,nC,D),M(2,nC,D),M(max(2*nC,(G-1)*NB*n),D),M(2,Z,D//Z,nC),M(3,Z,D//Z,nC),F(D//Z,nC),M(2,D//Z,nC),M(D//Z,nC),M(NB*G,W,n),M(2,NB*G,W,n),
+            M(G-1,NB,n,D),M(2,nC,D),F(BQ,D) if n<BQ else F(8,128),M(1,n,D),F(1,n,D),F(8*C,8,D),F(Z,8,D),F(8,D),F(W,1),
+            S(4),S(4),S(4),S(4),S(4,Z),S(4,Z),S(2),S(2),S(2),S(2),S(G,NB),S(G,NB),S(NB),S(4*C),S(4),S(),S(),S(2),S(4),S(4),S(2,2),S(8*C),S(8*C),S(Z),S(Z)],
+        compiler_params=pltpu.CompilerParams(collective_id=1,has_side_effects=True,vmem_limit_bytes=61*2**20),
         cost_estimate=pl.CostEstimate(flops=6*10**10,bytes_accessed=10**8,transcendentals=0),
         name="backward")(qkv,ot,do,lse,pd,segk,segq,ain.reshape(L,D),wts,xo,gmid,gain.reshape(1,D),vec,fb)
 

time: 348 us -> 341 us (0.980)
  Pallas kernels: 337 us -> 331 us
    pallas_call x1, Pallas kernels: 149 us -> 142 us  [backward(): pl.pallas_call(functools.partial(bwd_kernel, Z, C, n), out_shape=(jax.Sha...]
where the time goes in v5:
time: 341 us; the launch traced here: 336 us
  Pallas kernels  331 us (97%)
    pallas_call x1, Pallas kernels, backward(): pl.pallas_call(functools.partial(bwd_kernel, Z, C, n), out_shape=(jax.Sha...  142 us
    pallas_call x1, Pallas kernels, forward(): pl.pallas_call(functools.partial(fwd_kernel, Z, C, n), out_shape=(B(NB, n...  125 us
    pallas_call x1, Pallas kernels, middle(): pl.pallas_call(functools.partial(mid_kernel, Z, C, n), out_shape=(B(NB, n...  55 us

profile of v5, /device:TPU:6, one launch (start us, length us, event | category | flops | bytes accessed | tf_op | source)
XLA Modules:
  0.0 335.6 jit_solution(15522148304628599711)
XLA Ops:
  0.6 2.6 prep.1
  3.3 1.3 reshape.39.gain_ref
  4.6 0.0 copy-start.1
  4.6 124.6 %forward.1 = (bf16[4,256,1280]{2,1,0:T(8,128)(2,1)}, bf16[8,256,1280]{2,1,0:T(8,128)(2,1)}, bf16[4,480,1280]{2,1,0:T(8,128)(2,1)}, bf16[2,4,480,1280]{3,2,1,0:T(...) custom-call(bf16[2,512,1280]{2,1,0:T(8,128)(2,1)} %x_ref.1, ...), custom_call_target="tpu_custom_call" | custom-call | flops 30000001024 | bytes 100000000 | tf_op jit(solution)/shard_map/forward/pallas_call | solution.py:309
  129.2 0.0 copy-done.1
  129.2 0.6 reshape.40.gain_ref
  129.8 55.0 %middle.1 = (bf16[4,256,1280]{2,1,0:T(8,128)(2,1)}, bf16[2,512,1280]{2,1,0:T(8,128)(2,1)}, bf16[8,4,160,256]{3,2,1,0:T(8,128)(2,1)}, f32[4,256,1280]{2,1,0:T(8,1...) custom-call(bf16[4,2,4,160,256]{4,3,2,1,0:T(8,128)(2,1)} %get-tuple-element.47.mix_ref, ...), custom_call_target="tpu_custom_call" | custom-call | flops 30000001024 | bytes 100000000 | tf_op jit(solution)/shard_map/middle/pallas_call | solution.py:465
  184.8 0.0 copy-start.2
  184.8 142.3 %backward.1 = (bf16[2,512,1280]{2,1,0:T(8,128)(2,1)}, f32[2,160,480]{2,1,0:T(8,128)}, f32[2,160,480]{2,1,0:T(8,128)}, f32[8,1280]{1,0:T(8,128)}) custom-call(bf16[4,480,2048]{2,1,0:T(8,128)(2,1)} %get-tuple-element.52.qkv_ref, bf16[8,4,160,256]{3,2,1,0:T(8,128)(2,1)} %get-tuple-element.53.ot_ref, bf16[8,4,160,256]{3,2,1,0:T(8,128)(2,1)} %get-tuple-element.54.do_ref, ...), custom_call_target="tpu_custom_call" | custom-call | flops 60000002048 | bytes 100000000 | tf_op jit(solution)/shard_map/backward/pallas_call | solution.py:732
  327.2 0.0 copy-start
  327.2 0.0 copy-done.2
  327.2 0.5 multiply_bitcast_fusion.sf_ref
  327.7 6.1 %finish.1 = (f32[2,512,1280]{2,1,0:T(8,128)}, f32[160,320]{1,0:T(8,128)}, f32[160,320]{1,0:T(8,128)}, f32[160,320]{1,0:T(8,128)}, f32[160,320]{1,0:T(8,128)}, /*...) custom-call(bf16[2,512,1280]{2,1,0:T(8,128)(2,1)} %get-tuple-element.63.gi_ref, ...), custom_call_target="tpu_custom_call" | custom-call | tf_op jit(solution)/shard_map/finish/pallas_call | solution.py:763
  333.8 0.0 copy-done
  333.8 1.5 copy.24
Async XLA Ops:
  4.6 124.6 %copy-start.1 = (f32[1280]{0:T(1024)S(1)}, f32[1280]{0:T(1024)}, u32[]{:S(2)}) copy-start(f32[1280]{0:T(1024)} %param.20) | copy-start | bytes 15364
  184.8 142.3 %copy-start.2 = (f32[80]{0:T(128)S(1)}, f32[80]{0:T(128)}, u32[]{:S(2)}) copy-start(f32[80]{0:T(128)} %param.19) | copy-start | bytes 964
  327.2 6.7 %copy-start = (bf16[2,512,1280]{2,1,0:T(8,128)(2,1)S(1)}, bf16[2,512,1280]{2,1,0:T(8,128)(2,1)}, u32[]{:S(2)}) copy-start(bf16[2,512,1280]{2,1,0:T(8,128)(2,1)} %get-tuple-element.88) | copy-start | bytes 7864324

commit v6 on v5

--- a/solution.py
+++ b/solution.py
@@ -333,10 +333,10 @@
         compiler_params=pltpu.CompilerParams(vmem_limit_bytes=60*2**20),name="prep")(wq,wk,wv,wo.T,wu,wd.T,qs.reshape(1,-1))
 
 
-def mid_kernel(Z, C, n, mix_ref, w2_ref, xo_ref, cot_ref, coto_ref, gain_ref,
+def mid_kernel(Z, C, n, mixh_ref, w2_ref, xoh_ref, cot_ref, coto_ref, gain_ref,
                bo_ref, bh_ref, do_ref, gm_ref, fb_ref, vec_ref,
-               wo_scr, wu_scr, wd_scr, mi_scr, hid_scr, gup_scr, ga_scr, gt_scr, gs_scr, gr_scr, co_scr, up_scr, mid_scr,
-               wl, dos, dors, dol, gss, grs, cot_s, cot_r, out_s, fo_s, bos, bors):
+               wo_scr, wu_scr, wd_scr, mi_scr, hid_scr, gup_scr, ga_scr, gt_scr, gs_scr, gr_scr, co_scr, up_scr, mid_scr, mix_ref, xo_ref,
+               wl, dos, dors, dol, gss, grs, cot_s, cot_r, out_s, fo_s, bos, bors, inl):
     z,k,q,s=[lax.axis_index(a) for a in AXES]
     G=2*C; g0=k*C+s; NB=4*C
     D=gain_ref.shape[1]; K4=wo_scr.shape[0]//G; Ch=K4//4; N=NB*n
@@ -349,6 +349,9 @@
     for i,dst in enumerate((wo_scr,wu_scr,wd_scr)):
         wcp.append([pltpu.make_async_copy(w2_ref.at[g,m,pl.ds(i*Ch,Ch),:],dst.at[pl.ds((g*4+m)*Ch,Ch),:],wl.at[i,g,m]) for g in range(G) for m in range(4)])
         for cp in wcp[i]: cp.start()
+        if i==0:
+            ins=[pltpu.make_async_copy(mixh_ref,mix_ref,inl.at[0]),pltpu.make_async_copy(xoh_ref,xo_ref,inl.at[1])]
+            for cp in ins: cp.start()
     cots=spread_copies(C,n,cot_ref,co_scr,cot_s,cot_r)
     greet(Z,C)
     spread_far(cots,"start")
@@ -358,7 +361,7 @@
     def put(src,dst,sem):
         cp=pltpu.make_async_copy(src,dst,sem); cp.start(); outs.append(cp)
     vec_ref[...]=jnp.zeros_like(vec_ref)
-    for cp in wcp[0]: cp.wait()
+    for cp in wcp[0]+ins: cp.wait()
     def slot(e): return slice(e*n,(e+1)*n)
     def ahead(e):
         b=order[e]
@@ -464,9 +467,9 @@
     B=lambda *sh: jax.ShapeDtypeStruct(sh,bf16)
     return pl.pallas_call(functools.partial(mid_kernel,Z,C,n),
         out_shape=(B(NB,n,D),B(*cot.shape),B(NB*G,4,Ch,n),jax.ShapeDtypeStruct((NB,n,D),f32),B(4,nC,D),jax.ShapeDtypeStruct((8,D),f32)),
-        in_specs=[V,A,V,A,A,V],out_specs=(A,A,A,A,A,V),
-        scratch_shapes=[M(G*K4,D)]*3+[M(N,G*K4) if i in (1,2) else M(N,D) for i in range(4)]+[M(NB,G,4,Ch,n),M((G-1)*3*K4,D),M(G-1,3,K4,D),M(NB,n,D),pltpu.VMEM((NB,n,G*K4),f32),pltpu.VMEM((NB,n,D),f32),
-            S(3,G,4),S(G-1,NB),S(NB*G),S(NB),S(G-1,3),S(G-1,3),S(NB),S(NB),S(2,NB),S(3,4),S(NB),S(4*C)],
+        in_specs=[A,A,A,A,A,V],out_specs=(A,A,A,A,A,V),
+        scratch_shapes=[M(G*K4,D)]*3+[M(N,G*K4) if i in (1,2) else M(N,D) for i in range(4)]+[M(NB,G,4,Ch,n),M((G-1)*3*K4,D),M(G-1,3,K4,D),M(NB,n,D),pltpu.VMEM((NB,n,G*K4),f32),pltpu.VMEM((NB,n,D),f32),M(NB,G,4,Ch,n),M(NB,n,D),
+            S(3,G,4),S(G-1,NB),S(NB*G),S(NB),S(G-1,3),S(G-1,3),S(NB),S(NB),S(2,NB),S(3,4),S(NB),S(4*C),S(2)],
         compiler_params=pltpu.CompilerParams(collective_id=2,has_side_effects=True,vmem_limit_bytes=60*2**20),
         cost_estimate=pl.CostEstimate(flops=3*10**10,bytes_accessed=10**8,transcendentals=0),
         name="middle")(mix,w2o,xo,cot,coto,gain.reshape(1,D))
@@ -526,19 +529,21 @@
         t3_scr[...]=t
         ccp[e].start()
         gws[e][k]=t3_scr[pl.ds(pl.multiple_of(k*Dd,Dd),Dd),:]
+    first=load(fb_ref.at[3],dw_scr.at[0],0)
     kvcp=[pltpu.make_async_copy(qkv_ref.at[m],kv_scr.at[m],kvl.at[m]) for m in range(4)]
-    for m in (1,2,3,0): kvcp[m].start()
+    kvcp[1].start()
     acp=pltpu.make_async_copy(ain_ref,a_scr,al)
-    acp.start()
     def otcp(m): return pltpu.make_async_copy(ot_ref.at[:,m],ot_scr,otl)
     otcp(1).start()
     def docp(idx): return pltpu.make_async_copy(do_ref.at[:,lax.rem(idx+1,4)],do_scr.at[lax.rem(idx,2)],dol.at[lax.rem(idx,2)])
     docp(0).start()
     greet(Z,C)
     for m in (1,2): fcp[m].start()
-    load(fb_ref.at[3],dw_scr.at[0],0).wait()
+    first.wait()
     zsend(0,lambda ls: dw_scr[0,:,ls].astype(f32))
     ld0=load(fb_ref.at[0],dw_scr.at[1],1)
+    acp.start()
+    for m in (2,3,0): kvcp[m].start()
     sc_scr[...]=jnp.zeros_like(sc_scr)
     rowi=lax.broadcasted_iota(jnp.int32,(BQ,BQ),0)
     coli=lax.broadcasted_iota(jnp.int32,(BQ,BQ),1)

time: 341 us -> 337 us (0.988)
  Pallas kernels: 331 us -> 327 us
where the time goes in v6:
time: 337 us; the launch traced here: 332 us
  Pallas kernels  327 us (97%)
  local copies, waits for them, and re-layouts  3.4 us (1%)
    pallas_call x1, Pallas kernels, backward(): pl.pallas_call(functools.partial(bwd_kernel, Z, C, n), out_shape=(jax.Sha...  139 us
    pallas_call x1, Pallas kernels, forward(): pl.pallas_call(functools.partial(fwd_kernel, Z, C, n), out_shape=(B(NB, n...  125 us
    pallas_call x1, Pallas kernels, middle(): pl.pallas_call(functools.partial(mid_kernel, Z, C, n), out_shape=(B(NB, n...  54.4 us

profile of v6, /device:TPU:6, one launch (start us, length us, event | category | flops | bytes accessed | tf_op | source)
XLA Modules:
  0.0 331.7 jit_solution(18214070750623493797)
XLA Ops:
  0.6 2.6 prep.1
  3.3 1.3 reshape.39.gain_ref
  4.6 0.0 copy-start.1
  4.6 124.6 %forward.1 = (bf16[4,256,1280]{2,1,0:T(8,128)(2,1)}, bf16[8,256,1280]{2,1,0:T(8,128)(2,1)}, bf16[4,480,1280]{2,1,0:T(8,128)(2,1)}, bf16[2,4,480,1280]{3,2,1,0:T(...) custom-call(bf16[2,512,1280]{2,1,0:T(8,128)(2,1)} %x_ref.1, ...), custom_call_target="tpu_custom_call" | custom-call | flops 30000001024 | bytes 100000000 | tf_op jit(solution)/shard_map/forward/pallas_call | solution.py:309
  129.2 0.0 copy-done.1
  129.2 0.6 reshape.40.gain_ref
  129.8 54.4 %middle.1 = (bf16[4,256,1280]{2,1,0:T(8,128)(2,1)}, bf16[2,512,1280]{2,1,0:T(8,128)(2,1)}, bf16[8,4,160,256]{3,2,1,0:T(8,128)(2,1)}, f32[4,256,1280]{2,1,0:T(8,1...) custom-call(bf16[4,2,4,160,256]{4,3,2,1,0:T(8,128)(2,1)} %get-tuple-element.47.mixh_ref, ...), custom_call_target="tpu_custom_call" | custom-call | flops 30000001024 | bytes 100000000 | tf_op jit(solution)/shard_map/middle/pallas_call | solution.py:468
  184.2 0.0 copy-start.2
  184.2 139.0 %backward.1 = (bf16[2,512,1280]{2,1,0:T(8,128)(2,1)}, f32[2,160,480]{2,1,0:T(8,128)}, f32[2,160,480]{2,1,0:T(8,128)}, f32[8,1280]{1,0:T(8,128)}) custom-call(bf16[4,480,2048]{2,1,0:T(8,128)(2,1)} %get-tuple-element.52.qkv_ref, bf16[8,4,160,256]{3,2,1,0:T(8,128)(2,1)} %get-tuple-element.53.ot_ref, bf16[8,4,160,256]{3,2,1,0:T(8,128)(2,1)} %get-tuple-element.54.do_ref, ...), custom_call_target="tpu_custom_call" | custom-call | flops 60000002048 | bytes 100000000 | tf_op jit(solution)/shard_map/backward/pallas_call | solution.py:737
  323.3 0.0 copy-start
  323.3 0.0 copy-done.2
  323.3 0.5 multiply_bitcast_fusion.sf_ref
  323.8 6.1 %finish.1 = (f32[2,512,1280]{2,1,0:T(8,128)}, f32[160,320]{1,0:T(8,128)}, f32[160,320]{1,0:T(8,128)}, f32[160,320]{1,0:T(8,128)}, f32[160,320]{1,0:T(8,128)}, /*...) custom-call(bf16[2,512,1280]{2,1,0:T(8,128)(2,1)} %get-tuple-element.63.gi_ref, ...), custom_call_target="tpu_custom_call" | custom-call | tf_op jit(solution)/shard_map/finish/pallas_call | solution.py:768
  329.9 0.0 copy-done
  329.9 1.5 copy.24
Async XLA Ops:
  4.6 124.6 %copy-start.1 = (f32[1280]{0:T(1024)S(1)}, f32[1280]{0:T(1024)}, u32[]{:S(2)}) copy-start(f32[1280]{0:T(1024)} %param.20) | copy-start | bytes 15364
  184.2 139.1 %copy-start.2 = (f32[80]{0:T(128)S(1)}, f32[80]{0:T(128)}, u32[]{:S(2)}) copy-start(f32[80]{0:T(128)} %param.19) | copy-start | bytes 964
  323.3 6.7 %copy-start = (bf16[2,512,1280]{2,1,0:T(8,128)(2,1)S(1)}, bf16[2,512,1280]{2,1,0:T(8,128)(2,1)}, u32[]{:S(2)}) copy-start(bf16[2,512,1280]{2,1,0:T(8,128)(2,1)} %get-tuple-element.88) | copy-start | bytes 7864324

commit v7 on v6

--- a/solution.py
+++ b/solution.py
@@ -315,9 +315,11 @@
             S(4),S(4),S(2),S(2),S(4),S(4),S(G-1,4),S(G,4),S(4),S(G-1,NB,4),S(G,NB,4),S(NB,4),S(),S(),S(6),S(2,4),S(NB),S(NB)],
         compiler_params=pltpu.CompilerParams(collective_id=0,has_side_effects=True,vmem_limit_bytes=60*2**20),
         cost_estimate=pl.CostEstimate(flops=3*10**10,bytes_accessed=10**8,transcendentals=0),
-        name="forward")(tokens,w1h,w2h,cot,gain.reshape(1,D),pd,seg)
-
-def prep_kernel(Ch, wq_ref, wk_ref, wv_ref, wo_ref, wu_ref, wd_ref, qs_ref, w1_ref, w2_ref, pd_ref):
+        name="forward")(tokens,w1h,w2h,cot,gain,pd,seg)
+
+def prep_kernel(Ch, wq_ref, wk_ref, wv_ref, wo_ref, wu_ref, wd_ref, qs_ref, ga_ref, gm_ref, w1_ref, w2_ref, pd_ref, gar_ref, gmr_ref):
+    gar_ref[0,:]=ga_ref[...]
+    gmr_ref[0,:]=gm_ref[...]
     for ref,three in ((w1_ref,(wq_ref[...],wk_ref[...],wv_ref[...])),(w2_ref,(wo_ref[...],wu_ref[...],wd_ref[...]))):
         for i,w in enumerate(three):
             for h in range(2): ref[h,:,i*Ch:(i+1)*Ch]=w[:,h*Ch:(h+1)*Ch]
@@ -326,11 +328,11 @@
     col=jnp.broadcast_to(per_dim,(128,HD)).T
     for h in range(pd_ref.shape[0]//HD): pd_ref[h*HD:(h+1)*HD,:]=col
 
-def prep(wq, wk, wv, wo, wu, wd, qs):
+def prep(wq, wk, wv, wo, wu, wd, qs, ga, gm):
     Dd,Ct=wq.shape; Ch=Ct//2
     B=jax.ShapeDtypeStruct((2,Dd,3*Ch),bf16)
-    return pl.pallas_call(functools.partial(prep_kernel,Ch),out_shape=(B,B,jax.ShapeDtypeStruct((Ch,128),f32)),
-        compiler_params=pltpu.CompilerParams(vmem_limit_bytes=60*2**20),name="prep")(wq,wk,wv,wo.T,wu,wd.T,qs.reshape(1,-1))
+    return pl.pallas_call(functools.partial(prep_kernel,Ch),out_shape=(B,B,jax.ShapeDtypeStruct((Ch,128),f32))+(jax.ShapeDtypeStruct((1,ga.shape[0]),f32),)*2,
+        compiler_params=pltpu.CompilerParams(vmem_limit_bytes=60*2**20),name="prep")(wq,wk,wv,wo.T,wu,wd.T,qs.reshape(1,-1),ga,gm)
 
 
 def mid_kernel(Z, C, n, mixh_ref, w2_ref, xoh_ref, cot_ref, coto_ref, gain_ref,
@@ -472,7 +474,7 @@
             S(3,G,4),S(G-1,NB),S(NB*G),S(NB),S(G-1,3),S(G-1,3),S(NB),S(NB),S(2,NB),S(3,4),S(NB),S(4*C),S(2)],
         compiler_params=pltpu.CompilerParams(collective_id=2,has_side_effects=True,vmem_limit_bytes=60*2**20),
         cost_estimate=pl.CostEstimate(flops=3*10**10,bytes_accessed=10**8,transcendentals=0),
-        name="middle")(mix,w2o,xo,cot,coto,gain.reshape(1,D))
+        name="middle")(mix,w2o,xo,cot,coto,gain)
 
 def bwd_kernel(Z, C, n, qkv_ref, ot_ref, do_ref, lse_ref, pd_ref, segk_ref, segq_ref, ain_ref, wts_ref,
                xo_ref, gmid_ref, gain_ref, vec_ref, fb_ref,
@@ -743,7 +745,7 @@
             S(4),S(4),S(4),S(4),S(4,Z),S(4,Z),S(2),S(2),S(2),S(2),S(G,NB),S(G,NB),S(NB),S(4*C),S(4),S(),S(),S(2),S(4),S(4),S(2,2),S(8*C),S(8*C),S(Z),S(Z)],
         compiler_params=pltpu.CompilerParams(collective_id=1,has_side_effects=True,vmem_limit_bytes=61*2**20),
         cost_estimate=pl.CostEstimate(flops=6*10**10,bytes_accessed=10**8,transcendentals=0),
-        name="backward")(qkv,ot,do,lse,pd,segk,segq,ain.reshape(L,D),wts,xo,gmid,gain.reshape(1,D),vec,fb)
+        name="backward")(qkv,ot,do,lse,pd,segk,segq,ain.reshape(L,D),wts,xo,gmid,gain,vec,fb)
 
 def finish_kernel(Ch, gi_ref, gwm_ref, gwq_ref, vo_ref, sf_ref, ig_ref, gq_ref, gk_ref, gv_ref, go_ref, gu_ref, gd_ref, ga_ref, gs_ref, gm_ref):
     ig_ref[...]=gi_ref[...].astype(f32)
@@ -778,7 +780,7 @@
         R,Pn,D=tokens.shape
         Dd=w_query.shape[0]
 
-        w1h,w2h,pd=prep(w_query,w_key,w_value,w_out,w_up,w_down,query_scale)
+        w1h,w2h,pd,attn_gain,mlp_gain=prep(w_query,w_key,w_value,w_out,w_up,w_down,query_scale,attn_gain,mlp_gain)
         xo,ain,wts,w2o,mix,qkv,ot,lse,segk,segq,coto=forward(Z,C,tokens,w1h,w2h,cotangent,attn_gain,pd,segments)
         _,block_out,do,gmid,fb,vec=middle(Z,C,mix,w2o,xo,cotangent,coto,mlp_gain)
         gi,gwm,gwq,vo=backward(Z,C,qkv,ot,do,lse,pd,segk,segq,ain,wts,xo,gmid,attn_gain,vec,fb,R,Pn,Dd)

time: 337 us -> 335 us (level)
  no operation moved by 1% of the time
where the time goes in v7:
time: 335 us; the launch traced here: 330 us
  Pallas kernels  327 us (98%)
    pallas_call x1, Pallas kernels, backward(): pl.pallas_call(functools.partial(bwd_kernel, Z, C, n), out_shape=(jax.Sha...  139 us
    pallas_call x1, Pallas kernels, forward(): pl.pallas_call(functools.partial(fwd_kernel, Z, C, n), out_shape=(B(NB, n...  125 us
    pallas_call x1, Pallas kernels, middle(): pl.pallas_call(functools.partial(mid_kernel, Z, C, n), out_shape=(B(NB, n...  54.4 us

profile of v7, /device:TPU:6, one launch (start us, length us, event | category | flops | bytes accessed | tf_op | source)
XLA Modules:
  0.0 329.8 jit_solution(1560569678540520489)
XLA Ops:
  0.6 2.7 prep.1
  3.3 124.6 %forward.1 = (bf16[4,256,1280]{2,1,0:T(8,128)(2,1)}, bf16[8,256,1280]{2,1,0:T(8,128)(2,1)}, bf16[4,480,1280]{2,1,0:T(8,128)(2,1)}, bf16[2,4,480,1280]{3,2,1,0:T(...) custom-call(bf16[2,512,1280]{2,1,0:T(8,128)(2,1)} %x_ref.1, ...), custom_call_target="tpu_custom_call" | custom-call | flops 30000001024 | bytes 100000000 | tf_op jit(solution)/shard_map/forward/pallas_call | solution.py:309
  127.9 54.4 %middle.1 = (bf16[4,256,1280]{2,1,0:T(8,128)(2,1)}, bf16[2,512,1280]{2,1,0:T(8,128)(2,1)}, bf16[8,4,160,256]{3,2,1,0:T(8,128)(2,1)}, f32[4,256,1280]{2,1,0:T(8,1...) custom-call(bf16[4,2,4,160,256]{4,3,2,1,0:T(8,128)(2,1)} %get-tuple-element.50.mixh_ref, ...), custom_call_target="tpu_custom_call" | custom-call | flops 30000001024 | bytes 100000000 | tf_op jit(solution)/shard_map/middle/pallas_call | solution.py:470
  182.3 0.0 copy-start.1
  182.4 139.0 %backward.1 = (bf16[2,512,1280]{2,1,0:T(8,128)(2,1)}, f32[2,160,480]{2,1,0:T(8,128)}, f32[2,160,480]{2,1,0:T(8,128)}, f32[8,1280]{1,0:T(8,128)}) custom-call(bf16[4,480,2048]{2,1,0:T(8,128)(2,1)} %get-tuple-element.56.qkv_ref, bf16[8,4,160,256]{3,2,1,0:T(8,128)(2,1)} %get-tuple-element.57.ot_ref, bf16[8,4,160,256]{3,2,1,0:T(8,128)(2,1)} %get-tuple-element.58.do_ref, ...), custom_call_target="tpu_custom_call" | custom-call | flops 60000002048 | bytes 100000000 | tf_op jit(solution)/shard_map/backward/pallas_call | solution.py:739
  321.4 0.0 copy-start
  321.4 0.0 copy-done.1
  321.4 0.5 multiply_bitcast_fusion.sf_ref
  321.9 6.1 %finish.1 = (f32[2,512,1280]{2,1,0:T(8,128)}, f32[160,320]{1,0:T(8,128)}, f32[160,320]{1,0:T(8,128)}, f32[160,320]{1,0:T(8,128)}, f32[160,320]{1,0:T(8,128)}, /*...) custom-call(bf16[2,512,1280]{2,1,0:T(8,128)(2,1)} %get-tuple-element.67.gi_ref, ...), custom_call_target="tpu_custom_call" | custom-call | tf_op jit(solution)/shard_map/finish/pallas_call | solution.py:770
  328.1 0.0 copy-done
  328.1 1.5 copy.24
Async XLA Ops:
  182.3 139.1 %copy-start.1 = (f32[80]{0:T(128)S(1)}, f32[80]{0:T(128)}, u32[]{:S(2)}) copy-start(f32[80]{0:T(128)} %param.19) | copy-start | bytes 964
  321.4 6.7 %copy-start = (bf16[2,512,1280]{2,1,0:T(8,128)(2,1)S(1)}, bf16[2,512,1280]{2,1,0:T(8,128)(2,1)}, u32[]{:S(2)}) copy-start(bf16[2,512,1280]{2,1,0:T(8,128)(2,1)} %get-tuple-element.92) | copy-start | bytes 7864324
